TPU v7x, 256 devices: a whole 4x4x8 slice. The times are simulated.
256 devices in a mesh: leaf: 16 (over z, core), rep: 16 (over y, x).
Axes of the slice: x: 4, y: 4, z: 8, core: 2. Of those that a mesh axis runs over, the one named last changes fastest.
Arguments:
- curve_coordinates: float32 [2, 131072], P(None, 'leaf'), may hold values from -1.25 to 1.25, as said below
- weighted_density: float32 [131072], P('leaf'), may hold values from 0.02 to 0.2
- random_test_matrix: float32 [128, 131072], P('rep', 'leaf'), may hold values from -6 to 6
- sketch_matrix: float32 [128, 131072], P('rep', 'leaf'), may hold values from -12 to 12
Outputs:
- leaf_basis: float32 [128, 131072], P('rep', 'leaf')
- top_basis: float32 [16, 128, 256], P('leaf', 'rep')
Inputs may be any that keep to these rules, and one draw needn't show every extreme that they name: `curve_coordinates`: the points are in order along one closed smooth curve, one point in each of 131072 equal parameter cells.
All inputs are finite; a program needn't handle non-finite values.
Results may differ from a plain program's by a relative error of at most 0.00035.
Values sent between devices are 32-bit elements; how exact they have to be, the bound alone decides.
No kernel may reach another device: no remote copies, remote signals or barrier semaphores. Data moves between devices by JAX's collectives and lax.ppermute only.
A program may use at most 64 MiB of HBM per device.

v0:
```python
import math

import jax
import jax.numpy as jnp
from jax import lax
from jax.experimental import pallas as pl
from jax.experimental.pallas import tpu as pltpu
from jax.sharding import PartitionSpec as P

LEAF = 512
S = 128
NB = 32
SUB = 8
STEP = LEAF // S
F32 = jnp.float32
BF16 = jnp.bfloat16
LOG_SCALE = -0.25 / math.pi


def split3(x):
    high = x.astype(BF16)
    rest = x - high.astype(F32)
    mid = rest.astype(BF16)
    return high, mid, (rest - mid.astype(F32)).astype(BF16)


def product(a, b, dims):
    ah, am, al = a
    bh, bm, bl = b
    left = jnp.concatenate([ah, ah, am, ah, al, am], dims[0][0])
    right = jnp.concatenate([bh, bm, bh, bl, bh, bm], dims[1][0])
    return lax.dot_general(left, right, (dims, ((), ())), preferred_element_type=F32)


def nn(a, b):
    return product(a, b, ((1,), (0,)))


def nt(a, b):
    return product(a, b, ((1,), (1,)))


def tn(a, b):
    return product(a, b, ((0,), (0,)))


def block_rows(diagonal, rows):
    n, width = rows.shape
    groups = n // SUB
    tiles = width // S
    sub = lax.broadcasted_iota(jnp.int32, (SUB, S), 0)
    cols = [
        [
            jnp.broadcast_to(diagonal[SUB * g : SUB * (g + 1), j : j + 1], (SUB, S))
            if g >= j // SUB
            else None
            for g in range(groups)
        ]
        for j in range(n)
    ]
    work = [
        [rows[SUB * g : SUB * (g + 1), S * t : S * (t + 1)] for t in range(tiles)]
        for g in range(groups)
    ]
    scales = [jnp.zeros((SUB, S), F32)] * groups
    for k in range(n):
        gk, sk = divmod(k, SUB)
        scale = lax.rsqrt(jnp.broadcast_to(cols[k][gk][sk : sk + 1], (SUB, S)))
        factor = {g: cols[k][g] * scale for g in range(gk, groups)}
        scales[gk] = jnp.where(sub == sk, scale, scales[gk])
        for j in range(k + 1, n):
            gj, sj = divmod(j, SUB)
            other = factor[gj][sj : sj + 1]
            for g in range(gj, groups):
                cols[j][g] = cols[j][g] - factor[g] * other
        factor[gk] = jnp.where(sub > sk, factor[gk], 0.0)
        for t in range(tiles):
            pivot_row = work[gk][t][sk : sk + 1] * scale
            for g in range(gk + (sk == SUB - 1), groups):
                work[g][t] = work[g][t] - factor[g] * pivot_row
    return jnp.concatenate(
        [
            jnp.concatenate([tile * scales[g] for tile in work[g]], 1)
            for g in range(groups)
        ],
        0,
    )


def eliminate(whole):
    n = whole.shape[0]
    blocks = [whole[i : i + NB] for i in range(0, n, NB)]
    done = []
    for k in range(len(blocks)):
        upper = block_rows(blocks[k][:, k * NB : (k + 1) * NB], blocks[k])
        done.append(upper[:, n:])
        parts = split3(upper)
        for j in range(k + 1, len(blocks)):
            at = slice(j * NB, (j + 1) * NB)
            blocks[j] = blocks[j] - tn([p[:, at] for p in parts], parts)
    return jnp.concatenate(done, 0)


def squared_distances(cols, rows):
    dx = cols[:, 0:1] - rows[0:1]
    dy = cols[:, 1:2] - rows[1:2]
    return dx * dx + dy * dy


def pick(x, every):
    n, width = x.shape
    kept = width // every
    i = lax.broadcasted_iota(jnp.int32, (width, kept), 0)
    j = lax.broadcasted_iota(jnp.int32, (width, kept), 1)
    chosen = jnp.where(i == every * j, 1.0, 0.0).astype(BF16)
    parts = jnp.concatenate([p.astype(F32) for p in split3(x)], 0).astype(BF16)
    got = jnp.dot(parts, chosen, preferred_element_type=F32)
    return got[:n] + (got[n : 2 * n] + got[2 * n :])


def coupling(mine, other, scale):
    to_mine = jnp.log(squared_distances(mine.T, other)) * (other[2:3] * scale)
    to_other = jnp.log(squared_distances(other.T, mine)) * (mine[2:3] * scale)
    return to_mine, to_other


def prepare_kernel(
    rep_ref, coords_ref, density_ref, low_ref, high_ref,
    near_high_ref, near_mid_ref, far_ref, *rest,
):
    pair_refs, (wide, window, skeleton) = rest[:-3], rest[-3:]
    rep = rep_ref[0]
    width = coords_ref.shape[1]
    cells = width // LEAF
    wide[:, :LEAF] = low_ref[SUB:]
    wide[:2, LEAF : LEAF + width] = coords_ref[...]
    wide[2:3, LEAF : LEAF + width] = density_ref[...]
    wide[3:, LEAF : LEAF + width] = jnp.zeros((SUB - 3, width), F32)
    wide[:, LEAF + width :] = high_ref[SUB:]

    window[...] = wide[:, pl.ds(pl.multiple_of(rep * LEAF, LEAF), 3 * LEAF)]
    targets = window[:, LEAF : 2 * LEAF]

    def near_chunk(chunk, carry):
        at = pl.ds(pl.multiple_of(chunk * S, S), S)
        cols = window[:, at].T
        i = lax.broadcasted_iota(jnp.int32, (S, LEAF), 0) + (chunk * S - LEAF)
        same = i == lax.broadcasted_iota(jnp.int32, (S, LEAF), 1)
        squared = jnp.where(same, 1.0, squared_distances(cols, targets))
        itself = -2.0 * (1.0 - jnp.log(0.5 * cols[:, 2:3]))
        values = jnp.where(same, itself, jnp.log(squared)) * (cols[:, 2:3] * LOG_SCALE)
        high = values.astype(BF16)
        near_high_ref[at] = high
        near_mid_ref[at] = (values - high.astype(F32)).astype(BF16)
        return carry

    lax.fori_loop(0, 3 * LEAF // S, near_chunk, 0)

    leaves = [wide[:, LEAF * (i + 1) : LEAF * (i + 2)] for i in range(cells)]
    nodes = pick(jnp.concatenate(leaves, 0), STEP)
    for level, ref in enumerate(pair_refs):
        count = cells >> level
        for i in range(count):
            skeleton[i] = nodes[SUB * i : SUB * (i + 1)]
        index = rep >> level
        pair = coupling(
            skeleton[index], skeleton[index ^ 1], LOG_SCALE * (STEP << level)
        )
        for side in range(2):
            for part, value in enumerate(split3(pair[side])):
                ref[side, part] = value
        joined = [
            jnp.concatenate(
                [nodes[SUB * i : SUB * (i + 1)], nodes[SUB * (i + 1) : SUB * (i + 2)]], 1
            )
            for i in range(0, count, 2)
        ]
        nodes = pick(jnp.concatenate(joined, 0), 2)
    scale = jnp.where(
        lax.broadcasted_iota(jnp.int32, (SUB, S), 0) == 2,
        float(STEP << len(pair_refs)), 1.0,
    )
    far_ref[...] = nodes * scale


def leaf_kernel(data_ref, near_high_ref, near_mid_ref, z_ref, inverse_ref, hat_ref):
    near = jnp.zeros((S, LEAF), F32)
    for part in range(3):
        at = slice(part * LEAF, (part + 1) * LEAF)
        tests = data_ref[:, part + 1].reshape(S, LEAF)
        high, mid, _ = split3(tests)
        near_high, near_mid = near_high_ref[at], near_mid_ref[at]
        left = jnp.concatenate([high, high, mid], 1)
        right = jnp.concatenate([near_high, near_mid, near_high], 0)
        near = near + jnp.dot(left, right, preferred_element_type=F32)
    samples = data_ref[:, 0].reshape(S, LEAF)
    z = samples - near
    z_ref[...] = z
    parts = split3(z)
    both = [split3(samples), split3(data_ref[:, 2].reshape(S, LEAF))]
    gram = nt(parts, parts)
    rights = [nt(parts, x) for x in both]
    eye = jnp.where(
        lax.broadcasted_iota(jnp.int32, (S, S), 0) == lax.broadcasted_iota(jnp.int32, (S, S), 1),
        1.0, 0.0,
    ).astype(F32)
    got = eliminate(jnp.concatenate([gram, *rights, eye], 1))
    hat_ref[:S] = got[:, :S]
    hat_ref[S:] = got[:, S : 2 * S]
    inverse_ref[...] = got[:, 2 * S :]


def basis_kernel(inverse_ref, z_ref, q_ref):
    q = nn(split3(inverse_ref[...]), split3(z_ref[...])) * math.sqrt(LEAF)
    q_ref[...] = q.reshape(q_ref.shape)


def off_diagonal(to_mine, to_other, mine_ref, other_ref):
    z_mine = mine_ref[:S] - nn(to_mine, split3(other_ref[S : 2 * S]))
    z_other = other_ref[:S] - nn(to_other, split3(mine_ref[S : 2 * S]))
    return z_mine, z_other


def merge(to_mine, to_other, mine_ref, other_ref):
    z_mine, z_other = off_diagonal(to_mine, to_other, mine_ref, other_ref)
    left = split3(jnp.concatenate([z_mine.T, z_other.T], 1))
    mine = jnp.concatenate([z_mine, mine_ref[:S], mine_ref[S : 2 * S]], 1)
    other = jnp.concatenate([z_other, other_ref[:S], other_ref[S : 2 * S]], 1)
    return eliminate(nn(left, split3(jnp.concatenate([mine, other], 0))))


def near_parent_kernel(pair_ref, far_ref, mine_ref, other_ref, hat_ref):
    pair = [[pair_ref[side, part] for part in range(3)] for side in range(2)]
    got = merge(*pair, mine_ref, other_ref)
    hat_ref[:S] = got[:, :S]
    hat_ref[S : 2 * S] = got[:, S:]
    if hat_ref.shape[0] > 2 * S:
        hat_ref[2 * S :] = far_ref[...]


def far_parent_kernel(second_ref, mine_ref, other_ref, hat_ref):
    mine, other = mine_ref[2 * S :], other_ref[2 * S :]
    to_mine, to_other = coupling(mine, other, LOG_SCALE)
    got = merge(split3(to_mine), split3(to_other), mine_ref, other_ref)
    hat_ref[:S] = got[:, :S]
    hat_ref[S : 2 * S] = got[:, S:]
    second = second_ref[0] == 1
    joined = jnp.concatenate(
        [jnp.where(second, other, mine), jnp.where(second, mine, other)], 1
    )
    double = lax.broadcasted_iota(jnp.int32, (SUB, S), 0) == 2
    hat_ref[2 * S :] = pick(joined, 2) * jnp.where(double, 2.0, 1.0)


def top_kernel(place_ref, mine_ref, other_ref, q_ref, all_rows):
    mine, other = mine_ref[2 * S :], other_ref[2 * S :]
    to_mine, to_other = coupling(mine, other, LOG_SCALE)
    z_mine, z_other = off_diagonal(
        split3(to_mine), split3(to_other), mine_ref, other_ref
    )
    second = place_ref[0] == 1
    first = jnp.where(second, z_other, z_mine)
    last = jnp.where(second, z_mine, z_other)
    turned = jnp.concatenate([first.T, last.T], 1)
    gram = nn(split3(turned), split3(jnp.concatenate([first, last], 0)))
    all_rows[...] = eliminate(jnp.concatenate([gram, turned], 1)) * math.sqrt(2 * S)
    count = q_ref.shape[0]
    start = pl.multiple_of(place_ref[1] * count, count)
    q_ref[...] = all_rows[pl.ds(start, count)]


VMEM = pl.BlockSpec(memory_space=pltpu.VMEM)
SMEM = pl.BlockSpec(memory_space=pltpu.SMEM)


def call(kernel, outs, specs, *operands, scratch=(), flops=10**9):
    return pl.pallas_call(
        kernel,
        out_shape=[jax.ShapeDtypeStruct(shape, kind) for shape, kind in outs],
        in_specs=specs,
        out_specs=[VMEM] * len(outs),
        scratch_shapes=list(scratch),
        compiler_params=pltpu.CompilerParams(vmem_limit_bytes=32 * 1024 * 1024),
        cost_estimate=pl.CostEstimate(
            flops=flops, bytes_accessed=2**20, transcendentals=0
        ),
    )(*operands)


def swap(block, axis, mask):
    count = lax.axis_size(axis)
    return lax.ppermute(block, axis, [(i, i ^ mask) for i in range(count)])


def body(curve_coordinates, weighted_density, random_test_matrix, sketch_matrix):
    columns, width = random_test_matrix.shape
    cells = width // LEAF
    cell_levels = cells.bit_length() - 1
    rep = lax.axis_index("rep").astype(jnp.int32)
    leaf = lax.axis_index("leaf").astype(jnp.int32)
    count = lax.axis_size("leaf")

    density = weighted_density[None]

    def edge(at):
        return jnp.concatenate(
            [
                random_test_matrix[:, at],
                curve_coordinates[:, at],
                density[:, at],
                jnp.zeros((SUB - 3, LEAF), F32),
            ],
            0,
        )

    low = lax.ppermute(
        edge(slice(width - LEAF, width)), "leaf", [(i, (i + 1) % count) for i in range(count)]
    )
    high = lax.ppermute(
        edge(slice(0, LEAF)), "leaf", [(i, (i - 1) % count) for i in range(count)]
    )

    def by_leaf(block):
        return block.reshape(columns, -1, LEAF).transpose(1, 0, 2)

    tests = by_leaf(random_test_matrix)
    before = jnp.concatenate([low[None, :columns], tests[:-1]], 0)
    after = jnp.concatenate([tests[1:], high[None, :columns]], 0)
    parcels = jnp.stack([by_leaf(sketch_matrix), before, tests, after], 1)
    data = lax.all_to_all(parcels, "rep", 0, 0)

    near_high, near_mid, far, *pairs = call(
        prepare_kernel,
        [((3 * LEAF, LEAF), BF16)] * 2
        + [((SUB, S), F32)]
        + [((2, 3, S, S), BF16)] * cell_levels,
        [SMEM] + [VMEM] * 4,
        rep.reshape(1),
        curve_coordinates,
        density,
        low,
        high,
        scratch=[
            pltpu.VMEM((SUB, width + 2 * LEAF), F32),
            pltpu.VMEM((SUB, 3 * LEAF), F32),
            pltpu.VMEM((cells, SUB, S), F32),
        ],
        flops=10**10,
    )
    z, inverse, hat = call(
        leaf_kernel,
        [((S, LEAF), F32), ((S, S), F32), ((2 * S, S), F32)],
        [VMEM] * 3,
        data,
        near_high,
        near_mid,
    )
    (basis,) = call(
        basis_kernel, [((cells, columns, LEAF), F32)], [VMEM] * 2, inverse, z
    )
    leaf_basis = lax.all_to_all(basis, "rep", 0, 0)
    leaf_basis = leaf_basis.transpose(1, 0, 2).reshape(columns, width)

    for level, mask in enumerate((1, 3, 4, 12)):
        other = swap(hat, "rep", mask)
        rows = 2 * S + (SUB if level == cell_levels - 1 else 0)
        (hat,) = call(
            near_parent_kernel, [((rows, S), F32)], [VMEM] * 4, pairs[level], far, hat, other
        )
    for level, mask in enumerate((1, 2)):
        other = swap(hat, "leaf", mask)
        (hat,) = call(
            far_parent_kernel,
            [((2 * S + SUB, S), F32)],
            [SMEM] + [VMEM] * 2,
            (leaf >> level & 1).reshape(1),
            hat,
            other,
        )
    other = swap(hat, "leaf", 4)
    (top,) = call(
        top_kernel,
        [((columns, 2 * S), F32)],
        [SMEM] + [VMEM] * 2,
        jnp.stack([leaf >> 2 & 1, rep]),
        hat,
        other,
        scratch=[pltpu.VMEM((S, 2 * S), F32)],
    )
    return (leaf_basis, top[None])


def solution(mesh):
    return jax.shard_map(
        body,
        mesh=mesh,
        in_specs=(P(None, "leaf"), P("leaf"), P("rep", "leaf"), P("rep", "leaf")),
        out_specs=(P("rep", "leaf"), P("leaf", "rep", None)),
        check_vma=False,
    )
```

profile of v0, /device:TPU:1, one launch (start us, length us, event | category | flops | bytes accessed | tf_op | source)
XLA Modules:
  0.0 113.2 jit_solution(18084275729790998279)
XLA Ops:
  0.7 0.8 fusion.3
  1.4 0.7 fusion.2
  2.1 0.7 fusion
  3.0 3.2 %collective-permute-start.1 = (f32[16,512]{1,0:T(8,128)S(1)}, f32[16,512]{1,0:T(8,128)S(1)}, u32[]{:S(2)}, u32[]{:S(2)}) collective-permute-start(f32[16,512]{1,0:T(8,128)S(1)} %get-tuple-element.31), channel_id=1, source_target_pairs={{0,240},{16,0},{32,16},{48,32},{64,48},{80,64},{96,80},{112,96},{1... | collective-permute-start | bytes 98312 | tf_op jit(solution)/shard_map/ppermute | solution.py:319
  6.3 1.1 fusion.1
  7.7 2.9 %collective-permute-done.low_ref = f32[16,512]{1,0:T(8,128)S(1)} collective-permute-done((f32[16,512]{1,0:T(8,128)S(1)}, f32[16,512]{1,0:T(8,128)S(1)}, u32[]{:S(2)}, u32[]{:S(2)}) %collective-permute-start) | collective-permute-done | bytes 32800 | tf_op jit(solution)/shard_map/ppermute | solution.py:316
  10.6 1.1 pad_maximum_fusion
  11.6 6.9 %all-to-all-start = ((f32[16,4,8,512]{3,2,1,0:T(8,128)}), f32[16,4,8,512]{3,2,1,0:T(8,128)S(1)}, u32[]{:S(2)}, u32[]{:S(2)}) async-start(f32[16,4,8,512]{3,2,1,0:T(8,128)} %pad_maximum_fusion), calls=%async_computation | async-start | bytes 2097152 | tf_op jit(solution)/shard_map/all_to_all | solution.py:330
  18.6 4.8 %shard_map.59 = (bf16[1536,512]{1,0:T(8,128)(2,1)S(1)}, bf16[1536,512]{1,0:T(8,128)(2,1)S(1)}, f32[8,128]{1,0:T(8,128)S(1)}, bf16[2,3,128,128]{3,2,1,0:T(8,128)(...) custom-call(s32[1]{0:T(128)} %bitcast.14.rep_ref, ...), custom_call_target="tpu_custom_call" | custom-call | flops 10000000000 | bytes 1048576 | tf_op jit(solution)/shard_map/pallas_call | solution.py:277
  23.4 1.2 %copy-done = bf16[1536,512]{1,0:T(8,128)(2,1)} copy-done((bf16[1536,512]{1,0:T(8,128)(2,1)}, bf16[1536,512]{1,0:T(8,128)(2,1)S(1)}, u32[]{:S(2)}) %copy-start) | copy-done | bytes 1572888
  25.2 6.9 %all-to-all-done.data_ref = f32[16,4,8,512]{3,2,1,0:T(8,128)S(1)} async-done(((f32[16,4,8,512]{3,2,1,0:T(8,128)}), f32[16,4,8,512]{3,2,1,0:T(8,128)S(1)}, u32[]{:S(2)}, u32[]{:S(2)}) %all-to-all-start) | async-done | bytes 1048608 | tf_op jit(solution)/shard_map/all_to_all | solution.py:330
  32.1 1.4 %copy-done.1 = bf16[1536,512]{1,0:T(8,128)(2,1)S(1)} copy-done((bf16[1536,512]{1,0:T(8,128)(2,1)S(1)}, bf16[1536,512]{1,0:T(8,128)(2,1)}, u32[]{:S(2)}) %copy-start.1) | copy-done | bytes 1572888
  33.5 4.6 %shard_map.60 = (f32[128,512]{1,0:T(8,128)S(1)}, f32[128,128]{1,0:T(8,128)S(1)}, f32[256,128]{1,0:T(8,128)S(1)}) custom-call(f32[16,4,8,512]{3,2,1,0:T(8,128)S(1)} %all-to-all-done.data_ref, bf16[1536,512]{1,0:T(8,128)(2,1)S(1)} %get-tuple-element.12.near_high_ref, bf16[1536,512]{1,0:T(8,128)(2,1)S(1)} %copy-done.1), custom_call_target="tpu_custom_call" | custom-call | flops 1000000000 | bytes 1048576 | tf_op jit(solution)/shard_map/pallas_call | solution.py:277
  38.1 1.1 collective-permute-start.2
  39.1 2.8 %collective-permute-done.2.other_ref = f32[256,128]{1,0:T(8,128)S(1)} collective-permute-done((f32[256,128]{1,0:T(8,128)S(1)}, f32[256,128]{1,0:T(8,128)S(1)}, u32[]{:S(2)}, u32[]{:S(2)}) %collective-permute-start.2) | collective-permute-done | bytes 131104 | tf_op jit(solution)/shard_map/ppermute | solution.py:292
  42.0 3.8 %shard_map.62.mine_ref = f32[256,128]{1,0:T(8,128)S(1)} custom-call(bf16[2,3,128,128]{3,2,1,0:T(8,128)(2,1)S(1)} %copy-done.5, f32[8,128]{1,0:T(8,128)S(1)} %get-tuple-element.17.far_ref, f32[256,128]{1,0:T(8,128)S(1)} %get-tuple-element.21.mine_ref, f32[256,128]{1,0:T(8,128)S(1)} %collective-permute-done.2.other_ref), custom_call_target="tpu_custom_call" | custom-call | flops 1000000000 | bytes 1048576 | tf_op jit(solution)/shard_map/pallas_call | solution.py:277
  46.1 5.0 %collective-permute-done.3.other_ref = f32[256,128]{1,0:T(8,128)S(1)} collective-permute-done((f32[256,128]{1,0:T(8,128)S(1)}, f32[256,128]{1,0:T(8,128)S(1)}, u32[]{:S(2)}, u32[]{:S(2)}) %collective-permute-start.3) | collective-permute-done | bytes 131104 | tf_op jit(solution)/shard_map/ppermute | solution.py:292
  51.1 3.8 %shard_map.63.mine_ref = f32[256,128]{1,0:T(8,128)S(1)} custom-call(bf16[2,3,128,128]{3,2,1,0:T(8,128)(2,1)S(1)} %get-tuple-element.19.pair_ref, f32[8,128]{1,0:T(8,128)S(1)} %get-tuple-element.17.far_ref, f32[256,128]{1,0:T(8,128)S(1)} %shard_map.62.mine_ref, f32[256,128]{1,0:T(8,128)S(1)} %collective-permute-done.3.other_ref), custom_call_target="tpu_custom_call" | custom-call | flops 1000000000 | bytes 1048576 | tf_op jit(solution)/shard_map/pallas_call | solution.py:277
  55.0 3.8 %collective-permute-done.4.other_ref = f32[256,128]{1,0:T(8,128)S(1)} collective-permute-done((f32[256,128]{1,0:T(8,128)S(1)}, f32[256,128]{1,0:T(8,128)S(1)}, u32[]{:S(2)}, u32[]{:S(2)}) %collective-permute-start.4) | collective-permute-done | bytes 131104 | tf_op jit(solution)/shard_map/ppermute | solution.py:292
  58.8 3.8 %shard_map.64.mine_ref = f32[256,128]{1,0:T(8,128)S(1)} custom-call(bf16[2,3,128,128]{3,2,1,0:T(8,128)(2,1)S(1)} %get-tuple-element.18.pair_ref, f32[8,128]{1,0:T(8,128)S(1)} %get-tuple-element.17.far_ref, f32[256,128]{1,0:T(8,128)S(1)} %shard_map.63.mine_ref, f32[256,128]{1,0:T(8,128)S(1)} %collective-permute-done.4.other_ref), custom_call_target="tpu_custom_call" | custom-call | flops 1000000000 | bytes 1048576 | tf_op jit(solution)/shard_map/pallas_call | solution.py:277
  62.7 1.3 %collective-permute-start.5 = (f32[256,128]{1,0:T(8,128)S(1)}, f32[256,128]{1,0:T(8,128)S(1)}, u32[]{:S(2)}, u32[]{:S(2)}) collective-permute-start(f32[256,128]{1,0:T(8,128)S(1)} %shard_map.64.mine_ref), channel_id=1, source_target_pairs={{0,12},{1,13},{2,14},{3,15},{4,8},{5,9},{6,10},{7,11},{8,4},{9,5},... | collective-permute-start | bytes 393224 | tf_op jit(solution)/shard_map/ppermute | solution.py:292
  64.0 3.8 %collective-permute-done.5.other_ref = f32[256,128]{1,0:T(8,128)S(1)} collective-permute-done((f32[256,128]{1,0:T(8,128)S(1)}, f32[256,128]{1,0:T(8,128)S(1)}, u32[]{:S(2)}, u32[]{:S(2)}) %collective-permute-start.5) | collective-permute-done | bytes 131104 | tf_op jit(solution)/shard_map/ppermute | solution.py:292
  67.8 3.8 %shard_map.65.mine_ref = f32[264,128]{1,0:T(8,128)S(1)} custom-call(bf16[2,3,128,128]{3,2,1,0:T(8,128)(2,1)S(1)} %get-tuple-element.16.pair_ref, f32[8,128]{1,0:T(8,128)S(1)} %get-tuple-element.17.far_ref, f32[256,128]{1,0:T(8,128)S(1)} %shard_map.64.mine_ref, f32[256,128]{1,0:T(8,128)S(1)} %collective-permute-done.5.other_ref), custom_call_target="tpu_custom_call" | custom-call | flops 1000000000 | bytes 1048576 | tf_op jit(solution)/shard_map/pallas_call | solution.py:277
  71.6 10.0 %collective-permute-start.6 = (f32[264,128]{1,0:T(8,128)S(1)}, f32[264,128]{1,0:T(8,128)S(1)}, u32[]{:S(2)}, u32[]{:S(2)}) collective-permute-start(f32[264,128]{1,0:T(8,128)S(1)} %shard_map.65.mine_ref), channel_id=1, source_target_pairs={{0,16},{16,0},{32,48},{48,32},{64,80},{80,64},{96,112},{112,96},{1... | collective-permute-start | bytes 405512 | tf_op jit(solution)/shard_map/ppermute | solution.py:292
  81.6 1.0 collective-permute-done.6.other_ref
  82.6 4.2 %shard_map.66.mine_ref = f32[264,128]{1,0:T(8,128)S(1)} custom-call(s32[1]{0:T(128)} %bitcast.19.second_ref, f32[264,128]{1,0:T(8,128)S(1)} %shard_map.65.mine_ref, f32[264,128]{1,0:T(8,128)S(1)} %collective-permute-done.6.other_ref), custom_call_target="tpu_custom_call" | custom-call | flops 1000000000 | bytes 1048576 | tf_op jit(solution)/shard_map/pallas_call | solution.py:277
  86.8 1.0 shard_map.61
  87.8 3.5 %all-to-all-start.1 = ((f32[16,8,512]{2,1,0:T(8,128)}), f32[16,8,512]{2,1,0:T(8,128)S(1)}, u32[]{:S(2)}, u32[]{:S(2)}) async-start(f32[16,8,512]{2,1,0:T(8,128)} %shard_map.61), calls=%async_computation.1 | async-start | bytes 524288 | tf_op jit(solution)/shard_map/all_to_all | solution.py:361
  91.6 4.2 %shard_map.67.mine_ref = f32[264,128]{1,0:T(8,128)S(1)} custom-call(s32[1]{0:T(128)} %bitcast.18.second_ref, f32[264,128]{1,0:T(8,128)S(1)} %shard_map.66.mine_ref, f32[264,128]{1,0:T(8,128)S(1)} %collective-permute-done.7.other_ref), custom_call_target="tpu_custom_call" | custom-call | flops 1000000000 | bytes 1048576 | tf_op jit(solution)/shard_map/pallas_call | solution.py:277
  95.8 4.6 %collective-permute-start.8 = (f32[264,128]{1,0:T(8,128)S(1)}, f32[264,128]{1,0:T(8,128)S(1)}, u32[]{:S(2)}, u32[]{:S(2)}) collective-permute-start(f32[264,128]{1,0:T(8,128)S(1)} %shard_map.67.mine_ref), channel_id=1, source_target_pairs={{0,64},{16,80},{32,96},{48,112},{64,0},{80,16},{96,32},{112,48},{1... | collective-permute-start | bytes 405512 | tf_op jit(solution)/shard_map/ppermute | solution.py:292
  100.4 6.8 %collective-permute-done.8.other_ref = f32[264,128]{1,0:T(8,128)S(1)} collective-permute-done((f32[264,128]{1,0:T(8,128)S(1)}, f32[264,128]{1,0:T(8,128)S(1)}, u32[]{:S(2)}, u32[]{:S(2)}) %collective-permute-start.8) | collective-permute-done | bytes 135200 | tf_op jit(solution)/shard_map/ppermute | solution.py:292
  107.3 5.2 %shard_map.68 = f32[8,256]{1,0:T(8,128)} custom-call(s32[2]{0:T(128)S(1)} %pad_add_fusion.place_ref, f32[264,128]{1,0:T(8,128)S(1)} %shard_map.67.mine_ref, f32[264,128]{1,0:T(8,128)S(1)} %collective-permute-done.8.other_ref), custom_call_target="tpu_custom_call" | custom-call | flops 1000000000 | bytes 1048576 | tf_op jit(solution)/shard_map/pallas_call | solution.py:277
  (30 shorter events, 2.6 us)
Async XLA Ops:
  0.6 9.9 %copy-start.6 = (f32[8,8192]{1,0:T(8,128)S(1)}, f32[8,8192]{1,0:T(8,128)}, u32[]{:S(2)}) copy-start(f32[8,8192]{1,0:T(8,128)} %param.6) | copy-start | bytes 786436
  0.6 9.9 %copy-start.7 = (f32[8,8192]{1,0:T(8,128)S(1)}, f32[8,8192]{1,0:T(8,128)}, u32[]{:S(2)}) copy-start(f32[8,8192]{1,0:T(8,128)} %param.7) | copy-start | bytes 786436
  3.0 4.6 %collective-permute-start.1 = (f32[16,512]{1,0:T(8,128)S(1)}, f32[16,512]{1,0:T(8,128)S(1)}, u32[]{:S(2)}, u32[]{:S(2)}) collective-permute-start(f32[16,512]{1,0:T(8,128)S(1)} %get-tuple-element.31), channel_id=1, source_target_pairs={{0,240},{16,0},{32,16},{48,32},{64,48},{80,64},{96,80},{112,96},{1... | collective-permute-start | bytes 98312 | tf_op jit(solution)/shard_map/ppermute | solution.py:319
  6.3 4.3 %collective-permute-start = (f32[16,512]{1,0:T(8,128)S(1)}, f32[16,512]{1,0:T(8,128)S(1)}, u32[]{:S(2)}, u32[]{:S(2)}) collective-permute-start(f32[16,512]{1,0:T(8,128)S(1)} %get-tuple-element.30), channel_id=1, source_target_pairs={{0,16},{16,32},{32,48},{48,64},{64,80},{80,96},{96,112},{112,128},... | collective-permute-start | bytes 98312 | tf_op jit(solution)/shard_map/ppermute | solution.py:316
  11.6 6.9 %copy-start.2 = (f32[2,8192]{1,0:T(2,128)S(1)}, f32[2,8192]{1,0:T(2,128)}, u32[]{:S(2)}) copy-start(f32[2,8192]{1,0:T(2,128)} %coords_ref.1) | copy-start | bytes 196612
  11.6 6.9 %copy-start.3 = (f32[8192]{0:T(1024)S(1)}, f32[8192]{0:T(1024)}, u32[]{:S(2)}) copy-start(f32[8192]{0:T(1024)} %param.5) | copy-start | bytes 98308
  11.6 20.4 %all-to-all-start = ((f32[16,4,8,512]{3,2,1,0:T(8,128)}), f32[16,4,8,512]{3,2,1,0:T(8,128)S(1)}, u32[]{:S(2)}, u32[]{:S(2)}) async-start(f32[16,4,8,512]{3,2,1,0:T(8,128)} %pad_maximum_fusion), calls=%async_computation | async-start | bytes 2097152 | tf_op jit(solution)/shard_map/all_to_all | solution.py:330
  23.3 1.2 %copy-start = (bf16[1536,512]{1,0:T(8,128)(2,1)}, bf16[1536,512]{1,0:T(8,128)(2,1)S(1)}, u32[]{:S(2)}) copy-start(bf16[1536,512]{1,0:T(8,128)(2,1)S(1)} %get-tuple-element.13.near_mid_ref) | copy-start | bytes 4718596
  24.5 0.7 copy-start.4
  32.1 1.4 %copy-start.1 = (bf16[1536,512]{1,0:T(8,128)(2,1)S(1)}, bf16[1536,512]{1,0:T(8,128)(2,1)}, u32[]{:S(2)}) copy-start(bf16[1536,512]{1,0:T(8,128)(2,1)} %copy-done) | copy-start | bytes 4718596
  33.5 8.5 %copy-start.5 = (bf16[2,3,128,128]{3,2,1,0:T(8,128)(2,1)S(1)}, bf16[2,3,128,128]{3,2,1,0:T(8,128)(2,1)}, u32[]{:S(2)}) copy-start(bf16[2,3,128,128]{3,2,1,0:T(8,128)(2,1)} %copy-done.4) | copy-start | bytes 589828
  38.1 3.9 %collective-permute-start.2 = (f32[256,128]{1,0:T(8,128)S(1)}, f32[256,128]{1,0:T(8,128)S(1)}, u32[]{:S(2)}, u32[]{:S(2)}) collective-permute-start(f32[256,128]{1,0:T(8,128)S(1)} %get-tuple-element.21.mine_ref), channel_id=1, source_target_pairs={{0,1},{1,0},{2,3},{3,2},{4,5},{5,4},{6,7},{7,6},{8,9},{9,8},{10,11... | collective-permute-start | bytes 393224 | tf_op jit(solution)/shard_map/ppermute | solution.py:292
  45.8 5.3 %collective-permute-start.3 = (f32[256,128]{1,0:T(8,128)S(1)}, f32[256,128]{1,0:T(8,128)S(1)}, u32[]{:S(2)}, u32[]{:S(2)}) collective-permute-start(f32[256,128]{1,0:T(8,128)S(1)} %shard_map.62.mine_ref), channel_id=1, source_target_pairs={{0,3},{1,2},{2,1},{3,0},{4,7},{5,6},{6,5},{7,4},{8,11},{9,10},{10,... | collective-permute-start | bytes 393224 | tf_op jit(solution)/shard_map/ppermute | solution.py:292
  54.9 3.9 %collective-permute-start.4 = (f32[256,128]{1,0:T(8,128)S(1)}, f32[256,128]{1,0:T(8,128)S(1)}, u32[]{:S(2)}, u32[]{:S(2)}) collective-permute-start(f32[256,128]{1,0:T(8,128)S(1)} %shard_map.63.mine_ref), channel_id=1, source_target_pairs={{0,4},{1,5},{2,6},{3,7},{4,0},{5,1},{6,2},{7,3},{8,12},{9,13},{10,... | collective-permute-start | bytes 393224 | tf_op jit(solution)/shard_map/ppermute | solution.py:292
  62.7 5.1 %collective-permute-start.5 = (f32[256,128]{1,0:T(8,128)S(1)}, f32[256,128]{1,0:T(8,128)S(1)}, u32[]{:S(2)}, u32[]{:S(2)}) collective-permute-start(f32[256,128]{1,0:T(8,128)S(1)} %shard_map.64.mine_ref), channel_id=1, source_target_pairs={{0,12},{1,13},{2,14},{3,15},{4,8},{5,9},{6,10},{7,11},{8,4},{9,5},... | collective-permute-start | bytes 393224 | tf_op jit(solution)/shard_map/ppermute | solution.py:292
  71.6 11.0 %collective-permute-start.6 = (f32[264,128]{1,0:T(8,128)S(1)}, f32[264,128]{1,0:T(8,128)S(1)}, u32[]{:S(2)}, u32[]{:S(2)}) collective-permute-start(f32[264,128]{1,0:T(8,128)S(1)} %shard_map.65.mine_ref), channel_id=1, source_target_pairs={{0,16},{16,0},{32,48},{48,32},{64,80},{80,64},{96,112},{112,96},{1... | collective-permute-start | bytes 405512 | tf_op jit(solution)/shard_map/ppermute | solution.py:292
  86.8 4.8 %collective-permute-start.7 = (f32[264,128]{1,0:T(8,128)S(1)}, f32[264,128]{1,0:T(8,128)S(1)}, u32[]{:S(2)}, u32[]{:S(2)}) collective-permute-start(f32[264,128]{1,0:T(8,128)S(1)} %shard_map.66.mine_ref), channel_id=1, source_target_pairs={{0,32},{16,48},{32,0},{48,16},{64,96},{80,112},{96,64},{112,80},{1... | collective-permute-start | bytes 405512 | tf_op jit(solution)/shard_map/ppermute | solution.py:292
  87.8 12.6 %all-to-all-start.1 = ((f32[16,8,512]{2,1,0:T(8,128)}), f32[16,8,512]{2,1,0:T(8,128)S(1)}, u32[]{:S(2)}, u32[]{:S(2)}) async-start(f32[16,8,512]{2,1,0:T(8,128)} %shard_map.61), calls=%async_computation.1 | async-start | bytes 524288 | tf_op jit(solution)/shard_map/all_to_all | solution.py:361
  95.8 11.5 %collective-permute-start.8 = (f32[264,128]{1,0:T(8,128)S(1)}, f32[264,128]{1,0:T(8,128)S(1)}, u32[]{:S(2)}, u32[]{:S(2)}) collective-permute-start(f32[264,128]{1,0:T(8,128)S(1)} %shard_map.67.mine_ref), channel_id=1, source_target_pairs={{0,64},{16,80},{32,96},{48,112},{64,0},{80,16},{96,32},{112,48},{1... | collective-permute-start | bytes 405512 | tf_op jit(solution)/shard_map/ppermute | solution.py:292
where the time goes:
time: 114 us; the launch traced here: 113 us
  Pallas kernels  39.2 us (34%)
  waiting for transfers between devices  33.6 us (29%)
  starting transfers between devices  31 us (27%)
  local copies, waits for them, and re-layouts  7.36 us (6%)
  other arithmetic  1.28 us (1%)
    pallas_call x10, Pallas kernels, call(): pl.pallas_call(kernel, out_shape=[jax.ShapeDtypeStruct(shape, kind) for s...  39.2 us
    ppermute x7, waiting for transfers between devices, swap(): return lax.ppermute(block, axis, [(i, i ^ mask) for i in range(count)])  23.6 us
    ppermute x7, starting transfers between devices, swap(): return lax.ppermute(block, axis, [(i, i ^ mask) for i in range(count)])  17.3 us
    all_to_all x1, starting transfers between devices, body(): data = lax.all_to_all(parcels, 'rep', 0, 0)  6.89 us
    all_to_all x1, waiting for transfers between devices, body(): data = lax.all_to_all(parcels, 'rep', 0, 0)  6.87 us
    unnamed x17, local copies, waits for them, and re-layouts  3.98 us
    all_to_all x1, starting transfers between devices, body(): leaf_basis = lax.all_to_all(basis, 'rep', 0, 0)  3.53 us
    ppermute x1, starting transfers between devices, body(): lax.ppermute(edge(slice(0, LEAF)), 'leaf', [(i, (i - 1) % count) for i in...  3.24 us
  transfers between devices with their start and end apart: 11, of which 10 were waited for; matrix products, arithmetic and copies ran while one was open for 1% of the time, Pallas kernels for 9%

commit v1 on v0

--- a/solution.py
+++ b/solution.py
@@ -15,6 +15,7 @@
 F32 = jnp.float32
 BF16 = jnp.bfloat16
 LOG_SCALE = -0.25 / math.pi
+VMEM_LIMIT = 16 * 1024 * 1024
 
 
 def split3(x):
@@ -92,7 +93,11 @@
     blocks = [whole[i : i + NB] for i in range(0, n, NB)]
     done = []
     for k in range(len(blocks)):
-        upper = block_rows(blocks[k][:, k * NB : (k + 1) * NB], blocks[k])
+        diagonal = blocks[k][:, k * NB : (k + 1) * NB]
+        if k == len(blocks) - 1:
+            done.append(block_rows(diagonal, blocks[k][:, n:]))
+            break
+        upper = block_rows(diagonal, blocks[k])
         done.append(upper[:, n:])
         parts = split3(upper)
         for j in range(k + 1, len(blocks)):
@@ -183,16 +188,56 @@
     far_ref[...] = nodes * scale
 
 
-def leaf_kernel(data_ref, near_high_ref, near_mid_ref, z_ref, inverse_ref, hat_ref):
+def edges_kernel(
+    first_ref, last_ref, first_coords_ref, last_coords_ref, density_ref, low_ref, high_ref
+):
+    width = density_ref.shape[1]
+    sides = (
+        (high_ref, first_ref, first_coords_ref, 0),
+        (low_ref, last_ref, last_coords_ref, width - LEAF),
+    )
+    for ref, tests_ref, coords_ref, start in sides:
+        ref[:SUB] = tests_ref[...]
+        ref[SUB : SUB + 2] = coords_ref[...]
+        ref[SUB + 2 : SUB + 3] = density_ref[:, start : start + LEAF]
+        ref[SUB + 3 :] = jnp.zeros((SUB - 3, LEAF), F32)
+
+
+def turn(index, turned):
+    return jnp.where(turned == 1, index % 4 * 4 + index // 4, index)
+
+
+def pack_kernel(turned_ref, samples_ref, tests_ref, low_ref, high_ref, out_ref, wide):
+    width = samples_ref.shape[1]
+    wide[:, :LEAF] = low_ref[:SUB]
+    wide[:, LEAF : LEAF + width] = tests_ref[...]
+    wide[:, LEAF + width :] = high_ref[:SUB]
+    for i in range(out_ref.shape[0]):
+        leaf = turn(jnp.int32(i), turned_ref[0])
+        out_ref[i, 0] = samples_ref[:, pl.ds(pl.multiple_of(leaf * LEAF, LEAF), LEAF)]
+        for side in range(3):
+            start = pl.multiple_of((leaf + side) * LEAF, LEAF)
+            out_ref[i, side + 1] = wide[:, pl.ds(start, LEAF)]
+
+
+def leaf_kernel(
+    data_ref, near_high_ref, near_mid_hbm, z_ref, inverse_ref, hat_ref, near_mid_ref, sem
+):
+    fetch = pltpu.make_async_copy(near_mid_hbm, near_mid_ref, sem)
+    fetch.start()
     near = jnp.zeros((S, LEAF), F32)
+    highs = []
     for part in range(3):
-        at = slice(part * LEAF, (part + 1) * LEAF)
-        tests = data_ref[:, part + 1].reshape(S, LEAF)
-        high, mid, _ = split3(tests)
-        near_high, near_mid = near_high_ref[at], near_mid_ref[at]
-        left = jnp.concatenate([high, high, mid], 1)
-        right = jnp.concatenate([near_high, near_mid, near_high], 0)
+        near_high = near_high_ref[part * LEAF : (part + 1) * LEAF]
+        high, mid, _ = split3(data_ref[:, part + 1].reshape(S, LEAF))
+        left = jnp.concatenate([high, mid], 1)
+        right = jnp.concatenate([near_high, near_high], 0)
         near = near + jnp.dot(left, right, preferred_element_type=F32)
+        highs.append(high)
+    fetch.wait()
+    near = near + jnp.dot(
+        jnp.concatenate(highs, 1), near_mid_ref[...], preferred_element_type=F32
+    )
     samples = data_ref[:, 0].reshape(S, LEAF)
     z = samples - near
     z_ref[...] = z
@@ -238,7 +283,7 @@
         hat_ref[2 * S :] = far_ref[...]
 
 
-def far_parent_kernel(second_ref, mine_ref, other_ref, hat_ref):
+def far_parent_kernel(second_ref, mine_ref, other_ref, hat_ref, *half_refs):
     mine, other = mine_ref[2 * S :], other_ref[2 * S :]
     to_mine, to_other = coupling(mine, other, LOG_SCALE)
     got = merge(split3(to_mine), split3(to_other), mine_ref, other_ref)
@@ -250,9 +295,23 @@
     )
     double = lax.broadcasted_iota(jnp.int32, (SUB, S), 0) == 2
     hat_ref[2 * S :] = pick(joined, 2) * jnp.where(double, 2.0, 1.0)
-
-
-def top_kernel(place_ref, mine_ref, other_ref, q_ref, all_rows):
+    for half_ref in half_refs:
+        half_ref[...] = jnp.where(second_ref[1] == 1, hat_ref[S:], hat_ref[: S + SUB])
+
+
+def top_kernel(
+    place_ref, mine_ref, direct_ref, passed_ref, parts_ref, q_ref, basis_ref,
+    all_rows, other_ref, sems,
+):
+    copies = []
+    for i in range(parts_ref.shape[0]):
+        leaf = turn(jnp.int32(i), place_ref[2])
+        to = basis_ref.at[:, pl.ds(pl.multiple_of(leaf * LEAF, LEAF), LEAF)]
+        copies.append(pltpu.make_async_copy(parts_ref.at[i], to, sems.at[i]))
+        copies[-1].start()
+    upper_direct = place_ref[2] == 0
+    other_ref[: S + SUB] = jnp.where(upper_direct, direct_ref[...], passed_ref[...])
+    other_ref[S:] = jnp.where(upper_direct, passed_ref[...], direct_ref[...])
     mine, other = mine_ref[2 * S :], other_ref[2 * S :]
     to_mine, to_other = coupling(mine, other, LOG_SCALE)
     z_mine, z_other = off_diagonal(
@@ -267,29 +326,42 @@
     count = q_ref.shape[0]
     start = pl.multiple_of(place_ref[1] * count, count)
     q_ref[...] = all_rows[pl.ds(start, count)]
+    for copy in copies:
+        copy.wait()
 
 
 VMEM = pl.BlockSpec(memory_space=pltpu.VMEM)
 SMEM = pl.BlockSpec(memory_space=pltpu.SMEM)
-
-
-def call(kernel, outs, specs, *operands, scratch=(), flops=10**9):
+ANY = pl.BlockSpec(memory_space=pl.ANY)
+
+
+def call(kernel, outs, specs, *operands, out_specs=None, scratch=(), flops=10**9):
     return pl.pallas_call(
         kernel,
         out_shape=[jax.ShapeDtypeStruct(shape, kind) for shape, kind in outs],
         in_specs=specs,
-        out_specs=[VMEM] * len(outs),
+        out_specs=out_specs or [VMEM] * len(outs),
         scratch_shapes=list(scratch),
-        compiler_params=pltpu.CompilerParams(vmem_limit_bytes=32 * 1024 * 1024),
+        compiler_params=pltpu.CompilerParams(vmem_limit_bytes=VMEM_LIMIT),
         cost_estimate=pl.CostEstimate(
             flops=flops, bytes_accessed=2**20, transcendentals=0
         ),
     )(*operands)
 
 
-def swap(block, axis, mask):
-    count = lax.axis_size(axis)
-    return lax.ppermute(block, axis, [(i, i ^ mask) for i in range(count)])
+def swap(block, even, odd):
+    leaves, reps = lax.axis_size("leaf"), lax.axis_size("rep")
+    route = [
+        (i * reps + j, i * reps + (j ^ (odd if i % 2 else even)))
+        for i in range(leaves)
+        for j in range(reps)
+    ]
+    return lax.ppermute(block, ("leaf", "rep"), route)
+
+
+def cross(block, mask):
+    count = lax.axis_size("leaf")
+    return lax.ppermute(block, "leaf", [(i, i ^ mask) for i in range(count)])
 
 
 def body(curve_coordinates, weighted_density, random_test_matrix, sketch_matrix):
@@ -299,34 +371,36 @@
     rep = lax.axis_index("rep").astype(jnp.int32)
     leaf = lax.axis_index("leaf").astype(jnp.int32)
     count = lax.axis_size("leaf")
+    turned = leaf & 1
+    own = turn(rep, turned)
 
     density = weighted_density[None]
 
-    def edge(at):
-        return jnp.concatenate(
-            [
-                random_test_matrix[:, at],
-                curve_coordinates[:, at],
-                density[:, at],
-                jnp.zeros((SUB - 3, LEAF), F32),
-            ],
-            0,
-        )
-
-    low = lax.ppermute(
-        edge(slice(width - LEAF, width)), "leaf", [(i, (i + 1) % count) for i in range(count)]
-    )
-    high = lax.ppermute(
-        edge(slice(0, LEAF)), "leaf", [(i, (i - 1) % count) for i in range(count)]
-    )
-
-    def by_leaf(block):
-        return block.reshape(columns, -1, LEAF).transpose(1, 0, 2)
-
-    tests = by_leaf(random_test_matrix)
-    before = jnp.concatenate([low[None, :columns], tests[:-1]], 0)
-    after = jnp.concatenate([tests[1:], high[None, :columns]], 0)
-    parcels = jnp.stack([by_leaf(sketch_matrix), before, tests, after], 1)
+    def edge(rows, last):
+        return pl.BlockSpec((rows, LEAF), lambda i: (0, cells - 1 if last else 0))
+
+    low, high = pl.pallas_call(
+        edges_kernel,
+        grid=(1,),
+        out_shape=[jax.ShapeDtypeStruct((2 * SUB, LEAF), F32)] * 2,
+        in_specs=[edge(columns, False), edge(columns, True), edge(2, False), edge(2, True)]
+        + [pl.BlockSpec((1, width), lambda i: (0, 0))],
+        out_specs=[pl.BlockSpec((2 * SUB, LEAF), lambda i: (0, 0))] * 2,
+    )(random_test_matrix, random_test_matrix, curve_coordinates, curve_coordinates, density)
+    low = lax.ppermute(low, "leaf", [(i, (i + 1) % count) for i in range(count)])
+    high = lax.ppermute(high, "leaf", [(i, (i - 1) % count) for i in range(count)])
+
+    (parcels,) = call(
+        pack_kernel,
+        [((cells, 4, columns, LEAF), F32)],
+        [SMEM] + [VMEM] * 4,
+        turned.reshape(1),
+        sketch_matrix,
+        random_test_matrix,
+        low,
+        high,
+        scratch=[pltpu.VMEM((columns, width + 2 * LEAF), F32)],
+    )
     data = lax.all_to_all(parcels, "rep", 0, 0)
 
     near_high, near_mid, far, *pairs = call(
@@ -335,7 +409,7 @@
         + [((SUB, S), F32)]
         + [((2, 3, S, S), BF16)] * cell_levels,
         [SMEM] + [VMEM] * 4,
-        rep.reshape(1),
+        own.reshape(1),
         curve_coordinates,
         density,
         low,
@@ -350,42 +424,49 @@
     z, inverse, hat = call(
         leaf_kernel,
         [((S, LEAF), F32), ((S, S), F32), ((2 * S, S), F32)],
-        [VMEM] * 3,
+        [VMEM, VMEM, ANY],
         data,
         near_high,
         near_mid,
+        scratch=[pltpu.VMEM((3 * LEAF, LEAF), BF16), pltpu.SemaphoreType.DMA],
     )
     (basis,) = call(
         basis_kernel, [((cells, columns, LEAF), F32)], [VMEM] * 2, inverse, z
     )
-    leaf_basis = lax.all_to_all(basis, "rep", 0, 0)
-    leaf_basis = leaf_basis.transpose(1, 0, 2).reshape(columns, width)
-
-    for level, mask in enumerate((1, 3, 4, 12)):
-        other = swap(hat, "rep", mask)
+    parts = lax.all_to_all(basis, "rep", 0, 0)
+
+    for level, masks in enumerate(((1, 4), (3, 12), (4, 1), (12, 3))):
+        other = swap(hat, *masks)
         rows = 2 * S + (SUB if level == cell_levels - 1 else 0)
         (hat,) = call(
             near_parent_kernel, [((rows, S), F32)], [VMEM] * 4, pairs[level], far, hat, other
         )
-    for level, mask in enumerate((1, 2)):
-        other = swap(hat, "leaf", mask)
-        (hat,) = call(
+    for level in range(2):
+        other = cross(hat, 1 << level)
+        hat, *half = call(
             far_parent_kernel,
-            [((2 * S + SUB, S), F32)],
+            [((2 * S + SUB, S), F32), ((S + SUB, S), F32)][: level + 1],
             [SMEM] + [VMEM] * 2,
-            (leaf >> level & 1).reshape(1),
+            jnp.stack([leaf >> level & 1, turned]),
             hat,
             other,
         )
-    other = swap(hat, "leaf", 4)
-    (top,) = call(
+    direct = cross(half[0], 4)
+    top, leaf_basis = call(
         top_kernel,
-        [((columns, 2 * S), F32)],
-        [SMEM] + [VMEM] * 2,
-        jnp.stack([leaf >> 2 & 1, rep]),
+        [((columns, 2 * S), F32), ((columns, width), F32)],
+        [SMEM] + [VMEM] * 3 + [ANY],
+        jnp.stack([leaf >> 2 & 1, rep, turned]),
         hat,
-        other,
-        scratch=[pltpu.VMEM((S, 2 * S), F32)],
+        direct,
+        cross(direct, 1),
+        parts,
+        out_specs=[VMEM, ANY],
+        scratch=[
+            pltpu.VMEM((S, 2 * S), F32),
+            pltpu.VMEM((2 * S + SUB, S), F32),
+            pltpu.SemaphoreType.DMA((cells,)),
+        ],
     )
     return (leaf_basis, top[None])
 

time: 114 us -> 112 us (0.982)
  Pallas kernels: 39.2 us -> 43.2 us
  starting transfers between devices: 31 us -> 27.5 us
  local copies, waits for them, and re-layouts: 7.36 us -> 5.17 us
    ppermute x9 -> x10, starting transfers between devices: 20.6 us -> 17 us  [the longest x4 11.9 us: cross(): return lax.ppermute(block, 'leaf', [(i, i ^ mask) for i in range(count)])]
    slice x4 -> x0, local copies, waits for them, and re-layouts: 3.29 us -> none  [the longest x1 1.09 us: body(): before = jnp.concatenate([low[None, :columns], tests[:-1]], 0)]
    pallas_call x10 -> x11, Pallas kernels: 39.2 us -> 41.7 us  [call(): pl.pallas_call(kernel, out_shape=[jax.ShapeDtypeStruct(shape, kind) for s...]
    pallas_call x0 -> x1, Pallas kernels: none -> 1.47 us  [body(): pl.pallas_call(edges_kernel, grid=(1,), out_shape=[jax.ShapeDtypeStruct((...]
    all_to_all x1, waiting for transfers between devices: 6.87 us -> 8.31 us  [body(): data = lax.all_to_all(parcels, 'rep', 0, 0)]
    unnamed x17 -> x16, local copies, waits for them, and re-layouts: 3.98 us -> 5.17 us
    ppermute x9 -> x10, waiting for transfers between devices: 26.7 us -> 26 us  [the longest x4 16.3 us: swap(): return lax.ppermute(block, ('leaf', 'rep'), route)]
  transfers between devices with their start and end apart: 11 -> 12, of which waited for: 10 -> 10; matrix products, arithmetic and copies ran while one was open for 1% -> 0% of each run, Pallas kernels for 9% -> 9%
where the time goes in v1:
time: 112 us; the launch traced here: 111 us
  Pallas kernels  43.2 us (39%)
  waiting for transfers between devices  34.3 us (31%)
  starting transfers between devices  27.5 us (25%)
  local copies, waits for them, and re-layouts  5.17 us (5%)
    pallas_call x11, Pallas kernels, call(): pl.pallas_call(kernel, out_shape=[jax.ShapeDtypeStruct(shape, kind) for s...  41.7 us
    ppermute x4, waiting for transfers between devices, swap(): return lax.ppermute(block, ('leaf', 'rep'), route)  16.3 us
    ppermute x4, starting transfers between devices, cross(): return lax.ppermute(block, 'leaf', [(i, i ^ mask) for i in range(count)])  11.9 us
    all_to_all x1, waiting for transfers between devices, body(): data = lax.all_to_all(parcels, 'rep', 0, 0)  8.31 us
    all_to_all x1, starting transfers between devices, body(): data = lax.all_to_all(parcels, 'rep', 0, 0)  6.89 us
    ppermute x4, waiting for transfers between devices, cross(): return lax.ppermute(block, 'leaf', [(i, i ^ mask) for i in range(count)])  6.41 us
    unnamed x16, local copies, waits for them, and re-layouts  5.17 us
    all_to_all x1, starting transfers between devices, body(): parts = lax.all_to_all(basis, 'rep', 0, 0)  3.53 us
  transfers between devices with their start and end apart: 12, of which 10 were waited for; matrix products, arithmetic and copies ran while one was open for 0% of the time, Pallas kernels for 9%

profile of v1, /device:TPU:1, one launch (start us, length us, event | category | flops | bytes accessed | tf_op | source)
XLA Modules:
  0.0 111.3 jit_solution(8871982218129589724)
XLA Ops:
  0.6 1.5 %shard_map.59 = (f32[16,512]{1,0:T(8,128)}, f32[16,512]{1,0:T(8,128)}) custom-call(f32[8,8192]{1,0:T(8,128)} %tests_ref.1, f32[8,8192]{1,0:T(8,128)} %tests_ref.1, f32[2,8192]{1,0:T(2,128)} %coords_ref.1, f32[2,8192]{1,0:T(2,128)} %coords_ref.1, f32[1,8192]{1,0:T(1,128)} %bitcast.8), custom_call_target="tpu_custom_call" | custom-call | tf_op jit(solution)/shard_map/pallas_call | solution.py:382
  2.1 3.0 %collective-permute-start = (f32[16,512]{1,0:T(8,128)}, f32[16,512]{1,0:T(8,128)S(1)}, u32[]{:S(2)}, u32[]{:S(2)}) collective-permute-start(f32[16,512]{1,0:T(8,128)} %get-tuple-element.18), channel_id=1, source_target_pairs={{0,16},{16,32},{32,48},{48,64},{64,80},{80,96},{96,112},{112,128},... | collective-permute-start | bytes 98312 | tf_op jit(solution)/shard_map/ppermute | solution.py:390
  5.3 1.1 %collective-permute-done.low_ref = f32[16,512]{1,0:T(8,128)S(1)} collective-permute-done((f32[16,512]{1,0:T(8,128)}, f32[16,512]{1,0:T(8,128)S(1)}, u32[]{:S(2)}, u32[]{:S(2)}) %collective-permute-start) | collective-permute-done | bytes 32800 | tf_op jit(solution)/shard_map/ppermute | solution.py:390
  6.5 2.2 %collective-permute-done.1.high_ref = f32[16,512]{1,0:T(8,128)S(1)} collective-permute-done((f32[16,512]{1,0:T(8,128)}, f32[16,512]{1,0:T(8,128)S(1)}, u32[]{:S(2)}, u32[]{:S(2)}) %collective-permute-start.1) | collective-permute-done | bytes 32800 | tf_op jit(solution)/shard_map/ppermute | solution.py:391
  8.7 0.9 copy-done.2
  9.6 0.9 copy-done.5
  10.6 1.1 shard_map.61
  11.6 6.9 %all-to-all-start = ((f32[16,4,8,512]{3,2,1,0:T(8,128)}), f32[16,4,8,512]{3,2,1,0:T(8,128)S(1)}, u32[]{:S(2)}, u32[]{:S(2)}) async-start(f32[16,4,8,512]{3,2,1,0:T(8,128)} %shard_map.61), calls=%async_computation | async-start | bytes 2097152 | tf_op jit(solution)/shard_map/all_to_all | solution.py:404
  18.6 4.8 %shard_map.60 = (bf16[1536,512]{1,0:T(8,128)(2,1)S(1)}, bf16[1536,512]{1,0:T(8,128)(2,1)S(1)}, f32[8,128]{1,0:T(8,128)S(1)}, bf16[2,3,128,128]{3,2,1,0:T(8,128)(...) custom-call(s32[1]{0:T(128)} %bitcast.5.rep_ref, ...), custom_call_target="tpu_custom_call" | custom-call | flops 10000000000 | bytes 1048576 | tf_op jit(solution)/shard_map/pallas_call | solution.py:339
  23.4 1.2 %copy-done = bf16[1536,512]{1,0:T(8,128)(2,1)} copy-done((bf16[1536,512]{1,0:T(8,128)(2,1)}, bf16[1536,512]{1,0:T(8,128)(2,1)S(1)}, u32[]{:S(2)}) %copy-start) | copy-done | bytes 1572888
  25.2 8.3 %all-to-all-done.data_ref = f32[16,4,8,512]{3,2,1,0:T(8,128)S(1)} async-done(((f32[16,4,8,512]{3,2,1,0:T(8,128)}), f32[16,4,8,512]{3,2,1,0:T(8,128)S(1)}, u32[]{:S(2)}, u32[]{:S(2)}) %all-to-all-start) | async-done | bytes 1048608 | tf_op jit(solution)/shard_map/all_to_all | solution.py:404
  33.5 1.4 %copy-done.1 = bf16[1536,512]{1,0:T(8,128)(2,1)S(1)} copy-done((bf16[1536,512]{1,0:T(8,128)(2,1)S(1)}, bf16[1536,512]{1,0:T(8,128)(2,1)}, u32[]{:S(2)}) %copy-start.1) | copy-done | bytes 1572888
  35.0 4.8 %shard_map.62 = (f32[128,512]{1,0:T(8,128)S(1)}, f32[128,128]{1,0:T(8,128)S(1)}, f32[256,128]{1,0:T(8,128)S(1)}) custom-call(f32[16,4,8,512]{3,2,1,0:T(8,128)S(1)} %all-to-all-done.data_ref, bf16[1536,512]{1,0:T(8,128)(2,1)S(1)} %get-tuple-element.25.near_high_ref, bf16[1536,512]{1,0:T(8,128)(2,1)S(1)} %copy-done.1), custom_call_target="tpu_custom_call" | custom-call | flops 1000000000 | bytes 1048576 | tf_op jit(solution)/shard_map/pallas_call | solution.py:339
  39.8 3.8 %collective-permute-done.2.other_ref = f32[256,128]{1,0:T(8,128)S(1)} collective-permute-done((f32[256,128]{1,0:T(8,128)S(1)}, f32[256,128]{1,0:T(8,128)S(1)}, u32[]{:S(2)}, u32[]{:S(2)}) %collective-permute-start.2) | collective-permute-done | bytes 131104 | tf_op jit(solution)/shard_map/ppermute | solution.py:359
  43.6 3.8 %shard_map.63.mine_ref = f32[256,128]{1,0:T(8,128)S(1)} custom-call(bf16[2,3,128,128]{3,2,1,0:T(8,128)(2,1)S(1)} %copy-done.7, f32[8,128]{1,0:T(8,128)S(1)} %get-tuple-element.21.far_ref, f32[256,128]{1,0:T(8,128)S(1)} %get-tuple-element.27.mine_ref, f32[256,128]{1,0:T(8,128)S(1)} %collective-permute-done.2.other_ref), custom_call_target="tpu_custom_call" | custom-call | flops 1000000000 | bytes 1048576 | tf_op jit(solution)/shard_map/pallas_call | solution.py:339
  47.5 1.4 %collective-permute-start.3 = (f32[256,128]{1,0:T(8,128)S(1)}, f32[256,128]{1,0:T(8,128)S(1)}, u32[]{:S(2)}, u32[]{:S(2)}) collective-permute-start(f32[256,128]{1,0:T(8,128)S(1)} %shard_map.63.mine_ref), channel_id=1, source_target_pairs={{0,3},{1,2},{2,1},{3,0},{4,7},{5,6},{6,5},{7,4},{8,11},{9,10},{10,... | collective-permute-start | bytes 393224 | tf_op jit(solution)/shard_map/ppermute | solution.py:359
  48.9 3.9 %collective-permute-done.3.other_ref = f32[256,128]{1,0:T(8,128)S(1)} collective-permute-done((f32[256,128]{1,0:T(8,128)S(1)}, f32[256,128]{1,0:T(8,128)S(1)}, u32[]{:S(2)}, u32[]{:S(2)}) %collective-permute-start.3) | collective-permute-done | bytes 131104 | tf_op jit(solution)/shard_map/ppermute | solution.py:359
  52.8 3.8 %shard_map.64.mine_ref = f32[256,128]{1,0:T(8,128)S(1)} custom-call(bf16[2,3,128,128]{3,2,1,0:T(8,128)(2,1)S(1)} %get-tuple-element.23.pair_ref, f32[8,128]{1,0:T(8,128)S(1)} %get-tuple-element.21.far_ref, f32[256,128]{1,0:T(8,128)S(1)} %shard_map.63.mine_ref, f32[256,128]{1,0:T(8,128)S(1)} %collective-permute-done.3.other_ref), custom_call_target="tpu_custom_call" | custom-call | flops 1000000000 | bytes 1048576 | tf_op jit(solution)/shard_map/pallas_call | solution.py:339
  57.0 3.6 %collective-permute-done.4.other_ref = f32[256,128]{1,0:T(8,128)S(1)} collective-permute-done((f32[256,128]{1,0:T(8,128)S(1)}, f32[256,128]{1,0:T(8,128)S(1)}, u32[]{:S(2)}, u32[]{:S(2)}) %collective-permute-start.4) | collective-permute-done | bytes 131104 | tf_op jit(solution)/shard_map/ppermute | solution.py:359
  60.5 3.8 %shard_map.65.mine_ref = f32[256,128]{1,0:T(8,128)S(1)} custom-call(bf16[2,3,128,128]{3,2,1,0:T(8,128)(2,1)S(1)} %get-tuple-element.22.pair_ref, f32[8,128]{1,0:T(8,128)S(1)} %get-tuple-element.21.far_ref, f32[256,128]{1,0:T(8,128)S(1)} %shard_map.64.mine_ref, f32[256,128]{1,0:T(8,128)S(1)} %collective-permute-done.4.other_ref), custom_call_target="tpu_custom_call" | custom-call | flops 1000000000 | bytes 1048576 | tf_op jit(solution)/shard_map/pallas_call | solution.py:339
  64.5 5.0 %collective-permute-done.5.other_ref = f32[256,128]{1,0:T(8,128)S(1)} collective-permute-done((f32[256,128]{1,0:T(8,128)S(1)}, f32[256,128]{1,0:T(8,128)S(1)}, u32[]{:S(2)}, u32[]{:S(2)}) %collective-permute-start.5) | collective-permute-done | bytes 131104 | tf_op jit(solution)/shard_map/ppermute | solution.py:359
  69.5 3.8 %shard_map.66.mine_ref = f32[264,128]{1,0:T(8,128)S(1)} custom-call(bf16[2,3,128,128]{3,2,1,0:T(8,128)(2,1)S(1)} %get-tuple-element.20.pair_ref, f32[8,128]{1,0:T(8,128)S(1)} %get-tuple-element.21.far_ref, f32[256,128]{1,0:T(8,128)S(1)} %shard_map.65.mine_ref, f32[256,128]{1,0:T(8,128)S(1)} %collective-permute-done.5.other_ref), custom_call_target="tpu_custom_call" | custom-call | flops 1000000000 | bytes 1048576 | tf_op jit(solution)/shard_map/pallas_call | solution.py:339
  73.3 8.4 %collective-permute-start.6 = (f32[264,128]{1,0:T(8,128)S(1)}, f32[264,128]{1,0:T(8,128)S(1)}, u32[]{:S(2)}, u32[]{:S(2)}) collective-permute-start(f32[264,128]{1,0:T(8,128)S(1)} %shard_map.66.mine_ref), channel_id=1, source_target_pairs={{0,16},{16,0},{32,48},{48,32},{64,80},{80,64},{96,112},{112,96},{1... | collective-permute-start | bytes 405512 | tf_op jit(solution)/shard_map/ppermute | solution.py:364
  81.8 0.9 collective-permute-done.6.other_ref
  82.7 4.7 %shard_map.67.mine_ref = f32[264,128]{1,0:T(8,128)S(1)} custom-call(s32[2]{0:T(128)S(1)} %pad_add_fusion.2.second_ref, f32[264,128]{1,0:T(8,128)S(1)} %shard_map.66.mine_ref, f32[264,128]{1,0:T(8,128)S(1)} %collective-permute-done.6.other_ref), custom_call_target="tpu_custom_call" | custom-call | flops 1000000000 | bytes 1048576 | tf_op jit(solution)/shard_map/pallas_call | solution.py:339
  87.4 1.1 collective-permute-start.7
  88.5 1.0 shard_map.69
  89.5 3.5 %all-to-all-start.1 = ((f32[16,8,512]{2,1,0:T(8,128)}), f32[16,8,512]{2,1,0:T(8,128)S(1)}, u32[]{:S(2)}, u32[]{:S(2)}) async-start(f32[16,8,512]{2,1,0:T(8,128)} %shard_map.69), calls=%async_computation.1 | async-start | bytes 524288 | tf_op jit(solution)/shard_map/all_to_all | solution.py:436
  93.1 4.6 %shard_map.68 = (f32[264,128]{1,0:T(8,128)S(1)}, f32[136,128]{1,0:T(8,128)S(1)}) custom-call(s32[2]{0:T(128)S(1)} %pad_add_fusion.1.second_ref, f32[264,128]{1,0:T(8,128)S(1)} %shard_map.67.mine_ref, f32[264,128]{1,0:T(8,128)S(1)} %collective-permute-done.7.other_ref), custom_call_target="tpu_custom_call" | custom-call | flops 1000000000 | bytes 1048576 | tf_op jit(solution)/shard_map/pallas_call | solution.py:339
  97.7 1.6 %collective-permute-start.8 = (f32[136,128]{1,0:T(8,128)S(1)}, f32[136,128]{1,0:T(8,128)S(1)}, u32[]{:S(2)}, u32[]{:S(2)}) collective-permute-start(f32[136,128]{1,0:T(8,128)S(1)} %get-tuple-element.29), channel_id=1, source_target_pairs={{0,64},{16,80},{32,96},{48,112},{64,0},{80,16},{96,32},{112,48},{1... | collective-permute-start | bytes 208904 | tf_op jit(solution)/shard_map/ppermute | solution.py:364
  99.4 4.7 %collective-permute-done.8.direct_ref = f32[136,128]{1,0:T(8,128)S(1)} collective-permute-done((f32[136,128]{1,0:T(8,128)S(1)}, f32[136,128]{1,0:T(8,128)S(1)}, u32[]{:S(2)}, u32[]{:S(2)}) %collective-permute-start.8) | collective-permute-done | bytes 69664 | tf_op jit(solution)/shard_map/ppermute | solution.py:364
  105.7 5.5 %shard_map.70 = (f32[8,256]{1,0:T(8,128)}, f32[8,8192]{1,0:T(8,128)}) custom-call(s32[3]{0:T(128)S(1)} %pad_add_fusion.place_ref, f32[264,128]{1,0:T(8,128)S(1)} %get-tuple-element.28.mine_ref, f32[136,128]{1,0:T(8,128)S(1)} %collective-permute-done.8.direct_ref, f32[136,128]{1,0:T(8,128)S(1)} %collective-permute-done.9.passed_ref, ...), custom_call_target="tpu_custom_call" | custom-call | flops 1000000000 | bytes 1048576 | tf_op jit(solution)/shard_map/pallas_call | solution.py:339
  (23 shorter events, 3.3 us)
Async XLA Ops:
  2.1 4.4 %collective-permute-start = (f32[16,512]{1,0:T(8,128)}, f32[16,512]{1,0:T(8,128)S(1)}, u32[]{:S(2)}, u32[]{:S(2)}) collective-permute-start(f32[16,512]{1,0:T(8,128)} %get-tuple-element.18), channel_id=1, source_target_pairs={{0,16},{16,32},{32,48},{48,64},{64,80},{80,96},{96,112},{112,128},... | collective-permute-start | bytes 98312 | tf_op jit(solution)/shard_map/ppermute | solution.py:390
  5.1 3.6 %collective-permute-start.1 = (f32[16,512]{1,0:T(8,128)}, f32[16,512]{1,0:T(8,128)S(1)}, u32[]{:S(2)}, u32[]{:S(2)}) collective-permute-start(f32[16,512]{1,0:T(8,128)} %get-tuple-element.19), channel_id=1, source_target_pairs={{0,240},{16,0},{32,16},{48,32},{64,48},{80,64},{96,80},{112,96},{1... | collective-permute-start | bytes 98312 | tf_op jit(solution)/shard_map/ppermute | solution.py:391
  8.7 1.0 copy-start.2
  9.6 0.9 copy-start.5
  11.6 6.9 %copy-start.3 = (f32[2,8192]{1,0:T(2,128)S(1)}, f32[2,8192]{1,0:T(2,128)}, u32[]{:S(2)}) copy-start(f32[2,8192]{1,0:T(2,128)} %coords_ref.1) | copy-start | bytes 196612
  11.6 6.9 %copy-start.4 = (f32[8192]{0:T(1024)S(1)}, f32[8192]{0:T(1024)}, u32[]{:S(2)}) copy-start(f32[8192]{0:T(1024)} %param.5) | copy-start | bytes 98308
  11.6 21.9 %all-to-all-start = ((f32[16,4,8,512]{3,2,1,0:T(8,128)}), f32[16,4,8,512]{3,2,1,0:T(8,128)S(1)}, u32[]{:S(2)}, u32[]{:S(2)}) async-start(f32[16,4,8,512]{3,2,1,0:T(8,128)} %shard_map.61), calls=%async_computation | async-start | bytes 2097152 | tf_op jit(solution)/shard_map/all_to_all | solution.py:404
  23.4 1.2 %copy-start = (bf16[1536,512]{1,0:T(8,128)(2,1)}, bf16[1536,512]{1,0:T(8,128)(2,1)S(1)}, u32[]{:S(2)}) copy-start(bf16[1536,512]{1,0:T(8,128)(2,1)S(1)} %get-tuple-element.26.near_mid_hbm) | copy-start | bytes 4718596
  24.6 0.7 copy-start.6
  33.5 1.4 %copy-start.1 = (bf16[1536,512]{1,0:T(8,128)(2,1)S(1)}, bf16[1536,512]{1,0:T(8,128)(2,1)}, u32[]{:S(2)}) copy-start(bf16[1536,512]{1,0:T(8,128)(2,1)} %copy-done) | copy-start | bytes 4718596
  35.0 8.7 %copy-start.7 = (bf16[2,3,128,128]{3,2,1,0:T(8,128)(2,1)S(1)}, bf16[2,3,128,128]{3,2,1,0:T(8,128)(2,1)}, u32[]{:S(2)}) copy-start(bf16[2,3,128,128]{3,2,1,0:T(8,128)(2,1)} %copy-done.6) | copy-start | bytes 589828
  39.7 3.9 %collective-permute-start.2 = (f32[256,128]{1,0:T(8,128)S(1)}, f32[256,128]{1,0:T(8,128)S(1)}, u32[]{:S(2)}, u32[]{:S(2)}) collective-permute-start(f32[256,128]{1,0:T(8,128)S(1)} %get-tuple-element.27.mine_ref), channel_id=1, source_target_pairs={{0,1},{1,0},{2,3},{3,2},{4,5},{5,4},{6,7},{7,6},{8,9},{9,8},{10,11... | collective-permute-start | bytes 393224 | tf_op jit(solution)/shard_map/ppermute | solution.py:359
  47.5 5.3 %collective-permute-start.3 = (f32[256,128]{1,0:T(8,128)S(1)}, f32[256,128]{1,0:T(8,128)S(1)}, u32[]{:S(2)}, u32[]{:S(2)}) collective-permute-start(f32[256,128]{1,0:T(8,128)S(1)} %shard_map.63.mine_ref), channel_id=1, source_target_pairs={{0,3},{1,2},{2,1},{3,0},{4,7},{5,6},{6,5},{7,4},{8,11},{9,10},{10,... | collective-permute-start | bytes 393224 | tf_op jit(solution)/shard_map/ppermute | solution.py:359
  56.6 3.9 %collective-permute-start.4 = (f32[256,128]{1,0:T(8,128)S(1)}, f32[256,128]{1,0:T(8,128)S(1)}, u32[]{:S(2)}, u32[]{:S(2)}) collective-permute-start(f32[256,128]{1,0:T(8,128)S(1)} %shard_map.64.mine_ref), channel_id=1, source_target_pairs={{0,4},{1,5},{2,6},{3,7},{4,0},{5,1},{6,2},{7,3},{8,12},{9,13},{10,... | collective-permute-start | bytes 393224 | tf_op jit(solution)/shard_map/ppermute | solution.py:359
  64.4 5.1 %collective-permute-start.5 = (f32[256,128]{1,0:T(8,128)S(1)}, f32[256,128]{1,0:T(8,128)S(1)}, u32[]{:S(2)}, u32[]{:S(2)}) collective-permute-start(f32[256,128]{1,0:T(8,128)S(1)} %shard_map.65.mine_ref), channel_id=1, source_target_pairs={{0,12},{1,13},{2,14},{3,15},{4,8},{5,9},{6,10},{7,11},{8,4},{9,5},... | collective-permute-start | bytes 393224 | tf_op jit(solution)/shard_map/ppermute | solution.py:359
  73.3 9.4 %collective-permute-start.6 = (f32[264,128]{1,0:T(8,128)S(1)}, f32[264,128]{1,0:T(8,128)S(1)}, u32[]{:S(2)}, u32[]{:S(2)}) collective-permute-start(f32[264,128]{1,0:T(8,128)S(1)} %shard_map.66.mine_ref), channel_id=1, source_target_pairs={{0,16},{16,0},{32,48},{48,32},{64,80},{80,64},{96,112},{112,96},{1... | collective-permute-start | bytes 405512 | tf_op jit(solution)/shard_map/ppermute | solution.py:364
  87.4 5.7 %collective-permute-start.7 = (f32[264,128]{1,0:T(8,128)S(1)}, f32[264,128]{1,0:T(8,128)S(1)}, u32[]{:S(2)}, u32[]{:S(2)}) collective-permute-start(f32[264,128]{1,0:T(8,128)S(1)} %shard_map.67.mine_ref), channel_id=1, source_target_pairs={{0,32},{16,48},{32,0},{48,16},{64,96},{80,112},{96,64},{112,80},{1... | collective-permute-start | bytes 405512 | tf_op jit(solution)/shard_map/ppermute | solution.py:364
  89.5 15.3 %all-to-all-start.1 = ((f32[16,8,512]{2,1,0:T(8,128)}), f32[16,8,512]{2,1,0:T(8,128)S(1)}, u32[]{:S(2)}, u32[]{:S(2)}) async-start(f32[16,8,512]{2,1,0:T(8,128)} %shard_map.69), calls=%async_computation.1 | async-start | bytes 524288 | tf_op jit(solution)/shard_map/all_to_all | solution.py:436
  97.7 6.3 %collective-permute-start.8 = (f32[136,128]{1,0:T(8,128)S(1)}, f32[136,128]{1,0:T(8,128)S(1)}, u32[]{:S(2)}, u32[]{:S(2)}) collective-permute-start(f32[136,128]{1,0:T(8,128)S(1)} %get-tuple-element.29), channel_id=1, source_target_pairs={{0,64},{16,80},{32,96},{48,112},{64,0},{80,16},{96,32},{112,48},{1... | collective-permute-start | bytes 208904 | tf_op jit(solution)/shard_map/ppermute | solution.py:364
  104.0 1.7 %collective-permute-start.9 = (f32[136,128]{1,0:T(8,128)S(1)}, f32[136,128]{1,0:T(8,128)S(1)}, u32[]{:S(2)}, u32[]{:S(2)}) collective-permute-start(f32[136,128]{1,0:T(8,128)S(1)} %collective-permute-done.8.direct_ref), channel_id=1, source_target_pairs={{0,16},{16,0},{32,48},{48,32},{64,80},{80,64},{96,112},{112,96},{1... | collective-permute-start | bytes 208904 | tf_op jit(solution)/shard_map/ppermute | solution.py:364

commit v2 on v1

--- a/solution.py
+++ b/solution.py
@@ -64,16 +64,25 @@
         for g in range(groups)
     ]
     scales = [jnp.zeros((SUB, S), F32)] * groups
+    factors = []
+
+    def update(j, k):
+        gj, sj = divmod(j, SUB)
+        other = factors[k][gj][sj : sj + 1]
+        for g in range(gj, groups):
+            cols[j][g] = cols[j][g] - factors[k][g] * other
+
     for k in range(n):
         gk, sk = divmod(k, SUB)
         scale = lax.rsqrt(jnp.broadcast_to(cols[k][gk][sk : sk + 1], (SUB, S)))
         factor = {g: cols[k][g] * scale for g in range(gk, groups)}
+        factors.append(dict(factor))
         scales[gk] = jnp.where(sub == sk, scale, scales[gk])
-        for j in range(k + 1, n):
-            gj, sj = divmod(j, SUB)
-            other = factor[gj][sj : sj + 1]
-            for g in range(gj, groups):
-                cols[j][g] = cols[j][g] - factor[g] * other
+        if k + 1 < n:
+            update(k + 1, k)
+        if k + 2 < n:
+            for earlier in range(k + 1):
+                update(k + 2, earlier)
         factor[gk] = jnp.where(sub > sk, factor[gk], 0.0)
         for t in range(tiles):
             pivot_row = work[gk][t][sk : sk + 1] * scale
@@ -131,9 +140,9 @@
 
 def prepare_kernel(
     rep_ref, coords_ref, density_ref, low_ref, high_ref,
-    near_high_ref, near_mid_ref, far_ref, *rest,
+    near_high_ref, near_mid_hbm, far_ref, *rest,
 ):
-    pair_refs, (wide, window, skeleton) = rest[:-3], rest[-3:]
+    pair_refs, (wide, window, skeleton, near_mid_ref, sem) = rest[:-5], rest[-5:]
     rep = rep_ref[0]
     width = coords_ref.shape[1]
     cells = width // LEAF
@@ -160,6 +169,8 @@
         return carry
 
     lax.fori_loop(0, 3 * LEAF // S, near_chunk, 0)
+    store = pltpu.make_async_copy(near_mid_ref, near_mid_hbm, sem)
+    store.start()
 
     leaves = [wide[:, LEAF * (i + 1) : LEAF * (i + 2)] for i in range(cells)]
     nodes = pick(jnp.concatenate(leaves, 0), STEP)
@@ -186,6 +197,7 @@
         float(STEP << len(pair_refs)), 1.0,
     )
     far_ref[...] = nodes * scale
+    store.wait()
 
 
 def edges_kernel(
@@ -207,17 +219,42 @@
     return jnp.where(turned == 1, index % 4 * 4 + index // 4, index)
 
 
-def pack_kernel(turned_ref, samples_ref, tests_ref, low_ref, high_ref, out_ref, wide):
-    width = samples_ref.shape[1]
-    wide[:, :LEAF] = low_ref[:SUB]
-    wide[:, LEAF : LEAF + width] = tests_ref[...]
-    wide[:, LEAF + width :] = high_ref[:SUB]
-    for i in range(out_ref.shape[0]):
+def pack_kernel(turned_ref, samples_ref, tests_ref, out_ref, sems):
+    cells = out_ref.shape[0]
+    copies = []
+
+    def move(source, leaf, i, slot):
+        start = pl.multiple_of(leaf * LEAF, LEAF)
+        copies.append(
+            pltpu.make_async_copy(
+                source.at[:, pl.ds(start, LEAF)], out_ref.at[i, slot], sems.at[len(copies)]
+            )
+        )
+        copies[-1].start()
+
+    for i in range(cells):
         leaf = turn(jnp.int32(i), turned_ref[0])
-        out_ref[i, 0] = samples_ref[:, pl.ds(pl.multiple_of(leaf * LEAF, LEAF), LEAF)]
-        for side in range(3):
-            start = pl.multiple_of((leaf + side) * LEAF, LEAF)
-            out_ref[i, side + 1] = wide[:, pl.ds(start, LEAF)]
+        move(samples_ref, leaf, i, 0)
+        if i > 0:
+            move(tests_ref, leaf - 1, i, 1)
+        move(tests_ref, leaf, i, 2)
+        if i < cells - 1:
+            move(tests_ref, leaf + 1, i, 3)
+    for copy in copies:
+        copy.wait()
+
+
+def ends_kernel(packed_ref, low_ref, high_ref, out_ref, sems):
+    copies = [
+        pltpu.make_async_copy(low_ref.at[:SUB], out_ref.at[0, 1], sems.at[0]),
+        pltpu.make_async_copy(
+            high_ref.at[:SUB], out_ref.at[out_ref.shape[0] - 1, 3], sems.at[1]
+        ),
+    ]
+    for copy in copies:
+        copy.start()
+    for copy in copies:
+        copy.wait()
 
 
 def leaf_kernel(
@@ -274,33 +311,34 @@
     return eliminate(nn(left, split3(jnp.concatenate([mine, other], 0))))
 
 
-def near_parent_kernel(pair_ref, far_ref, mine_ref, other_ref, hat_ref):
+def far_kernel(second_ref, mine_ref, other_ref, pair_ref, *joined_refs):
+    mine, other = mine_ref[...], other_ref[...]
+    for side, block in enumerate(coupling(mine, other, LOG_SCALE)):
+        for part, value in enumerate(split3(block)):
+            pair_ref[side, part] = value
+    second = second_ref[0] == 1
+    joined = jnp.concatenate(
+        [jnp.where(second, other, mine), jnp.where(second, mine, other)], 1
+    )
+    double = lax.broadcasted_iota(jnp.int32, (SUB, S), 0) == 2
+    for ref in joined_refs:
+        ref[...] = pick(joined, 2) * jnp.where(double, 2.0, 1.0)
+
+
+def parent_kernel(pair_ref, mine_ref, other_ref, hat_ref):
     pair = [[pair_ref[side, part] for part in range(3)] for side in range(2)]
     got = merge(*pair, mine_ref, other_ref)
     hat_ref[:S] = got[:, :S]
-    hat_ref[S : 2 * S] = got[:, S:]
-    if hat_ref.shape[0] > 2 * S:
-        hat_ref[2 * S :] = far_ref[...]
-
-
-def far_parent_kernel(second_ref, mine_ref, other_ref, hat_ref, *half_refs):
-    mine, other = mine_ref[2 * S :], other_ref[2 * S :]
-    to_mine, to_other = coupling(mine, other, LOG_SCALE)
-    got = merge(split3(to_mine), split3(to_other), mine_ref, other_ref)
-    hat_ref[:S] = got[:, :S]
-    hat_ref[S : 2 * S] = got[:, S:]
-    second = second_ref[0] == 1
-    joined = jnp.concatenate(
-        [jnp.where(second, other, mine), jnp.where(second, mine, other)], 1
-    )
-    double = lax.broadcasted_iota(jnp.int32, (SUB, S), 0) == 2
-    hat_ref[2 * S :] = pick(joined, 2) * jnp.where(double, 2.0, 1.0)
-    for half_ref in half_refs:
-        half_ref[...] = jnp.where(second_ref[1] == 1, hat_ref[S:], hat_ref[: S + SUB])
+    hat_ref[S:] = got[:, S:]
+
+
+def last_parent_kernel(turned_ref, pair_ref, mine_ref, other_ref, hat_ref, half_ref):
+    parent_kernel(pair_ref, mine_ref, other_ref, hat_ref)
+    half_ref[...] = jnp.where(turned_ref[0] == 1, hat_ref[S:], hat_ref[:S])
 
 
 def top_kernel(
-    place_ref, mine_ref, direct_ref, passed_ref, parts_ref, q_ref, basis_ref,
+    place_ref, pair_ref, mine_ref, direct_ref, passed_ref, parts_ref, q_ref, basis_ref,
     all_rows, other_ref, sems,
 ):
     copies = []
@@ -310,13 +348,10 @@
         copies.append(pltpu.make_async_copy(parts_ref.at[i], to, sems.at[i]))
         copies[-1].start()
     upper_direct = place_ref[2] == 0
-    other_ref[: S + SUB] = jnp.where(upper_direct, direct_ref[...], passed_ref[...])
+    other_ref[:S] = jnp.where(upper_direct, direct_ref[...], passed_ref[...])
     other_ref[S:] = jnp.where(upper_direct, passed_ref[...], direct_ref[...])
-    mine, other = mine_ref[2 * S :], other_ref[2 * S :]
-    to_mine, to_other = coupling(mine, other, LOG_SCALE)
-    z_mine, z_other = off_diagonal(
-        split3(to_mine), split3(to_other), mine_ref, other_ref
-    )
+    pair = [[pair_ref[side, part] for part in range(3)] for side in range(2)]
+    z_mine, z_other = off_diagonal(*pair, mine_ref, other_ref)
     second = place_ref[0] == 1
     first = jnp.where(second, z_other, z_mine)
     last = jnp.where(second, z_mine, z_other)
@@ -333,15 +368,17 @@
 VMEM = pl.BlockSpec(memory_space=pltpu.VMEM)
 SMEM = pl.BlockSpec(memory_space=pltpu.SMEM)
 ANY = pl.BlockSpec(memory_space=pl.ANY)
-
-
-def call(kernel, outs, specs, *operands, out_specs=None, scratch=(), flops=10**9):
+HBM = pl.BlockSpec(memory_space=pltpu.HBM)
+
+
+def call(kernel, outs, specs, *operands, out_specs=None, scratch=(), aliases={}, flops=10**9):
     return pl.pallas_call(
         kernel,
         out_shape=[jax.ShapeDtypeStruct(shape, kind) for shape, kind in outs],
         in_specs=specs,
         out_specs=out_specs or [VMEM] * len(outs),
         scratch_shapes=list(scratch),
+        input_output_aliases=aliases,
         compiler_params=pltpu.CompilerParams(vmem_limit_bytes=VMEM_LIMIT),
         cost_estimate=pl.CostEstimate(
             flops=flops, bytes_accessed=2**20, transcendentals=0
@@ -393,13 +430,24 @@
     (parcels,) = call(
         pack_kernel,
         [((cells, 4, columns, LEAF), F32)],
-        [SMEM] + [VMEM] * 4,
+        [SMEM, HBM, HBM],
         turned.reshape(1),
         sketch_matrix,
         random_test_matrix,
+        out_specs=[HBM],
+        scratch=[pltpu.SemaphoreType.DMA((4 * cells - 2,))],
+    )
+    (parcels,) = call(
+        ends_kernel,
+        [((cells, 4, columns, LEAF), F32)],
+        [HBM, HBM, HBM],
+        parcels,
         low,
         high,
-        scratch=[pltpu.VMEM((columns, width + 2 * LEAF), F32)],
+        out_specs=[HBM],
+        scratch=[pltpu.SemaphoreType.DMA((2,))],
+        aliases={0: 0},
+        flops=10**6,
     )
     data = lax.all_to_all(parcels, "rep", 0, 0)
 
@@ -418,13 +466,16 @@
             pltpu.VMEM((SUB, width + 2 * LEAF), F32),
             pltpu.VMEM((SUB, 3 * LEAF), F32),
             pltpu.VMEM((cells, SUB, S), F32),
+            pltpu.VMEM((3 * LEAF, LEAF), BF16),
+            pltpu.SemaphoreType.DMA,
         ],
+        out_specs=[VMEM, HBM] + [VMEM] * (cell_levels + 1),
         flops=10**10,
     )
     z, inverse, hat = call(
         leaf_kernel,
         [((S, LEAF), F32), ((S, S), F32), ((2 * S, S), F32)],
-        [VMEM, VMEM, ANY],
+        [VMEM, VMEM, HBM],
         data,
         near_high,
         near_mid,
@@ -435,28 +486,42 @@
     )
     parts = lax.all_to_all(basis, "rep", 0, 0)
 
-    for level, masks in enumerate(((1, 4), (3, 12), (4, 1), (12, 3))):
-        other = swap(hat, *masks)
-        rows = 2 * S + (SUB if level == cell_levels - 1 else 0)
+    skeleton = far
+    for level in range(3):
+        pair, *joined = call(
+            far_kernel,
+            [((2, 3, S, S), BF16), ((SUB, S), F32)][: 2 - level // 2],
+            [SMEM] + [VMEM] * 2,
+            (leaf >> level & 1).reshape(1),
+            skeleton,
+            cross(skeleton, 1 << level),
+        )
+        pairs.append(pair)
+        skeleton = joined[0] if joined else None
+
+    for pair, masks in zip(pairs, ((1, 4), (3, 12), (4, 1), (12, 3))):
         (hat,) = call(
-            near_parent_kernel, [((rows, S), F32)], [VMEM] * 4, pairs[level], far, hat, other
+            parent_kernel, [((2 * S, S), F32)], [VMEM] * 3, pair, hat, swap(hat, *masks)
         )
-    for level in range(2):
-        other = cross(hat, 1 << level)
-        hat, *half = call(
-            far_parent_kernel,
-            [((2 * S + SUB, S), F32), ((S + SUB, S), F32)][: level + 1],
-            [SMEM] + [VMEM] * 2,
-            jnp.stack([leaf >> level & 1, turned]),
-            hat,
-            other,
-        )
-    direct = cross(half[0], 4)
+    (hat,) = call(
+        parent_kernel, [((2 * S, S), F32)], [VMEM] * 3, pairs[-3], hat, cross(hat, 1)
+    )
+    hat, half = call(
+        last_parent_kernel,
+        [((2 * S, S), F32), ((S, S), F32)],
+        [SMEM] + [VMEM] * 3,
+        turned.reshape(1),
+        pairs[-2],
+        hat,
+        cross(hat, 2),
+    )
+    direct = cross(half, 4)
     top, leaf_basis = call(
         top_kernel,
         [((columns, 2 * S), F32), ((columns, width), F32)],
-        [SMEM] + [VMEM] * 3 + [ANY],
+        [SMEM] + [VMEM] * 4 + [ANY],
         jnp.stack([leaf >> 2 & 1, rep, turned]),
+        pairs[-1],
         hat,
         direct,
         cross(direct, 1),
@@ -464,7 +529,7 @@
         out_specs=[VMEM, ANY],
         scratch=[
             pltpu.VMEM((S, 2 * S), F32),
-            pltpu.VMEM((2 * S + SUB, S), F32),
+            pltpu.VMEM((2 * S, S), F32),
             pltpu.SemaphoreType.DMA((cells,)),
         ],
     )

time: 112 us -> 111 us (level)
  starting transfers between devices: 27.5 us -> 33.5 us
  waiting for transfers between devices: 34.3 us -> 28.4 us
    ppermute x4 -> x7, starting transfers between devices: 11.9 us -> 16.9 us  [cross(): return lax.ppermute(block, 'leaf', [(i, i ^ mask) for i in range(count)])]
    ppermute x1, waiting for transfers between devices: 2.21 us -> 0.01 us  [body(): lax.ppermute(high, 'leaf', [(i, (i - 1) % count) for i in range(count)])]
    all_to_all x1, waiting for transfers between devices: 8.31 us -> 6.61 us  [body(): data = lax.all_to_all(parcels, 'rep', 0, 0)]
    ppermute x1, waiting for transfers between devices: 1.12 us -> 0.01 us  [body(): lax.ppermute(low, 'leaf', [(i, (i + 1) % count) for i in range(count)])]
    ppermute x4, waiting for transfers between devices: 16.3 us -> 15.2 us  [swap(): return lax.ppermute(block, ('leaf', 'rep'), route)]
    pallas_call x11 -> x15, Pallas kernels: 41.7 us -> 40.9 us  [call(): pl.pallas_call(kernel, out_shape=[jax.ShapeDtypeStruct(shape, kind) for s...]
    ppermute x4 -> x7, waiting for transfers between devices: 6.41 us -> 6.65 us  [cross(): return lax.ppermute(block, 'leaf', [(i, i ^ mask) for i in range(count)])]
  transfers between devices with their start and end apart: 12 -> 15, of which waited for: 10 -> 8; matrix products, arithmetic and copies ran while one was open for 0% -> 0% of each run, Pallas kernels for 9% -> 14%
where the time goes in v2:
time: 111 us
  Pallas kernels  42.3 us (38%)
  starting transfers between devices  33.5 us (30%)
  waiting for transfers between devices  28.4 us (26%)
  local copies, waits for them, and re-layouts  5.19 us (5%)
    pallas_call x15, Pallas kernels, call(): pl.pallas_call(kernel, out_shape=[jax.ShapeDtypeStruct(shape, kind) for s...  40.9 us
    ppermute x7, starting transfers between devices, cross(): return lax.ppermute(block, 'leaf', [(i, i ^ mask) for i in range(count)])  16.9 us
    ppermute x4, waiting for transfers between devices, swap(): return lax.ppermute(block, ('leaf', 'rep'), route)  15.2 us
    all_to_all x1, starting transfers between devices, body(): data = lax.all_to_all(parcels, 'rep', 0, 0)  6.78 us
    ppermute x7, waiting for transfers between devices, cross(): return lax.ppermute(block, 'leaf', [(i, i ^ mask) for i in range(count)])  6.65 us
    all_to_all x1, waiting for transfers between devices, body(): data = lax.all_to_all(parcels, 'rep', 0, 0)  6.61 us
    unnamed x16, local copies, waits for them, and re-layouts  5.19 us
    all_to_all x1, starting transfers between devices, body(): parts = lax.all_to_all(basis, 'rep', 0, 0)  3.53 us
  transfers between devices with their start and end apart: 15, of which 8 were waited for; matrix products, arithmetic and copies ran while one was open for 0% of the time, Pallas kernels for 14%

profile of v2, /device:TPU:1, one launch (start us, length us, event | category | flops | bytes accessed | tf_op | source)
XLA Modules:
  0.0 110.5 jit_solution(7779077483339244814)
XLA Ops:
  0.6 1.5 %shard_map.59 = (f32[16,512]{1,0:T(8,128)}, f32[16,512]{1,0:T(8,128)}) custom-call(f32[8,8192]{1,0:T(8,128)} %tests_ref.1, f32[8,8192]{1,0:T(8,128)} %tests_ref.1, f32[2,8192]{1,0:T(2,128)} %coords_ref.1, f32[2,8192]{1,0:T(2,128)} %coords_ref.1, f32[1,8192]{1,0:T(1,128)} %bitcast.8), custom_call_target="tpu_custom_call" | custom-call | tf_op jit(solution)/shard_map/pallas_call | solution.py:419
  2.1 3.0 %collective-permute-start = (f32[16,512]{1,0:T(8,128)}, f32[16,512]{1,0:T(8,128)S(1)}, u32[]{:S(2)}, u32[]{:S(2)}) collective-permute-start(f32[16,512]{1,0:T(8,128)} %get-tuple-element.22), channel_id=1, source_target_pairs={{0,16},{16,32},{32,48},{48,64},{64,80},{80,96},{96,112},{112,128},... | collective-permute-start | bytes 98312 | tf_op jit(solution)/shard_map/ppermute | solution.py:427
  5.3 0.9 copy-done.2
  6.3 0.9 copy-done.5
  7.2 1.5 %shard_map.64.packed_ref = f32[16,4,8,512]{3,2,1,0:T(8,128)} custom-call(s32[1]{0:T(128)} %bitcast.2.turned_ref, f32[8,8192]{1,0:T(8,128)S(1)} %copy-done.5, f32[8,8192]{1,0:T(8,128)S(1)} %copy-done.2), custom_call_target="tpu_custom_call" | custom-call | flops 1000000000 | bytes 1048576 | tf_op jit(solution)/shard_map/pallas_call | solution.py:375
  9.5 6.8 %all-to-all-start = ((f32[16,4,8,512]{3,2,1,0:T(8,128)}), f32[16,4,8,512]{3,2,1,0:T(8,128)S(1)}, u32[]{:S(2)}, u32[]{:S(2)}) async-start(f32[16,4,8,512]{3,2,1,0:T(8,128)} %shard_map.65), calls=%async_computation | async-start | bytes 2097152 | tf_op jit(solution)/shard_map/all_to_all | solution.py:452
  16.3 4.9 %shard_map.60 = (bf16[1536,512]{1,0:T(8,128)(2,1)S(1)}, bf16[1536,512]{1,0:T(8,128)(2,1)S(1)}, f32[8,128]{1,0:T(8,128)S(1)}, bf16[2,3,128,128]{3,2,1,0:T(8,128)(...) custom-call(s32[1]{0:T(128)} %bitcast.5.rep_ref, ...), custom_call_target="tpu_custom_call" | custom-call | flops 10000000000 | bytes 1048576 | tf_op jit(solution)/shard_map/pallas_call | solution.py:375
  21.2 1.2 %copy-done = bf16[1536,512]{1,0:T(8,128)(2,1)} copy-done((bf16[1536,512]{1,0:T(8,128)(2,1)}, bf16[1536,512]{1,0:T(8,128)(2,1)S(1)}, u32[]{:S(2)}) %copy-start) | copy-done | bytes 1572888
  23.1 6.6 %all-to-all-done.data_ref = f32[16,4,8,512]{3,2,1,0:T(8,128)S(1)} async-done(((f32[16,4,8,512]{3,2,1,0:T(8,128)}), f32[16,4,8,512]{3,2,1,0:T(8,128)S(1)}, u32[]{:S(2)}, u32[]{:S(2)}) %all-to-all-start) | async-done | bytes 1048608 | tf_op jit(solution)/shard_map/all_to_all | solution.py:452
  29.7 1.4 %copy-done.1 = bf16[1536,512]{1,0:T(8,128)(2,1)S(1)} copy-done((bf16[1536,512]{1,0:T(8,128)(2,1)S(1)}, bf16[1536,512]{1,0:T(8,128)(2,1)}, u32[]{:S(2)}) %copy-start.1) | copy-done | bytes 1572888
  31.1 4.7 %shard_map.66 = (f32[128,512]{1,0:T(8,128)S(1)}, f32[128,128]{1,0:T(8,128)S(1)}, f32[256,128]{1,0:T(8,128)S(1)}) custom-call(f32[16,4,8,512]{3,2,1,0:T(8,128)S(1)} %all-to-all-done.data_ref, bf16[1536,512]{1,0:T(8,128)(2,1)S(1)} %get-tuple-element.33.near_high_ref, bf16[1536,512]{1,0:T(8,128)(2,1)S(1)} %copy-done.1), custom_call_target="tpu_custom_call" | custom-call | flops 1000000000 | bytes 1048576 | tf_op jit(solution)/shard_map/pallas_call | solution.py:375
  35.9 3.8 %collective-permute-done.5.other_ref = f32[256,128]{1,0:T(8,128)S(1)} collective-permute-done((f32[256,128]{1,0:T(8,128)S(1)}, f32[256,128]{1,0:T(8,128)S(1)}, u32[]{:S(2)}, u32[]{:S(2)}) %collective-permute-start.5) | collective-permute-done | bytes 131104 | tf_op jit(solution)/shard_map/ppermute | solution.py:396
  39.7 3.7 %shard_map.67.mine_ref = f32[256,128]{1,0:T(8,128)S(1)} custom-call(bf16[2,3,128,128]{3,2,1,0:T(8,128)(2,1)S(1)} %copy-done.7, f32[256,128]{1,0:T(8,128)S(1)} %get-tuple-element.35.mine_ref, f32[256,128]{1,0:T(8,128)S(1)} %collective-permute-done.5.other_ref), custom_call_target="tpu_custom_call" | custom-call | flops 1000000000 | bytes 1048576 | tf_op jit(solution)/shard_map/pallas_call | solution.py:375
  43.4 1.6 %collective-permute-start.6 = (f32[256,128]{1,0:T(8,128)S(1)}, f32[256,128]{1,0:T(8,128)S(1)}, u32[]{:S(2)}, u32[]{:S(2)}) collective-permute-start(f32[256,128]{1,0:T(8,128)S(1)} %shard_map.67.mine_ref), channel_id=1, source_target_pairs={{0,3},{1,2},{2,1},{3,0},{4,7},{5,6},{6,5},{7,4},{8,11},{9,10},{10,... | collective-permute-start | bytes 393224 | tf_op jit(solution)/shard_map/ppermute | solution.py:396
  45.0 3.7 %collective-permute-done.6.other_ref = f32[256,128]{1,0:T(8,128)S(1)} collective-permute-done((f32[256,128]{1,0:T(8,128)S(1)}, f32[256,128]{1,0:T(8,128)S(1)}, u32[]{:S(2)}, u32[]{:S(2)}) %collective-permute-start.6) | collective-permute-done | bytes 131104 | tf_op jit(solution)/shard_map/ppermute | solution.py:396
  48.7 3.7 %shard_map.68.mine_ref = f32[256,128]{1,0:T(8,128)S(1)} custom-call(bf16[2,3,128,128]{3,2,1,0:T(8,128)(2,1)S(1)} %get-tuple-element.31.pair_ref, f32[256,128]{1,0:T(8,128)S(1)} %shard_map.67.mine_ref, f32[256,128]{1,0:T(8,128)S(1)} %collective-permute-done.6.other_ref), custom_call_target="tpu_custom_call" | custom-call | flops 1000000000 | bytes 1048576 | tf_op jit(solution)/shard_map/pallas_call | solution.py:375
  52.4 1.3 %collective-permute-start.7 = (f32[256,128]{1,0:T(8,128)S(1)}, f32[256,128]{1,0:T(8,128)S(1)}, u32[]{:S(2)}, u32[]{:S(2)}) collective-permute-start(f32[256,128]{1,0:T(8,128)S(1)} %shard_map.68.mine_ref), channel_id=1, source_target_pairs={{0,4},{1,5},{2,6},{3,7},{4,0},{5,1},{6,2},{7,3},{8,12},{9,13},{10,... | collective-permute-start | bytes 393224 | tf_op jit(solution)/shard_map/ppermute | solution.py:396
  53.7 2.7 %collective-permute-done.7.other_ref = f32[256,128]{1,0:T(8,128)S(1)} collective-permute-done((f32[256,128]{1,0:T(8,128)S(1)}, f32[256,128]{1,0:T(8,128)S(1)}, u32[]{:S(2)}, u32[]{:S(2)}) %collective-permute-start.7) | collective-permute-done | bytes 131104 | tf_op jit(solution)/shard_map/ppermute | solution.py:396
  56.3 3.7 %shard_map.69.mine_ref = f32[256,128]{1,0:T(8,128)S(1)} custom-call(bf16[2,3,128,128]{3,2,1,0:T(8,128)(2,1)S(1)} %get-tuple-element.30.pair_ref, f32[256,128]{1,0:T(8,128)S(1)} %shard_map.68.mine_ref, f32[256,128]{1,0:T(8,128)S(1)} %collective-permute-done.7.other_ref), custom_call_target="tpu_custom_call" | custom-call | flops 1000000000 | bytes 1048576 | tf_op jit(solution)/shard_map/pallas_call | solution.py:375
  60.1 5.0 %collective-permute-done.8.other_ref = f32[256,128]{1,0:T(8,128)S(1)} collective-permute-done((f32[256,128]{1,0:T(8,128)S(1)}, f32[256,128]{1,0:T(8,128)S(1)}, u32[]{:S(2)}, u32[]{:S(2)}) %collective-permute-start.8) | collective-permute-done | bytes 131104 | tf_op jit(solution)/shard_map/ppermute | solution.py:396
  65.1 3.7 %shard_map.70.mine_ref = f32[256,128]{1,0:T(8,128)S(1)} custom-call(bf16[2,3,128,128]{3,2,1,0:T(8,128)(2,1)S(1)} %get-tuple-element.29.pair_ref, f32[256,128]{1,0:T(8,128)S(1)} %shard_map.69.mine_ref, f32[256,128]{1,0:T(8,128)S(1)} %collective-permute-done.8.other_ref), custom_call_target="tpu_custom_call" | custom-call | flops 1000000000 | bytes 1048576 | tf_op jit(solution)/shard_map/pallas_call | solution.py:375
  68.9 9.8 %collective-permute-start.9 = (f32[256,128]{1,0:T(8,128)S(1)}, f32[256,128]{1,0:T(8,128)S(1)}, u32[]{:S(2)}, u32[]{:S(2)}) collective-permute-start(f32[256,128]{1,0:T(8,128)S(1)} %shard_map.70.mine_ref), channel_id=1, source_target_pairs={{0,16},{16,0},{32,48},{48,32},{64,80},{80,64},{96,112},{112,96},{1... | collective-permute-start | bytes 393224 | tf_op jit(solution)/shard_map/ppermute | solution.py:401
  78.7 1.1 collective-permute-done.2.other_ref
  80.0 2.1 %collective-permute-start.3 = (f32[8,128]{1,0:T(8,128)S(1)}, f32[8,128]{1,0:T(8,128)S(1)}, u32[]{:S(2)}, u32[]{:S(2)}) collective-permute-start(f32[8,128]{1,0:T(8,128)S(1)} %get-tuple-element.25.mine_ref), channel_id=1, source_target_pairs={{0,32},{16,48},{32,0},{48,16},{64,96},{80,112},{96,64},{112,80},{1... | collective-permute-start | bytes 12296 | tf_op jit(solution)/shard_map/ppermute | solution.py:401
  82.1 3.7 %shard_map.71.mine_ref = f32[256,128]{1,0:T(8,128)S(1)} custom-call(bf16[2,3,128,128]{3,2,1,0:T(8,128)(2,1)S(1)} %get-tuple-element.28.pair_ref, f32[256,128]{1,0:T(8,128)S(1)} %shard_map.70.mine_ref, f32[256,128]{1,0:T(8,128)S(1)} %collective-permute-done.9.other_ref), custom_call_target="tpu_custom_call" | custom-call | flops 1000000000 | bytes 1048576 | tf_op jit(solution)/shard_map/pallas_call | solution.py:375
  86.2 2.9 %collective-permute-start.4 = (f32[8,128]{1,0:T(8,128)S(1)}, f32[8,128]{1,0:T(8,128)S(1)}, u32[]{:S(2)}, u32[]{:S(2)}) collective-permute-start(f32[8,128]{1,0:T(8,128)S(1)} %get-tuple-element.26.mine_ref), channel_id=1, source_target_pairs={{0,64},{16,80},{32,96},{48,112},{64,0},{80,16},{96,32},{112,48},{1... | collective-permute-start | bytes 12296 | tf_op jit(solution)/shard_map/ppermute | solution.py:401
  89.1 1.0 shard_map.73
  90.1 3.5 %all-to-all-start.1 = ((f32[16,8,512]{2,1,0:T(8,128)}), f32[16,8,512]{2,1,0:T(8,128)S(1)}, u32[]{:S(2)}, u32[]{:S(2)}) async-start(f32[16,8,512]{2,1,0:T(8,128)} %shard_map.73), calls=%async_computation.1 | async-start | bytes 524288 | tf_op jit(solution)/shard_map/all_to_all | solution.py:487
  93.6 3.7 %shard_map.72 = (f32[256,128]{1,0:T(8,128)S(1)}, f32[128,128]{1,0:T(8,128)S(1)}) custom-call(s32[1]{0:T(128)} %bitcast.2.turned_ref, bf16[2,3,128,128]{3,2,1,0:T(8,128)(2,1)S(1)} %get-tuple-element.27.pair_ref, f32[256,128]{1,0:T(8,128)S(1)} %shard_map.71.mine_ref, f32[256,128]{1,0:T(8,128)S(1)} %collective-permute-done.10.other_ref), custom_call_target="tpu_custom_call" | custom-call | flops 1000000000 | bytes 1048576 | tf_op jit(solution)/shard_map/pallas_call | solution.py:375
  97.5 4.9 %collective-permute-done.11.direct_ref = f32[128,128]{1,0:T(8,128)S(1)} collective-permute-done((f32[128,128]{1,0:T(8,128)S(1)}, f32[128,128]{1,0:T(8,128)S(1)}, u32[]{:S(2)}, u32[]{:S(2)}) %collective-permute-start.11) | collective-permute-done | bytes 65568 | tf_op jit(solution)/shard_map/ppermute | solution.py:401
  102.4 1.9 %collective-permute-start.12 = (f32[128,128]{1,0:T(8,128)S(1)}, f32[128,128]{1,0:T(8,128)S(1)}, u32[]{:S(2)}, u32[]{:S(2)}) collective-permute-start(f32[128,128]{1,0:T(8,128)S(1)} %collective-permute-done.11.direct_ref), channel_id=1, source_target_pairs={{0,16},{16,0},{32,48},{48,32},{64,80},{80,64},{96,112},{112,96},{1... | collective-permute-start | bytes 196616 | tf_op jit(solution)/shard_map/ppermute | solution.py:401
  105.2 5.1 %shard_map.74 = (f32[8,256]{1,0:T(8,128)}, f32[8,8192]{1,0:T(8,128)}) custom-call(s32[3]{0:T(128)S(1)} %pad_add_fusion.place_ref, bf16[2,3,128,128]{3,2,1,0:T(8,128)(2,1)S(1)} %shard_map.63.pair_ref, f32[256,128]{1,0:T(8,128)S(1)} %get-tuple-element.36.mine_ref, f32[128,128]{1,0:T(8,128)S(1)} %collective-permute-done.11.direct_ref, ...), custom_call_target="tpu_custom_call" | custom-call | flops 1000000000 | bytes 1048576 | tf_op jit(solution)/shard_map/pallas_call | solution.py:375
  (31 shorter events, 3.5 us)
Async XLA Ops:
  2.1 6.7 %collective-permute-start = (f32[16,512]{1,0:T(8,128)}, f32[16,512]{1,0:T(8,128)S(1)}, u32[]{:S(2)}, u32[]{:S(2)}) collective-permute-start(f32[16,512]{1,0:T(8,128)} %get-tuple-element.22), channel_id=1, source_target_pairs={{0,16},{16,32},{32,48},{48,64},{64,80},{80,96},{96,112},{112,128},... | collective-permute-start | bytes 98312 | tf_op jit(solution)/shard_map/ppermute | solution.py:427
  5.1 3.7 %collective-permute-start.1 = (f32[16,512]{1,0:T(8,128)}, f32[16,512]{1,0:T(8,128)S(1)}, u32[]{:S(2)}, u32[]{:S(2)}) collective-permute-start(f32[16,512]{1,0:T(8,128)} %get-tuple-element.23), channel_id=1, source_target_pairs={{0,240},{16,0},{32,16},{48,32},{64,48},{80,64},{96,80},{112,96},{1... | collective-permute-start | bytes 98312 | tf_op jit(solution)/shard_map/ppermute | solution.py:428
  5.3 0.9 copy-start.2
  6.3 0.9 copy-start.5
  9.4 6.8 %copy-start.3 = (f32[2,8192]{1,0:T(2,128)S(1)}, f32[2,8192]{1,0:T(2,128)}, u32[]{:S(2)}) copy-start(f32[2,8192]{1,0:T(2,128)} %coords_ref.1) | copy-start | bytes 196612
  9.4 6.8 %copy-start.4 = (f32[8192]{0:T(1024)S(1)}, f32[8192]{0:T(1024)}, u32[]{:S(2)}) copy-start(f32[8192]{0:T(1024)} %param.5) | copy-start | bytes 98308
  9.5 20.2 %all-to-all-start = ((f32[16,4,8,512]{3,2,1,0:T(8,128)}), f32[16,4,8,512]{3,2,1,0:T(8,128)S(1)}, u32[]{:S(2)}, u32[]{:S(2)}) async-start(f32[16,4,8,512]{3,2,1,0:T(8,128)} %shard_map.65), calls=%async_computation | async-start | bytes 2097152 | tf_op jit(solution)/shard_map/all_to_all | solution.py:452
  21.2 1.2 %copy-start = (bf16[1536,512]{1,0:T(8,128)(2,1)}, bf16[1536,512]{1,0:T(8,128)(2,1)S(1)}, u32[]{:S(2)}) copy-start(bf16[1536,512]{1,0:T(8,128)(2,1)S(1)} %get-tuple-element.34.near_mid_hbm) | copy-start | bytes 4718596
  22.4 0.7 copy-start.6
  29.7 1.4 %copy-start.1 = (bf16[1536,512]{1,0:T(8,128)(2,1)S(1)}, bf16[1536,512]{1,0:T(8,128)(2,1)}, u32[]{:S(2)}) copy-start(bf16[1536,512]{1,0:T(8,128)(2,1)} %copy-done) | copy-start | bytes 4718596
  31.1 8.6 %copy-start.7 = (bf16[2,3,128,128]{3,2,1,0:T(8,128)(2,1)S(1)}, bf16[2,3,128,128]{3,2,1,0:T(8,128)(2,1)}, u32[]{:S(2)}) copy-start(bf16[2,3,128,128]{3,2,1,0:T(8,128)(2,1)} %copy-done.6) | copy-start | bytes 589828
  35.8 3.9 %collective-permute-start.5 = (f32[256,128]{1,0:T(8,128)S(1)}, f32[256,128]{1,0:T(8,128)S(1)}, u32[]{:S(2)}, u32[]{:S(2)}) collective-permute-start(f32[256,128]{1,0:T(8,128)S(1)} %get-tuple-element.35.mine_ref), channel_id=1, source_target_pairs={{0,1},{1,0},{2,3},{3,2},{4,5},{5,4},{6,7},{7,6},{8,9},{9,8},{10,11... | collective-permute-start | bytes 393224 | tf_op jit(solution)/shard_map/ppermute | solution.py:396
  43.4 5.3 %collective-permute-start.6 = (f32[256,128]{1,0:T(8,128)S(1)}, f32[256,128]{1,0:T(8,128)S(1)}, u32[]{:S(2)}, u32[]{:S(2)}) collective-permute-start(f32[256,128]{1,0:T(8,128)S(1)} %shard_map.67.mine_ref), channel_id=1, source_target_pairs={{0,3},{1,2},{2,1},{3,0},{4,7},{5,6},{6,5},{7,4},{8,11},{9,10},{10,... | collective-permute-start | bytes 393224 | tf_op jit(solution)/shard_map/ppermute | solution.py:396
  52.4 3.9 %collective-permute-start.7 = (f32[256,128]{1,0:T(8,128)S(1)}, f32[256,128]{1,0:T(8,128)S(1)}, u32[]{:S(2)}, u32[]{:S(2)}) collective-permute-start(f32[256,128]{1,0:T(8,128)S(1)} %shard_map.68.mine_ref), channel_id=1, source_target_pairs={{0,4},{1,5},{2,6},{3,7},{4,0},{5,1},{6,2},{7,3},{8,12},{9,13},{10,... | collective-permute-start | bytes 393224 | tf_op jit(solution)/shard_map/ppermute | solution.py:396
  60.0 5.1 %collective-permute-start.8 = (f32[256,128]{1,0:T(8,128)S(1)}, f32[256,128]{1,0:T(8,128)S(1)}, u32[]{:S(2)}, u32[]{:S(2)}) collective-permute-start(f32[256,128]{1,0:T(8,128)S(1)} %shard_map.69.mine_ref), channel_id=1, source_target_pairs={{0,12},{1,13},{2,14},{3,15},{4,8},{5,9},{6,10},{7,11},{8,4},{9,5},... | collective-permute-start | bytes 393224 | tf_op jit(solution)/shard_map/ppermute | solution.py:396
  68.9 13.2 %collective-permute-start.9 = (f32[256,128]{1,0:T(8,128)S(1)}, f32[256,128]{1,0:T(8,128)S(1)}, u32[]{:S(2)}, u32[]{:S(2)}) collective-permute-start(f32[256,128]{1,0:T(8,128)S(1)} %shard_map.70.mine_ref), channel_id=1, source_target_pairs={{0,16},{16,0},{32,48},{48,32},{64,80},{80,64},{96,112},{112,96},{1... | collective-permute-start | bytes 393224 | tf_op jit(solution)/shard_map/ppermute | solution.py:401
  78.6 1.2 %collective-permute-start.2 = (f32[8,128]{1,0:T(8,128)S(1)}, f32[8,128]{1,0:T(8,128)S(1)}, u32[]{:S(2)}, u32[]{:S(2)}) collective-permute-start(f32[8,128]{1,0:T(8,128)S(1)} %get-tuple-element.24.mine_ref), channel_id=1, source_target_pairs={{0,16},{16,0},{32,48},{48,32},{64,80},{80,64},{96,112},{112,96},{1... | collective-permute-start | bytes 12296 | tf_op jit(solution)/shard_map/ppermute | solution.py:401
  80.0 5.9 %collective-permute-start.3 = (f32[8,128]{1,0:T(8,128)S(1)}, f32[8,128]{1,0:T(8,128)S(1)}, u32[]{:S(2)}, u32[]{:S(2)}) collective-permute-start(f32[8,128]{1,0:T(8,128)S(1)} %get-tuple-element.25.mine_ref), channel_id=1, source_target_pairs={{0,32},{16,48},{32,0},{48,16},{64,96},{80,112},{96,64},{112,80},{1... | collective-permute-start | bytes 12296 | tf_op jit(solution)/shard_map/ppermute | solution.py:401
  85.8 7.8 %collective-permute-start.10 = (f32[256,128]{1,0:T(8,128)S(1)}, f32[256,128]{1,0:T(8,128)S(1)}, u32[]{:S(2)}, u32[]{:S(2)}) collective-permute-start(f32[256,128]{1,0:T(8,128)S(1)} %shard_map.71.mine_ref), channel_id=1, source_target_pairs={{0,32},{16,48},{32,0},{48,16},{64,96},{80,112},{96,64},{112,80},{1... | collective-permute-start | bytes 393224 | tf_op jit(solution)/shard_map/ppermute | solution.py:401
  86.2 18.1 %collective-permute-start.4 = (f32[8,128]{1,0:T(8,128)S(1)}, f32[8,128]{1,0:T(8,128)S(1)}, u32[]{:S(2)}, u32[]{:S(2)}) collective-permute-start(f32[8,128]{1,0:T(8,128)S(1)} %get-tuple-element.26.mine_ref), channel_id=1, source_target_pairs={{0,64},{16,80},{32,96},{48,112},{64,0},{80,16},{96,32},{112,48},{1... | collective-permute-start | bytes 12296 | tf_op jit(solution)/shard_map/ppermute | solution.py:401
  90.1 14.5 %all-to-all-start.1 = ((f32[16,8,512]{2,1,0:T(8,128)}), f32[16,8,512]{2,1,0:T(8,128)S(1)}, u32[]{:S(2)}, u32[]{:S(2)}) async-start(f32[16,8,512]{2,1,0:T(8,128)} %shard_map.73), calls=%async_computation.1 | async-start | bytes 524288 | tf_op jit(solution)/shard_map/all_to_all | solution.py:487
  97.3 5.1 %collective-permute-start.11 = (f32[128,128]{1,0:T(8,128)S(1)}, f32[128,128]{1,0:T(8,128)S(1)}, u32[]{:S(2)}, u32[]{:S(2)}) collective-permute-start(f32[128,128]{1,0:T(8,128)S(1)} %get-tuple-element.37), channel_id=1, source_target_pairs={{0,64},{16,80},{32,96},{48,112},{64,0},{80,16},{96,32},{112,48},{1... | collective-permute-start | bytes 196616 | tf_op jit(solution)/shard_map/ppermute | solution.py:401
  102.4 2.8 %collective-permute-start.12 = (f32[128,128]{1,0:T(8,128)S(1)}, f32[128,128]{1,0:T(8,128)S(1)}, u32[]{:S(2)}, u32[]{:S(2)}) collective-permute-start(f32[128,128]{1,0:T(8,128)S(1)} %collective-permute-done.11.direct_ref), channel_id=1, source_target_pairs={{0,16},{16,0},{32,48},{48,32},{64,80},{80,64},{96,112},{112,96},{1... | collective-permute-start | bytes 196616 | tf_op jit(solution)/shard_map/ppermute | solution.py:401

commit v3 on v2

--- a/solution.py
+++ b/solution.py
@@ -258,7 +258,7 @@
 
 
 def leaf_kernel(
-    data_ref, near_high_ref, near_mid_hbm, z_ref, inverse_ref, hat_ref, near_mid_ref, sem
+    data_ref, near_high_ref, near_mid_hbm, _, z_ref, inverse_ref, hat_ref, near_mid_ref, sem
 ):
     fetch = pltpu.make_async_copy(near_mid_hbm, near_mid_ref, sem)
     fetch.start()
@@ -325,7 +325,8 @@
         ref[...] = pick(joined, 2) * jnp.where(double, 2.0, 1.0)
 
 
-def parent_kernel(pair_ref, mine_ref, other_ref, hat_ref):
+def parent_kernel(pair_ref, mine_ref, other_ref, *rest):
+    hat_ref = rest[-1]
     pair = [[pair_ref[side, part] for part in range(3)] for side in range(2)]
     got = merge(*pair, mine_ref, other_ref)
     hat_ref[:S] = got[:, :S]
@@ -374,7 +375,10 @@
 def call(kernel, outs, specs, *operands, out_specs=None, scratch=(), aliases={}, flops=10**9):
     return pl.pallas_call(
         kernel,
-        out_shape=[jax.ShapeDtypeStruct(shape, kind) for shape, kind in outs],
+        out_shape=[
+            (pltpu.HBM if spec is HBM else jax.ShapeDtypeStruct)(shape, kind)
+            for (shape, kind), spec in zip(outs, out_specs or [VMEM] * len(outs))
+        ],
         in_specs=specs,
         out_specs=out_specs or [VMEM] * len(outs),
         scratch_shapes=list(scratch),
@@ -384,6 +388,10 @@
             flops=flops, bytes_accessed=2**20, transcendentals=0
         ),
     )(*operands)
+
+
+def in_hbm(block):
+    return pltpu.with_memory_space_constraint(block, pltpu.HBM)
 
 
 def swap(block, even, odd):
@@ -432,8 +440,8 @@
         [((cells, 4, columns, LEAF), F32)],
         [SMEM, HBM, HBM],
         turned.reshape(1),
-        sketch_matrix,
-        random_test_matrix,
+        in_hbm(sketch_matrix),
+        in_hbm(random_test_matrix),
         out_specs=[HBM],
         scratch=[pltpu.SemaphoreType.DMA((4 * cells - 2,))],
     )
@@ -472,20 +480,6 @@
         out_specs=[VMEM, HBM] + [VMEM] * (cell_levels + 1),
         flops=10**10,
     )
-    z, inverse, hat = call(
-        leaf_kernel,
-        [((S, LEAF), F32), ((S, S), F32), ((2 * S, S), F32)],
-        [VMEM, VMEM, HBM],
-        data,
-        near_high,
-        near_mid,
-        scratch=[pltpu.VMEM((3 * LEAF, LEAF), BF16), pltpu.SemaphoreType.DMA],
-    )
-    (basis,) = call(
-        basis_kernel, [((cells, columns, LEAF), F32)], [VMEM] * 2, inverse, z
-    )
-    parts = lax.all_to_all(basis, "rep", 0, 0)
-
     skeleton = far
     for level in range(3):
         pair, *joined = call(
@@ -499,9 +493,31 @@
         pairs.append(pair)
         skeleton = joined[0] if joined else None
 
-    for pair, masks in zip(pairs, ((1, 4), (3, 12), (4, 1), (12, 3))):
+    z, inverse, hat = call(
+        leaf_kernel,
+        [((S, LEAF), F32), ((S, S), F32), ((2 * S, S), F32)],
+        [VMEM, VMEM, HBM, ANY],
+        data,
+        near_high,
+        in_hbm(near_mid),
+        pairs[-2],
+        scratch=[pltpu.VMEM((3 * LEAF, LEAF), BF16), pltpu.SemaphoreType.DMA],
+    )
+    (basis,) = call(
+        basis_kernel, [((cells, columns, LEAF), F32)], [VMEM] * 2, inverse, z
+    )
+    parts = lax.all_to_all(basis, "rep", 0, 0)
+
+    for level, masks in enumerate(((1, 4), (3, 12), (4, 1), (12, 3))):
+        pair = pairs[level]
         (hat,) = call(
-            parent_kernel, [((2 * S, S), F32)], [VMEM] * 3, pair, hat, swap(hat, *masks)
+            parent_kernel,
+            [((2 * S, S), F32)],
+            [VMEM] * 3 + [ANY] * (level == 1),
+            pair,
+            hat,
+            swap(hat, *masks),
+            *pairs[-1:] * (level == 1),
         )
     (hat,) = call(
         parent_kernel, [((2 * S, S), F32)], [VMEM] * 3, pairs[-3], hat, cross(hat, 1)

time: 111 us -> 139 us (1.25)
  Pallas kernels: 42.3 us -> 74.7 us
  waiting for transfers between devices: 28.4 us -> 17.3 us
  starting transfers between devices: 33.5 us -> 43.2 us
  local copies, waits for them, and re-layouts: 5.19 us -> 2.05 us
    pallas_call x15, Pallas kernels: 40.9 us -> 73.3 us  [call(): pl.pallas_call(kernel, out_shape=[(pltpu.HBM if spec is HBM else jax.Shap...]
    ppermute x4, waiting for transfers between devices: 15.2 us -> 7.92 us  [swap(): return lax.ppermute(block, ('leaf', 'rep'), route)]
    all_to_all x1, waiting for transfers between devices: 6.61 us -> 0.01 us  [body(): data = lax.all_to_all(parcels, 'rep', 0, 0)]
    ppermute x4, starting transfers between devices: 3.04 us -> 7.96 us  [swap(): return lax.ppermute(block, ('leaf', 'rep'), route)]
    ppermute x7, starting transfers between devices: 16.9 us -> 20.5 us  [cross(): return lax.ppermute(block, 'leaf', [(i, i ^ mask) for i in range(count)])]
    unnamed x16, local copies, waits for them, and re-layouts: 5.19 us -> 2.05 us
    ppermute x7, waiting for transfers between devices: 6.65 us -> 9.38 us  [cross(): return lax.ppermute(block, 'leaf', [(i, i ^ mask) for i in range(count)])]
  transfers between devices with their start and end apart: 15 -> 15, of which waited for: 8 -> 9; matrix products, arithmetic and copies ran while one was open for 0% -> 0% of each run, Pallas kernels for 14% -> 31%
where the time goes in v3:
time: 139 us; the launch traced here: 138 us
  Pallas kernels  74.7 us (54%)
  starting transfers between devices  43.2 us (31%)
  waiting for transfers between devices  17.3 us (12%)
  local copies, waits for them, and re-layouts  2.05 us (1%)
    pallas_call x15, Pallas kernels, call(): pl.pallas_call(kernel, out_shape=[(pltpu.HBM if spec is HBM else jax.Shap...  73.3 us
    ppermute x7, starting transfers between devices, cross(): return lax.ppermute(block, 'leaf', [(i, i ^ mask) for i in range(count)])  20.5 us
    ppermute x7, waiting for transfers between devices, cross(): return lax.ppermute(block, 'leaf', [(i, i ^ mask) for i in range(count)])  9.38 us
    ppermute x4, starting transfers between devices, swap(): return lax.ppermute(block, ('leaf', 'rep'), route)  7.96 us
    ppermute x4, waiting for transfers between devices, swap(): return lax.ppermute(block, ('leaf', 'rep'), route)  7.92 us
    all_to_all x1, starting transfers between devices, body(): data = lax.all_to_all(parcels, 'rep', 0, 0)  6.69 us
    all_to_all x1, starting transfers between devices, body(): parts = lax.all_to_all(basis, 'rep', 0, 0)  4.86 us
    ppermute x1, starting transfers between devices, body(): lax.ppermute(low, 'leaf', [(i, (i + 1) % count) for i in range(count)])  3.03 us
  transfers between devices with their start and end apart: 15, of which 9 were waited for; matrix products, arithmetic and copies ran while one was open for 0% of the time, Pallas kernels for 31%

profile of v3, /device:TPU:1, one launch (start us, length us, event | category | flops | bytes accessed | tf_op | source)
XLA Modules:
  0.0 138.4 jit_solution(17268398465247629664)
XLA Ops:
  0.6 1.5 %shard_map.59 = (f32[16,512]{1,0:T(8,128)}, f32[16,512]{1,0:T(8,128)}) custom-call(f32[8,8192]{1,0:T(8,128)} %tests_ref.1, f32[8,8192]{1,0:T(8,128)} %tests_ref.1, f32[2,8192]{1,0:T(2,128)} %coords_ref.1, f32[2,8192]{1,0:T(2,128)} %coords_ref.1, f32[1,8192]{1,0:T(1,128)} %bitcast.8), custom_call_target="tpu_custom_call" | custom-call | tf_op jit(solution)/shard_map/pallas_call | solution.py:427
  2.1 3.0 %collective-permute-start = (f32[16,512]{1,0:T(8,128)}, f32[16,512]{1,0:T(8,128)S(1)}, u32[]{:S(2)}, u32[]{:S(2)}) collective-permute-start(f32[16,512]{1,0:T(8,128)} %get-tuple-element.22), channel_id=1, source_target_pairs={{0,16},{16,32},{32,48},{48,64},{64,80},{80,96},{96,112},{112,128},... | collective-permute-start | bytes 98312 | tf_op jit(solution)/shard_map/ppermute | solution.py:435
  5.3 32.4 %shard_map.64.packed_ref = f32[16,4,8,512]{3,2,1,0:T(8,128)} custom-call(s32[1]{0:T(128)} %bitcast.2.turned_ref, f32[8,8192]{1,0:T(8,128)} %samples_ref.1, f32[8,8192]{1,0:T(8,128)} %tests_ref.1), custom_call_target="tpu_custom_call" | custom-call | flops 1000000000 | bytes 1048576 | tf_op jit(solution)/shard_map/pallas_call | solution.py:376
  38.5 6.7 %all-to-all-start = ((f32[16,4,8,512]{3,2,1,0:T(8,128)}), f32[16,4,8,512]{3,2,1,0:T(8,128)S(1)}, u32[]{:S(2)}, u32[]{:S(2)}) async-start(f32[16,4,8,512]{3,2,1,0:T(8,128)} %shard_map.65), calls=%async_computation | async-start | bytes 2097152 | tf_op jit(solution)/shard_map/all_to_all | solution.py:460
  45.2 5.3 %shard_map.60 = (bf16[1536,512]{1,0:T(8,128)(2,1)S(1)}, bf16[1536,512]{1,0:T(8,128)(2,1)}, f32[8,128]{1,0:T(8,128)S(1)}, bf16[2,3,128,128]{3,2,1,0:T(8,128)(2,1)...) custom-call(s32[1]{0:T(128)} %bitcast.5.rep_ref, ...), custom_call_target="tpu_custom_call" | custom-call | flops 10000000000 | bytes 1048576 | tf_op jit(solution)/shard_map/pallas_call | solution.py:376
  51.8 4.1 %collective-permute-start.2 = (f32[8,128]{1,0:T(8,128)S(1)}, f32[8,128]{1,0:T(8,128)S(1)}, u32[]{:S(2)}, u32[]{:S(2)}) collective-permute-start(f32[8,128]{1,0:T(8,128)S(1)} %get-tuple-element.24.mine_ref), channel_id=1, source_target_pairs={{0,16},{16,0},{32,48},{48,32},{64,80},{80,64},{96,112},{112,96},{1... | collective-permute-start | bytes 12296 | tf_op jit(solution)/shard_map/ppermute | solution.py:409
  57.6 2.7 %collective-permute-done.3.other_ref = f32[8,128]{1,0:T(8,128)S(1)} collective-permute-done((f32[8,128]{1,0:T(8,128)S(1)}, f32[8,128]{1,0:T(8,128)S(1)}, u32[]{:S(2)}, u32[]{:S(2)}) %collective-permute-start.3) | collective-permute-done | bytes 4128 | tf_op jit(solution)/shard_map/ppermute | solution.py:409
  60.7 5.9 %shard_map.66 = (f32[128,512]{1,0:T(8,128)S(1)}, f32[128,128]{1,0:T(8,128)S(1)}, f32[256,128]{1,0:T(8,128)S(1)}) custom-call(f32[16,4,8,512]{3,2,1,0:T(8,128)S(1)} %all-to-all-done.data_ref, bf16[1536,512]{1,0:T(8,128)(2,1)S(1)} %get-tuple-element.33.near_high_ref, bf16[1536,512]{1,0:T(8,128)(2,1)} %get-tuple-element.34.near_mid_hbm, ...), custom_call_target="tpu_custom_call" | custom-call | flops 1000000000 | bytes 1048576 | tf_op jit(solution)/shard_map/pallas_call | solution.py:376
  66.6 1.7 %collective-permute-start.5 = (f32[256,128]{1,0:T(8,128)S(1)}, f32[256,128]{1,0:T(8,128)S(1)}, u32[]{:S(2)}, u32[]{:S(2)}) collective-permute-start(f32[256,128]{1,0:T(8,128)S(1)} %get-tuple-element.35.mine_ref), channel_id=1, source_target_pairs={{0,1},{1,0},{2,3},{3,2},{4,5},{5,4},{6,7},{7,6},{8,9},{9,8},{10,11... | collective-permute-start | bytes 393224 | tf_op jit(solution)/shard_map/ppermute | solution.py:404
  68.3 2.4 %collective-permute-done.5.other_ref = f32[256,128]{1,0:T(8,128)S(1)} collective-permute-done((f32[256,128]{1,0:T(8,128)S(1)}, f32[256,128]{1,0:T(8,128)S(1)}, u32[]{:S(2)}, u32[]{:S(2)}) %collective-permute-start.5) | collective-permute-done | bytes 131104 | tf_op jit(solution)/shard_map/ppermute | solution.py:404
  70.7 3.7 %shard_map.67.mine_ref = f32[256,128]{1,0:T(8,128)S(1)} custom-call(bf16[2,3,128,128]{3,2,1,0:T(8,128)(2,1)S(1)} %copy-done.7, f32[256,128]{1,0:T(8,128)S(1)} %get-tuple-element.35.mine_ref, f32[256,128]{1,0:T(8,128)S(1)} %collective-permute-done.5.other_ref), custom_call_target="tpu_custom_call" | custom-call | flops 1000000000 | bytes 1048576 | tf_op jit(solution)/shard_map/pallas_call | solution.py:376
  74.4 2.8 %collective-permute-start.6 = (f32[256,128]{1,0:T(8,128)S(1)}, f32[256,128]{1,0:T(8,128)S(1)}, u32[]{:S(2)}, u32[]{:S(2)}) collective-permute-start(f32[256,128]{1,0:T(8,128)S(1)} %shard_map.67.mine_ref), channel_id=1, source_target_pairs={{0,3},{1,2},{2,1},{3,0},{4,7},{5,6},{6,5},{7,4},{8,11},{9,10},{10,... | collective-permute-start | bytes 393224 | tf_op jit(solution)/shard_map/ppermute | solution.py:404
  77.1 1.8 %collective-permute-start.4 = (f32[8,128]{1,0:T(8,128)S(1)}, f32[8,128]{1,0:T(8,128)S(1)}, u32[]{:S(2)}, u32[]{:S(2)}) collective-permute-start(f32[8,128]{1,0:T(8,128)S(1)} %get-tuple-element.26.mine_ref), channel_id=1, source_target_pairs={{0,64},{16,80},{32,96},{48,112},{64,0},{80,16},{96,32},{112,48},{1... | collective-permute-start | bytes 12296 | tf_op jit(solution)/shard_map/ppermute | solution.py:409
  78.9 1.6 %collective-permute-done.4.other_ref = f32[8,128]{1,0:T(8,128)S(1)} collective-permute-done((f32[8,128]{1,0:T(8,128)S(1)}, f32[8,128]{1,0:T(8,128)S(1)}, u32[]{:S(2)}, u32[]{:S(2)}) %collective-permute-start.4) | collective-permute-done | bytes 4128 | tf_op jit(solution)/shard_map/ppermute | solution.py:409
  80.7 3.7 %shard_map.68.mine_ref = f32[256,128]{1,0:T(8,128)S(1)} custom-call(bf16[2,3,128,128]{3,2,1,0:T(8,128)(2,1)S(1)} %get-tuple-element.31.pair_ref, f32[256,128]{1,0:T(8,128)S(1)} %shard_map.67.mine_ref, f32[256,128]{1,0:T(8,128)S(1)} %collective-permute-done.6.other_ref, bf16[2,3,128,128]{3,2,1,0:T(8,128)(2,1)S(1)} %shard_map.63.rest_0_.pair_ref), custom_call_target="tpu_custom_call" | custom-call | flops 1000000000 | bytes 1048576 | tf_op jit(solution)/shard_map/pallas_call | solution.py:376
  84.4 1.3 collective-permute-start.7
  85.7 2.6 %collective-permute-done.7.other_ref = f32[256,128]{1,0:T(8,128)S(1)} collective-permute-done((f32[256,128]{1,0:T(8,128)S(1)}, f32[256,128]{1,0:T(8,128)S(1)}, u32[]{:S(2)}, u32[]{:S(2)}) %collective-permute-start.7) | collective-permute-done | bytes 131104 | tf_op jit(solution)/shard_map/ppermute | solution.py:404
  88.4 3.7 %shard_map.69.mine_ref = f32[256,128]{1,0:T(8,128)S(1)} custom-call(bf16[2,3,128,128]{3,2,1,0:T(8,128)(2,1)S(1)} %copy-done.5, f32[256,128]{1,0:T(8,128)S(1)} %shard_map.68.mine_ref, f32[256,128]{1,0:T(8,128)S(1)} %collective-permute-done.7.other_ref), custom_call_target="tpu_custom_call" | custom-call | flops 1000000000 | bytes 1048576 | tf_op jit(solution)/shard_map/pallas_call | solution.py:376
  92.1 2.2 %collective-permute-start.8 = (f32[256,128]{1,0:T(8,128)S(1)}, f32[256,128]{1,0:T(8,128)S(1)}, u32[]{:S(2)}, u32[]{:S(2)}) collective-permute-start(f32[256,128]{1,0:T(8,128)S(1)} %shard_map.69.mine_ref), channel_id=1, source_target_pairs={{0,12},{1,13},{2,14},{3,15},{4,8},{5,9},{6,10},{7,11},{8,4},{9,5},... | collective-permute-start | bytes 393224 | tf_op jit(solution)/shard_map/ppermute | solution.py:404
  94.3 2.9 %collective-permute-done.8.other_ref = f32[256,128]{1,0:T(8,128)S(1)} collective-permute-done((f32[256,128]{1,0:T(8,128)S(1)}, f32[256,128]{1,0:T(8,128)S(1)}, u32[]{:S(2)}, u32[]{:S(2)}) %collective-permute-start.8) | collective-permute-done | bytes 131104 | tf_op jit(solution)/shard_map/ppermute | solution.py:404
  97.2 3.7 %shard_map.70.mine_ref = f32[256,128]{1,0:T(8,128)S(1)} custom-call(bf16[2,3,128,128]{3,2,1,0:T(8,128)(2,1)S(1)} %get-tuple-element.29.pair_ref, f32[256,128]{1,0:T(8,128)S(1)} %shard_map.69.mine_ref, f32[256,128]{1,0:T(8,128)S(1)} %collective-permute-done.8.other_ref), custom_call_target="tpu_custom_call" | custom-call | flops 1000000000 | bytes 1048576 | tf_op jit(solution)/shard_map/pallas_call | solution.py:376
  100.9 6.6 %collective-permute-start.9 = (f32[256,128]{1,0:T(8,128)S(1)}, f32[256,128]{1,0:T(8,128)S(1)}, u32[]{:S(2)}, u32[]{:S(2)}) collective-permute-start(f32[256,128]{1,0:T(8,128)S(1)} %shard_map.70.mine_ref), channel_id=1, source_target_pairs={{0,16},{16,0},{32,48},{48,32},{64,80},{80,64},{96,112},{112,96},{1... | collective-permute-start | bytes 393224 | tf_op jit(solution)/shard_map/ppermute | solution.py:409
  107.4 1.0 collective-permute-done.9.other_ref
  108.4 3.7 %shard_map.71.mine_ref = f32[256,128]{1,0:T(8,128)S(1)} custom-call(bf16[2,3,128,128]{3,2,1,0:T(8,128)(2,1)S(1)} %copy-done.3, f32[256,128]{1,0:T(8,128)S(1)} %shard_map.70.mine_ref, f32[256,128]{1,0:T(8,128)S(1)} %collective-permute-done.9.other_ref), custom_call_target="tpu_custom_call" | custom-call | flops 1000000000 | bytes 1048576 | tf_op jit(solution)/shard_map/pallas_call | solution.py:376
  112.1 3.6 %collective-permute-start.10 = (f32[256,128]{1,0:T(8,128)S(1)}, f32[256,128]{1,0:T(8,128)S(1)}, u32[]{:S(2)}, u32[]{:S(2)}) collective-permute-start(f32[256,128]{1,0:T(8,128)S(1)} %shard_map.71.mine_ref), channel_id=1, source_target_pairs={{0,32},{16,48},{32,0},{48,16},{64,96},{80,112},{96,64},{112,80},{1... | collective-permute-start | bytes 393224 | tf_op jit(solution)/shard_map/ppermute | solution.py:409
  115.7 1.0 shard_map.73
  116.7 4.9 %all-to-all-start.1 = ((f32[16,8,512]{2,1,0:T(8,128)}), f32[16,8,512]{2,1,0:T(8,128)S(1)}, u32[]{:S(2)}, u32[]{:S(2)}) async-start(f32[16,8,512]{2,1,0:T(8,128)} %shard_map.73), calls=%async_computation.1 | async-start | bytes 524288 | tf_op jit(solution)/shard_map/all_to_all | solution.py:509
  121.6 3.7 %shard_map.72 = (f32[256,128]{1,0:T(8,128)S(1)}, f32[128,128]{1,0:T(8,128)S(1)}) custom-call(s32[1]{0:T(128)} %bitcast.2.turned_ref, bf16[2,3,128,128]{3,2,1,0:T(8,128)(2,1)S(1)} %get-tuple-element.27._.pair_ref, f32[256,128]{1,0:T(8,128)S(1)} %shard_map.71.mine_ref, f32[256,128]{1,0:T(8,128)S(1)} %collective-permute-done.10.other_ref), custom_call_target="tpu_custom_call" | custom-call | flops 1000000000 | bytes 1048576 | tf_op jit(solution)/shard_map/pallas_call | solution.py:376
  125.3 2.7 %collective-permute-start.11 = (f32[128,128]{1,0:T(8,128)S(1)}, f32[128,128]{1,0:T(8,128)S(1)}, u32[]{:S(2)}, u32[]{:S(2)}) collective-permute-start(f32[128,128]{1,0:T(8,128)S(1)} %get-tuple-element.37), channel_id=1, source_target_pairs={{0,64},{16,80},{32,96},{48,112},{64,0},{80,16},{96,32},{112,48},{1... | collective-permute-start | bytes 196616 | tf_op jit(solution)/shard_map/ppermute | solution.py:409
  128.0 2.4 %collective-permute-done.11.direct_ref = f32[128,128]{1,0:T(8,128)S(1)} collective-permute-done((f32[128,128]{1,0:T(8,128)S(1)}, f32[128,128]{1,0:T(8,128)S(1)}, u32[]{:S(2)}, u32[]{:S(2)}) %collective-permute-start.11) | collective-permute-done | bytes 65568 | tf_op jit(solution)/shard_map/ppermute | solution.py:409
  130.4 1.8 %collective-permute-start.12 = (f32[128,128]{1,0:T(8,128)S(1)}, f32[128,128]{1,0:T(8,128)S(1)}, u32[]{:S(2)}, u32[]{:S(2)}) collective-permute-start(f32[128,128]{1,0:T(8,128)S(1)} %collective-permute-done.11.direct_ref), channel_id=1, source_target_pairs={{0,16},{16,0},{32,48},{48,32},{64,80},{80,64},{96,112},{112,96},{1... | collective-permute-start | bytes 196616 | tf_op jit(solution)/shard_map/ppermute | solution.py:409
  133.1 5.1 %shard_map.74 = (f32[8,256]{1,0:T(8,128)}, f32[8,8192]{1,0:T(8,128)}) custom-call(s32[3]{0:T(128)S(1)} %pad_add_fusion.place_ref, bf16[2,3,128,128]{3,2,1,0:T(8,128)(2,1)S(1)} %shard_map.63.rest_0_.pair_ref, f32[256,128]{1,0:T(8,128)S(1)} %get-tuple-element.36.mine_ref, f32[128,128]{1,0:T(8,128)S(1)} %collective-permute-done.11.direct_ref, ...), custom_call_target="tpu_custom_call" | custom-call | flops 1000000000 | bytes 1048576 | tf_op jit(solution)/shard_map/pallas_call | solution.py:376
  (31 shorter events, 5.4 us)
Async XLA Ops:
  2.1 35.7 %collective-permute-start = (f32[16,512]{1,0:T(8,128)}, f32[16,512]{1,0:T(8,128)S(1)}, u32[]{:S(2)}, u32[]{:S(2)}) collective-permute-start(f32[16,512]{1,0:T(8,128)} %get-tuple-element.22), channel_id=1, source_target_pairs={{0,16},{16,32},{32,48},{48,64},{64,80},{80,96},{96,112},{112,128},... | collective-permute-start | bytes 98312 | tf_op jit(solution)/shard_map/ppermute | solution.py:435
  5.1 32.7 %collective-permute-start.1 = (f32[16,512]{1,0:T(8,128)}, f32[16,512]{1,0:T(8,128)S(1)}, u32[]{:S(2)}, u32[]{:S(2)}) collective-permute-start(f32[16,512]{1,0:T(8,128)} %get-tuple-element.23), channel_id=1, source_target_pairs={{0,240},{16,0},{32,16},{48,32},{64,48},{80,64},{96,80},{112,96},{1... | collective-permute-start | bytes 98312 | tf_op jit(solution)/shard_map/ppermute | solution.py:436
  38.5 6.7 %copy-start = (f32[2,8192]{1,0:T(2,128)S(1)}, f32[2,8192]{1,0:T(2,128)}, u32[]{:S(2)}) copy-start(f32[2,8192]{1,0:T(2,128)} %coords_ref.1) | copy-start | bytes 196612
  38.5 6.7 %copy-start.1 = (f32[8192]{0:T(1024)S(1)}, f32[8192]{0:T(1024)}, u32[]{:S(2)}) copy-start(f32[8192]{0:T(1024)} %param.5) | copy-start | bytes 98308
  38.5 22.2 %all-to-all-start = ((f32[16,4,8,512]{3,2,1,0:T(8,128)}), f32[16,4,8,512]{3,2,1,0:T(8,128)S(1)}, u32[]{:S(2)}, u32[]{:S(2)}) async-start(f32[16,4,8,512]{3,2,1,0:T(8,128)} %shard_map.65), calls=%async_computation | async-start | bytes 2097152 | tf_op jit(solution)/shard_map/all_to_all | solution.py:460
  50.5 0.7 copy-start.4
  51.1 0.7 copy-start.6
  51.8 4.9 %collective-permute-start.2 = (f32[8,128]{1,0:T(8,128)S(1)}, f32[8,128]{1,0:T(8,128)S(1)}, u32[]{:S(2)}, u32[]{:S(2)}) collective-permute-start(f32[8,128]{1,0:T(8,128)S(1)} %get-tuple-element.24.mine_ref), channel_id=1, source_target_pairs={{0,16},{16,0},{32,48},{48,32},{64,80},{80,64},{96,112},{112,96},{1... | collective-permute-start | bytes 12296 | tf_op jit(solution)/shard_map/ppermute | solution.py:409
  57.0 0.7 copy-start.2
  57.6 2.8 %collective-permute-start.3 = (f32[8,128]{1,0:T(8,128)S(1)}, f32[8,128]{1,0:T(8,128)S(1)}, u32[]{:S(2)}, u32[]{:S(2)}) collective-permute-start(f32[8,128]{1,0:T(8,128)S(1)} %get-tuple-element.25.mine_ref), channel_id=1, source_target_pairs={{0,32},{16,48},{32,0},{48,16},{64,96},{80,112},{96,64},{112,80},{1... | collective-permute-start | bytes 12296 | tf_op jit(solution)/shard_map/ppermute | solution.py:409
  60.7 10.0 %copy-start.7 = (bf16[2,3,128,128]{3,2,1,0:T(8,128)(2,1)S(1)}, bf16[2,3,128,128]{3,2,1,0:T(8,128)(2,1)}, u32[]{:S(2)}) copy-start(bf16[2,3,128,128]{3,2,1,0:T(8,128)(2,1)} %copy-done.6) | copy-start | bytes 589828
  66.6 4.1 %collective-permute-start.5 = (f32[256,128]{1,0:T(8,128)S(1)}, f32[256,128]{1,0:T(8,128)S(1)}, u32[]{:S(2)}, u32[]{:S(2)}) collective-permute-start(f32[256,128]{1,0:T(8,128)S(1)} %get-tuple-element.35.mine_ref), channel_id=1, source_target_pairs={{0,1},{1,0},{2,3},{3,2},{4,5},{5,4},{6,7},{7,6},{8,9},{9,8},{10,11... | collective-permute-start | bytes 393224 | tf_op jit(solution)/shard_map/ppermute | solution.py:404
  74.4 6.4 %collective-permute-start.6 = (f32[256,128]{1,0:T(8,128)S(1)}, f32[256,128]{1,0:T(8,128)S(1)}, u32[]{:S(2)}, u32[]{:S(2)}) collective-permute-start(f32[256,128]{1,0:T(8,128)S(1)} %shard_map.67.mine_ref), channel_id=1, source_target_pairs={{0,3},{1,2},{2,1},{3,0},{4,7},{5,6},{6,5},{7,4},{8,11},{9,10},{10,... | collective-permute-start | bytes 393224 | tf_op jit(solution)/shard_map/ppermute | solution.py:404
  77.1 3.4 %collective-permute-start.4 = (f32[8,128]{1,0:T(8,128)S(1)}, f32[8,128]{1,0:T(8,128)S(1)}, u32[]{:S(2)}, u32[]{:S(2)}) collective-permute-start(f32[8,128]{1,0:T(8,128)S(1)} %get-tuple-element.26.mine_ref), channel_id=1, source_target_pairs={{0,64},{16,80},{32,96},{48,112},{64,0},{80,16},{96,32},{112,48},{1... | collective-permute-start | bytes 12296 | tf_op jit(solution)/shard_map/ppermute | solution.py:409
  80.7 7.6 %copy-start.5 = (bf16[2,3,128,128]{3,2,1,0:T(8,128)(2,1)S(1)}, bf16[2,3,128,128]{3,2,1,0:T(8,128)(2,1)}, u32[]{:S(2)}) copy-start(bf16[2,3,128,128]{3,2,1,0:T(8,128)(2,1)} %copy-done.4) | copy-start | bytes 589828
  84.4 3.9 %collective-permute-start.7 = (f32[256,128]{1,0:T(8,128)S(1)}, f32[256,128]{1,0:T(8,128)S(1)}, u32[]{:S(2)}, u32[]{:S(2)}) collective-permute-start(f32[256,128]{1,0:T(8,128)S(1)} %shard_map.68.mine_ref), channel_id=1, source_target_pairs={{0,4},{1,5},{2,6},{3,7},{4,0},{5,1},{6,2},{7,3},{8,12},{9,13},{10,... | collective-permute-start | bytes 393224 | tf_op jit(solution)/shard_map/ppermute | solution.py:404
  92.1 5.1 %collective-permute-start.8 = (f32[256,128]{1,0:T(8,128)S(1)}, f32[256,128]{1,0:T(8,128)S(1)}, u32[]{:S(2)}, u32[]{:S(2)}) collective-permute-start(f32[256,128]{1,0:T(8,128)S(1)} %shard_map.69.mine_ref), channel_id=1, source_target_pairs={{0,12},{1,13},{2,14},{3,15},{4,8},{5,9},{6,10},{7,11},{8,4},{9,5},... | collective-permute-start | bytes 393224 | tf_op jit(solution)/shard_map/ppermute | solution.py:404
  97.2 11.3 %copy-start.3 = (bf16[2,3,128,128]{3,2,1,0:T(8,128)(2,1)S(1)}, bf16[2,3,128,128]{3,2,1,0:T(8,128)(2,1)}, u32[]{:S(2)}) copy-start(bf16[2,3,128,128]{3,2,1,0:T(8,128)(2,1)} %copy-done.2) | copy-start | bytes 589828
  100.9 7.5 %collective-permute-start.9 = (f32[256,128]{1,0:T(8,128)S(1)}, f32[256,128]{1,0:T(8,128)S(1)}, u32[]{:S(2)}, u32[]{:S(2)}) collective-permute-start(f32[256,128]{1,0:T(8,128)S(1)} %shard_map.70.mine_ref), channel_id=1, source_target_pairs={{0,16},{16,0},{32,48},{48,32},{64,80},{80,64},{96,112},{112,96},{1... | collective-permute-start | bytes 393224 | tf_op jit(solution)/shard_map/ppermute | solution.py:409
  112.1 9.4 %collective-permute-start.10 = (f32[256,128]{1,0:T(8,128)S(1)}, f32[256,128]{1,0:T(8,128)S(1)}, u32[]{:S(2)}, u32[]{:S(2)}) collective-permute-start(f32[256,128]{1,0:T(8,128)S(1)} %shard_map.71.mine_ref), channel_id=1, source_target_pairs={{0,32},{16,48},{32,0},{48,16},{64,96},{80,112},{96,64},{112,80},{1... | collective-permute-start | bytes 393224 | tf_op jit(solution)/shard_map/ppermute | solution.py:409
  116.7 15.6 %all-to-all-start.1 = ((f32[16,8,512]{2,1,0:T(8,128)}), f32[16,8,512]{2,1,0:T(8,128)S(1)}, u32[]{:S(2)}, u32[]{:S(2)}) async-start(f32[16,8,512]{2,1,0:T(8,128)} %shard_map.73), calls=%async_computation.1 | async-start | bytes 524288 | tf_op jit(solution)/shard_map/all_to_all | solution.py:509
  125.3 5.1 %collective-permute-start.11 = (f32[128,128]{1,0:T(8,128)S(1)}, f32[128,128]{1,0:T(8,128)S(1)}, u32[]{:S(2)}, u32[]{:S(2)}) collective-permute-start(f32[128,128]{1,0:T(8,128)S(1)} %get-tuple-element.37), channel_id=1, source_target_pairs={{0,64},{16,80},{32,96},{48,112},{64,0},{80,16},{96,32},{112,48},{1... | collective-permute-start | bytes 196616 | tf_op jit(solution)/shard_map/ppermute | solution.py:409
  130.4 2.7 %collective-permute-start.12 = (f32[128,128]{1,0:T(8,128)S(1)}, f32[128,128]{1,0:T(8,128)S(1)}, u32[]{:S(2)}, u32[]{:S(2)}) collective-permute-start(f32[128,128]{1,0:T(8,128)S(1)} %collective-permute-done.11.direct_ref), channel_id=1, source_target_pairs={{0,16},{16,0},{32,48},{48,32},{64,80},{80,64},{96,112},{112,96},{1... | collective-permute-start | bytes 196616 | tf_op jit(solution)/shard_map/ppermute | solution.py:409

commit v4 on v3

--- a/solution.py
+++ b/solution.py
@@ -219,8 +219,16 @@
     return jnp.where(turned == 1, index % 4 * 4 + index // 4, index)
 
 
-def pack_kernel(turned_ref, samples_ref, tests_ref, out_ref, sems):
+def pack_kernel(turned_ref, samples_hbm, tests_hbm, out_ref, samples_ref, tests_ref, ins, sems):
     cells = out_ref.shape[0]
+    loads = [
+        pltpu.make_async_copy(samples_hbm, samples_ref, ins.at[0]),
+        pltpu.make_async_copy(tests_hbm, tests_ref, ins.at[1]),
+    ]
+    for load in loads:
+        load.start()
+    for load in loads:
+        load.wait()
     copies = []
 
     def move(source, leaf, i, slot):
@@ -258,10 +266,15 @@
 
 
 def leaf_kernel(
-    data_ref, near_high_ref, near_mid_hbm, _, z_ref, inverse_ref, hat_ref, near_mid_ref, sem
+    data_ref, near_high_ref, near_mid_hbm, _, z_ref, inverse_ref, hat_ref, near_mid_ref, sems
 ):
-    fetch = pltpu.make_async_copy(near_mid_hbm, near_mid_ref, sem)
-    fetch.start()
+    pieces = [pl.ds(part * LEAF, LEAF) for part in range(3)]
+    fetches = [
+        pltpu.make_async_copy(near_mid_hbm.at[at], near_mid_ref.at[at], sems.at[i])
+        for i, at in enumerate(pieces)
+    ]
+    for fetch in fetches:
+        fetch.start()
     near = jnp.zeros((S, LEAF), F32)
     highs = []
     for part in range(3):
@@ -271,7 +284,8 @@
         right = jnp.concatenate([near_high, near_high], 0)
         near = near + jnp.dot(left, right, preferred_element_type=F32)
         highs.append(high)
-    fetch.wait()
+    for fetch in fetches:
+        fetch.wait()
     near = near + jnp.dot(
         jnp.concatenate(highs, 1), near_mid_ref[...], preferred_element_type=F32
     )
@@ -333,21 +347,28 @@
     hat_ref[S:] = got[:, S:]
 
 
+def laying_parent_kernel(
+    turned_ref, pair_ref, mine_ref, other_ref, parts_ref, hat_ref, basis_ref, sems
+):
+    copies = []
+    for i in range(parts_ref.shape[0]):
+        leaf = turn(jnp.int32(i), turned_ref[0])
+        to = basis_ref.at[:, pl.ds(pl.multiple_of(leaf * LEAF, LEAF), LEAF)]
+        copies.append(pltpu.make_async_copy(parts_ref.at[i], to, sems.at[i]))
+        copies[-1].start()
+    parent_kernel(pair_ref, mine_ref, other_ref, hat_ref)
+    for copy in copies:
+        copy.wait()
+
+
 def last_parent_kernel(turned_ref, pair_ref, mine_ref, other_ref, hat_ref, half_ref):
     parent_kernel(pair_ref, mine_ref, other_ref, hat_ref)
     half_ref[...] = jnp.where(turned_ref[0] == 1, hat_ref[S:], hat_ref[:S])
 
 
 def top_kernel(
-    place_ref, pair_ref, mine_ref, direct_ref, passed_ref, parts_ref, q_ref, basis_ref,
-    all_rows, other_ref, sems,
+    place_ref, pair_ref, mine_ref, direct_ref, passed_ref, q_ref, all_rows, other_ref
 ):
-    copies = []
-    for i in range(parts_ref.shape[0]):
-        leaf = turn(jnp.int32(i), place_ref[2])
-        to = basis_ref.at[:, pl.ds(pl.multiple_of(leaf * LEAF, LEAF), LEAF)]
-        copies.append(pltpu.make_async_copy(parts_ref.at[i], to, sems.at[i]))
-        copies[-1].start()
     upper_direct = place_ref[2] == 0
     other_ref[:S] = jnp.where(upper_direct, direct_ref[...], passed_ref[...])
     other_ref[S:] = jnp.where(upper_direct, passed_ref[...], direct_ref[...])
@@ -362,8 +383,6 @@
     count = q_ref.shape[0]
     start = pl.multiple_of(place_ref[1] * count, count)
     q_ref[...] = all_rows[pl.ds(start, count)]
-    for copy in copies:
-        copy.wait()
 
 
 VMEM = pl.BlockSpec(memory_space=pltpu.VMEM)
@@ -443,7 +462,12 @@
         in_hbm(sketch_matrix),
         in_hbm(random_test_matrix),
         out_specs=[HBM],
-        scratch=[pltpu.SemaphoreType.DMA((4 * cells - 2,))],
+        scratch=[
+            pltpu.VMEM((columns, width), F32),
+            pltpu.VMEM((columns, width), F32),
+            pltpu.SemaphoreType.DMA((2,)),
+            pltpu.SemaphoreType.DMA((4 * cells - 2,)),
+        ],
     )
     (parcels,) = call(
         ends_kernel,
@@ -501,7 +525,7 @@
         near_high,
         in_hbm(near_mid),
         pairs[-2],
-        scratch=[pltpu.VMEM((3 * LEAF, LEAF), BF16), pltpu.SemaphoreType.DMA],
+        scratch=[pltpu.VMEM((3 * LEAF, LEAF), BF16), pltpu.SemaphoreType.DMA((3,))],
     )
     (basis,) = call(
         basis_kernel, [((cells, columns, LEAF), F32)], [VMEM] * 2, inverse, z
@@ -519,8 +543,17 @@
             swap(hat, *masks),
             *pairs[-1:] * (level == 1),
         )
-    (hat,) = call(
-        parent_kernel, [((2 * S, S), F32)], [VMEM] * 3, pairs[-3], hat, cross(hat, 1)
+    hat, leaf_basis = call(
+        laying_parent_kernel,
+        [((2 * S, S), F32), ((columns, width), F32)],
+        [SMEM] + [VMEM] * 3 + [ANY],
+        turned.reshape(1),
+        pairs[-3],
+        hat,
+        cross(hat, 1),
+        parts,
+        out_specs=[VMEM, HBM],
+        scratch=[pltpu.SemaphoreType.DMA((cells,))],
     )
     hat, half = call(
         last_parent_kernel,
@@ -532,21 +565,18 @@
         cross(hat, 2),
     )
     direct = cross(half, 4)
-    top, leaf_basis = call(
+    (top,) = call(
         top_kernel,
-        [((columns, 2 * S), F32), ((columns, width), F32)],
-        [SMEM] + [VMEM] * 4 + [ANY],
+        [((columns, 2 * S), F32)],
+        [SMEM] + [VMEM] * 4,
         jnp.stack([leaf >> 2 & 1, rep, turned]),
         pairs[-1],
         hat,
         direct,
         cross(direct, 1),
-        parts,
-        out_specs=[VMEM, ANY],
         scratch=[
             pltpu.VMEM((S, 2 * S), F32),
             pltpu.VMEM((2 * S, S), F32),
-            pltpu.SemaphoreType.DMA((cells,)),
         ],
     )
     return (leaf_basis, top[None])

time: 139 us -> 110 us (0.79)
  Pallas kernels: 74.7 us -> 44.9 us
  starting transfers between devices: 43.2 us -> 44.6 us
    pallas_call x15, Pallas kernels: 73.3 us -> 43.4 us  [call(): pl.pallas_call(kernel, out_shape=[(pltpu.HBM if spec is HBM else jax.Shap...]
    ppermute x7, starting transfers between devices: 20.5 us -> 24.2 us  [cross(): return lax.ppermute(block, 'leaf', [(i, i ^ mask) for i in range(count)])]
    ppermute x4, starting transfers between devices: 7.96 us -> 4.68 us  [swap(): return lax.ppermute(block, ('leaf', 'rep'), route)]
    ppermute x4, waiting for transfers between devices: 7.92 us -> 6.17 us  [swap(): return lax.ppermute(block, ('leaf', 'rep'), route)]
  transfers between devices with their start and end apart: 15 -> 15, of which waited for: 9 -> 10; matrix products, arithmetic and copies ran while one was open for 0% -> 0% of each run, Pallas kernels for 31% -> 12%
where the time goes in v4:
time: 110 us
  Pallas kernels  44.9 us (41%)
  starting transfers between devices  44.6 us (41%)
  waiting for transfers between devices  17.5 us (16%)
  local copies, waits for them, and re-layouts  2.05 us (2%)
    pallas_call x15, Pallas kernels, call(): pl.pallas_call(kernel, out_shape=[(pltpu.HBM if spec is HBM else jax.Shap...  43.4 us
    ppermute x7, starting transfers between devices, cross(): return lax.ppermute(block, 'leaf', [(i, i ^ mask) for i in range(count)])  24.2 us
    ppermute x7, waiting for transfers between devices, cross(): return lax.ppermute(block, 'leaf', [(i, i ^ mask) for i in range(count)])  10.6 us
    all_to_all x1, starting transfers between devices, body(): data = lax.all_to_all(parcels, 'rep', 0, 0)  6.9 us
    ppermute x4, waiting for transfers between devices, swap(): return lax.ppermute(block, ('leaf', 'rep'), route)  6.17 us
    all_to_all x1, starting transfers between devices, body(): parts = lax.all_to_all(basis, 'rep', 0, 0)  5.54 us
    ppermute x4, starting transfers between devices, swap(): return lax.ppermute(block, ('leaf', 'rep'), route)  4.68 us
    ppermute x1, starting transfers between devices, body(): lax.ppermute(low, 'leaf', [(i, (i + 1) % count) for i in range(count)])  3.03 us
  transfers between devices with their start and end apart: 15, of which 10 were waited for; matrix products, arithmetic and copies ran while one was open for 0% of the time, Pallas kernels for 12%

profile of v4, /device:TPU:1, one launch (start us, length us, event | category | flops | bytes accessed | tf_op | source)
XLA Modules:
  0.0 109.9 jit_solution(69334754590242477)
XLA Ops:
  0.6 1.5 %shard_map.59 = (f32[16,512]{1,0:T(8,128)}, f32[16,512]{1,0:T(8,128)}) custom-call(f32[8,8192]{1,0:T(8,128)} %tests_hbm.1, f32[8,8192]{1,0:T(8,128)} %tests_hbm.1, f32[2,8192]{1,0:T(2,128)} %coords_ref.1, f32[2,8192]{1,0:T(2,128)} %coords_ref.1, f32[1,8192]{1,0:T(1,128)} %bitcast.8), custom_call_target="tpu_custom_call" | custom-call | tf_op jit(solution)/shard_map/pallas_call | solution.py:446
  2.1 3.0 %collective-permute-start = (f32[16,512]{1,0:T(8,128)}, f32[16,512]{1,0:T(8,128)S(1)}, u32[]{:S(2)}, u32[]{:S(2)}) collective-permute-start(f32[16,512]{1,0:T(8,128)} %get-tuple-element.22), channel_id=1, source_target_pairs={{0,16},{16,32},{32,48},{48,64},{64,80},{80,96},{96,112},{112,128},... | collective-permute-start | bytes 98312 | tf_op jit(solution)/shard_map/ppermute | solution.py:454
  5.3 2.6 %shard_map.62.packed_ref = f32[16,4,8,512]{3,2,1,0:T(8,128)} custom-call(s32[1]{0:T(128)} %bitcast.turned_ref, f32[8,8192]{1,0:T(8,128)} %samples_hbm.1, f32[8,8192]{1,0:T(8,128)} %tests_hbm.1), custom_call_target="tpu_custom_call" | custom-call | flops 1000000000 | bytes 1048576 | tf_op jit(solution)/shard_map/pallas_call | solution.py:395
  9.3 6.9 %all-to-all-start = ((f32[16,4,8,512]{3,2,1,0:T(8,128)}), f32[16,4,8,512]{3,2,1,0:T(8,128)S(1)}, u32[]{:S(2)}, u32[]{:S(2)}) async-start(f32[16,4,8,512]{3,2,1,0:T(8,128)} %shard_map.63), calls=%async_computation | async-start | bytes 2097152 | tf_op jit(solution)/shard_map/all_to_all | solution.py:484
  16.3 5.3 %shard_map.60 = (bf16[1536,512]{1,0:T(8,128)(2,1)S(1)}, bf16[1536,512]{1,0:T(8,128)(2,1)}, f32[8,128]{1,0:T(8,128)S(1)}, bf16[2,3,128,128]{3,2,1,0:T(8,128)(2,1)...) custom-call(s32[1]{0:T(128)} %bitcast.2.rep_ref, ...), custom_call_target="tpu_custom_call" | custom-call | flops 10000000000 | bytes 1048576 | tf_op jit(solution)/shard_map/pallas_call | solution.py:395
  23.6 3.1 %collective-permute-start.2 = (f32[8,128]{1,0:T(8,128)S(1)}, f32[8,128]{1,0:T(8,128)S(1)}, u32[]{:S(2)}, u32[]{:S(2)}) collective-permute-start(f32[8,128]{1,0:T(8,128)S(1)} %get-tuple-element.24.mine_ref), channel_id=1, source_target_pairs={{0,16},{16,0},{32,48},{48,32},{64,80},{80,64},{96,112},{112,96},{1... | collective-permute-start | bytes 12296 | tf_op jit(solution)/shard_map/ppermute | solution.py:428
  26.7 0.8 collective-permute-done.2.other_ref
  27.9 2.7 %collective-permute-done.3.other_ref = f32[8,128]{1,0:T(8,128)S(1)} collective-permute-done((f32[8,128]{1,0:T(8,128)S(1)}, f32[8,128]{1,0:T(8,128)S(1)}, u32[]{:S(2)}, u32[]{:S(2)}) %collective-permute-start.3) | collective-permute-done | bytes 4128 | tf_op jit(solution)/shard_map/ppermute | solution.py:428
  30.9 5.8 %shard_map.65 = (f32[128,512]{1,0:T(8,128)S(1)}, f32[128,128]{1,0:T(8,128)S(1)}, f32[256,128]{1,0:T(8,128)S(1)}) custom-call(f32[16,4,8,512]{3,2,1,0:T(8,128)S(1)} %all-to-all-done.data_ref, bf16[1536,512]{1,0:T(8,128)(2,1)S(1)} %get-tuple-element.30.near_high_ref, bf16[1536,512]{1,0:T(8,128)(2,1)} %get-tuple-element.31.near_mid_hbm, ...), custom_call_target="tpu_custom_call" | custom-call | flops 1000000000 | bytes 1048576 | tf_op jit(solution)/shard_map/pallas_call | solution.py:395
  36.8 1.7 %collective-permute-start.4 = (f32[256,128]{1,0:T(8,128)S(1)}, f32[256,128]{1,0:T(8,128)S(1)}, u32[]{:S(2)}, u32[]{:S(2)}) collective-permute-start(f32[256,128]{1,0:T(8,128)S(1)} %get-tuple-element.34.mine_ref), channel_id=1, source_target_pairs={{0,1},{1,0},{2,3},{3,2},{4,5},{5,4},{6,7},{7,6},{8,9},{9,8},{10,11... | collective-permute-start | bytes 393224 | tf_op jit(solution)/shard_map/ppermute | solution.py:423
  38.5 2.4 %collective-permute-done.4.other_ref = f32[256,128]{1,0:T(8,128)S(1)} collective-permute-done((f32[256,128]{1,0:T(8,128)S(1)}, f32[256,128]{1,0:T(8,128)S(1)}, u32[]{:S(2)}, u32[]{:S(2)}) %collective-permute-start.4) | collective-permute-done | bytes 131104 | tf_op jit(solution)/shard_map/ppermute | solution.py:423
  40.9 3.7 %shard_map.66.mine_ref = f32[256,128]{1,0:T(8,128)S(1)} custom-call(bf16[2,3,128,128]{3,2,1,0:T(8,128)(2,1)S(1)} %copy-done.7, f32[256,128]{1,0:T(8,128)S(1)} %get-tuple-element.34.mine_ref, f32[256,128]{1,0:T(8,128)S(1)} %collective-permute-done.4.other_ref), custom_call_target="tpu_custom_call" | custom-call | flops 1000000000 | bytes 1048576 | tf_op jit(solution)/shard_map/pallas_call | solution.py:395
  44.6 2.8 %collective-permute-start.5 = (f32[256,128]{1,0:T(8,128)S(1)}, f32[256,128]{1,0:T(8,128)S(1)}, u32[]{:S(2)}, u32[]{:S(2)}) collective-permute-start(f32[256,128]{1,0:T(8,128)S(1)} %shard_map.66.mine_ref), channel_id=1, source_target_pairs={{0,3},{1,2},{2,1},{3,0},{4,7},{5,6},{6,5},{7,4},{8,11},{9,10},{10,... | collective-permute-start | bytes 393224 | tf_op jit(solution)/shard_map/ppermute | solution.py:423
  47.3 7.0 %collective-permute-start.6 = (f32[8,128]{1,0:T(8,128)S(1)}, f32[8,128]{1,0:T(8,128)S(1)}, u32[]{:S(2)}, u32[]{:S(2)}) collective-permute-start(f32[8,128]{1,0:T(8,128)S(1)} %get-tuple-element.35.mine_ref), channel_id=1, source_target_pairs={{0,64},{16,80},{32,96},{48,112},{64,0},{80,16},{96,32},{112,48},{1... | collective-permute-start | bytes 12296 | tf_op jit(solution)/shard_map/ppermute | solution.py:428
  54.4 1.0 collective-permute-done.6.other_ref
  55.6 3.7 %shard_map.68.mine_ref = f32[256,128]{1,0:T(8,128)S(1)} custom-call(bf16[2,3,128,128]{3,2,1,0:T(8,128)(2,1)S(1)} %get-tuple-element.28.pair_ref, f32[256,128]{1,0:T(8,128)S(1)} %shard_map.66.mine_ref, f32[256,128]{1,0:T(8,128)S(1)} %collective-permute-done.5.other_ref, bf16[2,3,128,128]{3,2,1,0:T(8,128)(2,1)S(1)} %shard_map.67.rest_0_.pair_ref), custom_call_target="tpu_custom_call" | custom-call | flops 1000000000 | bytes 1048576 | tf_op jit(solution)/shard_map/pallas_call | solution.py:395
  59.4 3.8 %collective-permute-done.7.other_ref = f32[256,128]{1,0:T(8,128)S(1)} collective-permute-done((f32[256,128]{1,0:T(8,128)S(1)}, f32[256,128]{1,0:T(8,128)S(1)}, u32[]{:S(2)}, u32[]{:S(2)}) %collective-permute-start.7) | collective-permute-done | bytes 131104 | tf_op jit(solution)/shard_map/ppermute | solution.py:423
  63.2 3.7 %shard_map.69.mine_ref = f32[256,128]{1,0:T(8,128)S(1)} custom-call(bf16[2,3,128,128]{3,2,1,0:T(8,128)(2,1)S(1)} %copy-done.5, f32[256,128]{1,0:T(8,128)S(1)} %shard_map.68.mine_ref, f32[256,128]{1,0:T(8,128)S(1)} %collective-permute-done.7.other_ref), custom_call_target="tpu_custom_call" | custom-call | flops 1000000000 | bytes 1048576 | tf_op jit(solution)/shard_map/pallas_call | solution.py:395
  67.0 1.0 shard_map.71
  68.0 5.5 %all-to-all-start.1 = ((f32[16,8,512]{2,1,0:T(8,128)}), f32[16,8,512]{2,1,0:T(8,128)S(1)}, u32[]{:S(2)}, u32[]{:S(2)}) async-start(f32[16,8,512]{2,1,0:T(8,128)} %shard_map.71), calls=%async_computation.1 | async-start | bytes 524288 | tf_op jit(solution)/shard_map/all_to_all | solution.py:533
  73.6 3.7 %shard_map.70.mine_ref = f32[256,128]{1,0:T(8,128)S(1)} custom-call(bf16[2,3,128,128]{3,2,1,0:T(8,128)(2,1)S(1)} %copy-done.3, f32[256,128]{1,0:T(8,128)S(1)} %shard_map.69.mine_ref, f32[256,128]{1,0:T(8,128)S(1)} %collective-permute-done.8.other_ref), custom_call_target="tpu_custom_call" | custom-call | flops 1000000000 | bytes 1048576 | tf_op jit(solution)/shard_map/pallas_call | solution.py:395
  77.3 4.2 %collective-permute-start.9 = (f32[256,128]{1,0:T(8,128)S(1)}, f32[256,128]{1,0:T(8,128)S(1)}, u32[]{:S(2)}, u32[]{:S(2)}) collective-permute-start(f32[256,128]{1,0:T(8,128)S(1)} %shard_map.70.mine_ref), channel_id=1, source_target_pairs={{0,16},{16,0},{32,48},{48,32},{64,80},{80,64},{96,112},{112,96},{1... | collective-permute-start | bytes 393224 | tf_op jit(solution)/shard_map/ppermute | solution.py:428
  81.5 1.0 collective-permute-done.9.other_ref
  82.5 4.1 %shard_map.72 = (f32[256,128]{1,0:T(8,128)S(1)}, f32[8,8192]{1,0:T(8,128)}) custom-call(s32[1]{0:T(128)} %bitcast.turned_ref, bf16[2,3,128,128]{3,2,1,0:T(8,128)(2,1)S(1)} %get-tuple-element.25.pair_ref, f32[256,128]{1,0:T(8,128)S(1)} %shard_map.70.mine_ref, f32[256,128]{1,0:T(8,128)S(1)} %collective-permute-done.9.other_ref, ...), custom_call_target="tpu_custom_call" | custom-call | flops 1000000000 | bytes 1048576 | tf_op jit(solution)/shard_map/pallas_call | solution.py:395
  86.5 1.4 %collective-permute-start.10 = (f32[256,128]{1,0:T(8,128)S(1)}, f32[256,128]{1,0:T(8,128)S(1)}, u32[]{:S(2)}, u32[]{:S(2)}) collective-permute-start(f32[256,128]{1,0:T(8,128)S(1)} %get-tuple-element.39.mine_ref), channel_id=1, source_target_pairs={{0,32},{16,48},{32,0},{48,16},{64,96},{80,112},{96,64},{112,80},{1... | collective-permute-start | bytes 393224 | tf_op jit(solution)/shard_map/ppermute | solution.py:428
  87.9 2.5 %collective-permute-done.10.other_ref = f32[256,128]{1,0:T(8,128)S(1)} collective-permute-done((f32[256,128]{1,0:T(8,128)S(1)}, f32[256,128]{1,0:T(8,128)S(1)}, u32[]{:S(2)}, u32[]{:S(2)}) %collective-permute-start.10) | collective-permute-done | bytes 131104 | tf_op jit(solution)/shard_map/ppermute | solution.py:428
  90.4 3.7 %shard_map.73 = (f32[256,128]{1,0:T(8,128)S(1)}, f32[128,128]{1,0:T(8,128)S(1)}) custom-call(s32[1]{0:T(128)} %bitcast.turned_ref, bf16[2,3,128,128]{3,2,1,0:T(8,128)(2,1)S(1)} %get-tuple-element.33._.pair_ref, f32[256,128]{1,0:T(8,128)S(1)} %get-tuple-element.39.mine_ref, f32[256,128]{1,0:T(8,128)S(1)} %collective-permute-done.10.other_ref), custom_call_target="tpu_custom_call" | custom-call | flops 1000000000 | bytes 1048576 | tf_op jit(solution)/shard_map/pallas_call | solution.py:395
  94.1 2.7 %collective-permute-start.11 = (f32[128,128]{1,0:T(8,128)S(1)}, f32[128,128]{1,0:T(8,128)S(1)}, u32[]{:S(2)}, u32[]{:S(2)}) collective-permute-start(f32[128,128]{1,0:T(8,128)S(1)} %get-tuple-element.41), channel_id=1, source_target_pairs={{0,64},{16,80},{32,96},{48,112},{64,0},{80,16},{96,32},{112,48},{1... | collective-permute-start | bytes 196616 | tf_op jit(solution)/shard_map/ppermute | solution.py:428
  96.9 1.7 %collective-permute-done.11.direct_ref = f32[128,128]{1,0:T(8,128)S(1)} collective-permute-done((f32[128,128]{1,0:T(8,128)S(1)}, f32[128,128]{1,0:T(8,128)S(1)}, u32[]{:S(2)}, u32[]{:S(2)}) %collective-permute-start.11) | collective-permute-done | bytes 65568 | tf_op jit(solution)/shard_map/ppermute | solution.py:428
  98.5 5.7 %collective-permute-start.12 = (f32[128,128]{1,0:T(8,128)S(1)}, f32[128,128]{1,0:T(8,128)S(1)}, u32[]{:S(2)}, u32[]{:S(2)}) collective-permute-start(f32[128,128]{1,0:T(8,128)S(1)} %collective-permute-done.11.direct_ref), channel_id=1, source_target_pairs={{0,16},{16,0},{32,48},{48,32},{64,80},{80,64},{96,112},{112,96},{1... | collective-permute-start | bytes 196616 | tf_op jit(solution)/shard_map/ppermute | solution.py:428
  104.3 0.8 collective-permute-done.12.passed_ref
  105.1 4.8 %shard_map.74 = f32[8,256]{1,0:T(8,128)} custom-call(s32[3]{0:T(128)S(1)} %pad_add_fusion.place_ref, bf16[2,3,128,128]{3,2,1,0:T(8,128)(2,1)S(1)} %shard_map.67.rest_0_.pair_ref, f32[256,128]{1,0:T(8,128)S(1)} %get-tuple-element.40.mine_ref, f32[128,128]{1,0:T(8,128)S(1)} %collective-permute-done.11.direct_ref, f32[128,128]{1,0:T(8,128)S(1)} %collective-permute-done.12.passed_ref), custom_call_target="tpu_custom_call" | custom-call | flops 1000000000 | bytes 1048576 | tf_op jit(solution)/shard_map/pallas_call | solution.py:395
  (31 shorter events, 4.7 us)
Async XLA Ops:
  2.1 5.9 %collective-permute-start = (f32[16,512]{1,0:T(8,128)}, f32[16,512]{1,0:T(8,128)S(1)}, u32[]{:S(2)}, u32[]{:S(2)}) collective-permute-start(f32[16,512]{1,0:T(8,128)} %get-tuple-element.22), channel_id=1, source_target_pairs={{0,16},{16,32},{32,48},{48,64},{64,80},{80,96},{96,112},{112,128},... | collective-permute-start | bytes 98312 | tf_op jit(solution)/shard_map/ppermute | solution.py:454
  5.1 3.6 %collective-permute-start.1 = (f32[16,512]{1,0:T(8,128)}, f32[16,512]{1,0:T(8,128)S(1)}, u32[]{:S(2)}, u32[]{:S(2)}) collective-permute-start(f32[16,512]{1,0:T(8,128)} %get-tuple-element.23), channel_id=1, source_target_pairs={{0,240},{16,0},{32,16},{48,32},{64,48},{80,64},{96,80},{112,96},{1... | collective-permute-start | bytes 98312 | tf_op jit(solution)/shard_map/ppermute | solution.py:455
  9.3 6.9 %copy-start = (f32[2,8192]{1,0:T(2,128)S(1)}, f32[2,8192]{1,0:T(2,128)}, u32[]{:S(2)}) copy-start(f32[2,8192]{1,0:T(2,128)} %coords_ref.1) | copy-start | bytes 196612
  9.3 6.9 %copy-start.1 = (f32[8192]{0:T(1024)S(1)}, f32[8192]{0:T(1024)}, u32[]{:S(2)}) copy-start(f32[8192]{0:T(1024)} %param.5) | copy-start | bytes 98308
  9.3 21.6 %all-to-all-start = ((f32[16,4,8,512]{3,2,1,0:T(8,128)}), f32[16,4,8,512]{3,2,1,0:T(8,128)S(1)}, u32[]{:S(2)}, u32[]{:S(2)}) async-start(f32[16,4,8,512]{3,2,1,0:T(8,128)} %shard_map.63), calls=%async_computation | async-start | bytes 2097152 | tf_op jit(solution)/shard_map/all_to_all | solution.py:484
  21.5 0.7 copy-start.2
  22.2 0.7 copy-start.4
  22.9 0.7 copy-start.6
  23.6 4.0 %collective-permute-start.2 = (f32[8,128]{1,0:T(8,128)S(1)}, f32[8,128]{1,0:T(8,128)S(1)}, u32[]{:S(2)}, u32[]{:S(2)}) collective-permute-start(f32[8,128]{1,0:T(8,128)S(1)} %get-tuple-element.24.mine_ref), channel_id=1, source_target_pairs={{0,16},{16,0},{32,48},{48,32},{64,80},{80,64},{96,112},{112,96},{1... | collective-permute-start | bytes 12296 | tf_op jit(solution)/shard_map/ppermute | solution.py:428
  27.8 2.8 %collective-permute-start.3 = (f32[8,128]{1,0:T(8,128)S(1)}, f32[8,128]{1,0:T(8,128)S(1)}, u32[]{:S(2)}, u32[]{:S(2)}) collective-permute-start(f32[8,128]{1,0:T(8,128)S(1)} %get-tuple-element.32.mine_ref), channel_id=1, source_target_pairs={{0,32},{16,48},{32,0},{48,16},{64,96},{80,112},{96,64},{112,80},{1... | collective-permute-start | bytes 12296 | tf_op jit(solution)/shard_map/ppermute | solution.py:428
  30.9 9.9 %copy-start.7 = (bf16[2,3,128,128]{3,2,1,0:T(8,128)(2,1)S(1)}, bf16[2,3,128,128]{3,2,1,0:T(8,128)(2,1)}, u32[]{:S(2)}) copy-start(bf16[2,3,128,128]{3,2,1,0:T(8,128)(2,1)} %copy-done.6) | copy-start | bytes 589828
  36.8 4.1 %collective-permute-start.4 = (f32[256,128]{1,0:T(8,128)S(1)}, f32[256,128]{1,0:T(8,128)S(1)}, u32[]{:S(2)}, u32[]{:S(2)}) collective-permute-start(f32[256,128]{1,0:T(8,128)S(1)} %get-tuple-element.34.mine_ref), channel_id=1, source_target_pairs={{0,1},{1,0},{2,3},{3,2},{4,5},{5,4},{6,7},{7,6},{8,9},{9,8},{10,11... | collective-permute-start | bytes 393224 | tf_op jit(solution)/shard_map/ppermute | solution.py:423
  44.6 11.0 %collective-permute-start.5 = (f32[256,128]{1,0:T(8,128)S(1)}, f32[256,128]{1,0:T(8,128)S(1)}, u32[]{:S(2)}, u32[]{:S(2)}) collective-permute-start(f32[256,128]{1,0:T(8,128)S(1)} %shard_map.66.mine_ref), channel_id=1, source_target_pairs={{0,3},{1,2},{2,1},{3,0},{4,7},{5,6},{6,5},{7,4},{8,11},{9,10},{10,... | collective-permute-start | bytes 393224 | tf_op jit(solution)/shard_map/ppermute | solution.py:423
  47.3 8.0 %collective-permute-start.6 = (f32[8,128]{1,0:T(8,128)S(1)}, f32[8,128]{1,0:T(8,128)S(1)}, u32[]{:S(2)}, u32[]{:S(2)}) collective-permute-start(f32[8,128]{1,0:T(8,128)S(1)} %get-tuple-element.35.mine_ref), channel_id=1, source_target_pairs={{0,64},{16,80},{32,96},{48,112},{64,0},{80,16},{96,32},{112,48},{1... | collective-permute-start | bytes 12296 | tf_op jit(solution)/shard_map/ppermute | solution.py:428
  55.6 7.6 %copy-start.5 = (bf16[2,3,128,128]{3,2,1,0:T(8,128)(2,1)S(1)}, bf16[2,3,128,128]{3,2,1,0:T(8,128)(2,1)}, u32[]{:S(2)}) copy-start(bf16[2,3,128,128]{3,2,1,0:T(8,128)(2,1)} %copy-done.4) | copy-start | bytes 589828
  59.3 3.9 %collective-permute-start.7 = (f32[256,128]{1,0:T(8,128)S(1)}, f32[256,128]{1,0:T(8,128)S(1)}, u32[]{:S(2)}, u32[]{:S(2)}) collective-permute-start(f32[256,128]{1,0:T(8,128)S(1)} %shard_map.68.mine_ref), channel_id=1, source_target_pairs={{0,4},{1,5},{2,6},{3,7},{4,0},{5,1},{6,2},{7,3},{8,12},{9,13},{10,... | collective-permute-start | bytes 393224 | tf_op jit(solution)/shard_map/ppermute | solution.py:423
  66.9 6.7 %collective-permute-start.8 = (f32[256,128]{1,0:T(8,128)S(1)}, f32[256,128]{1,0:T(8,128)S(1)}, u32[]{:S(2)}, u32[]{:S(2)}) collective-permute-start(f32[256,128]{1,0:T(8,128)S(1)} %shard_map.69.mine_ref), channel_id=1, source_target_pairs={{0,12},{1,13},{2,14},{3,15},{4,8},{5,9},{6,10},{7,11},{8,4},{9,5},... | collective-permute-start | bytes 393224 | tf_op jit(solution)/shard_map/ppermute | solution.py:423
  67.0 6.6 %copy-start.3 = (bf16[2,3,128,128]{3,2,1,0:T(8,128)(2,1)S(1)}, bf16[2,3,128,128]{3,2,1,0:T(8,128)(2,1)}, u32[]{:S(2)}) copy-start(bf16[2,3,128,128]{3,2,1,0:T(8,128)(2,1)} %copy-done.2) | copy-start | bytes 589828
  68.0 13.4 %all-to-all-start.1 = ((f32[16,8,512]{2,1,0:T(8,128)}), f32[16,8,512]{2,1,0:T(8,128)S(1)}, u32[]{:S(2)}, u32[]{:S(2)}) async-start(f32[16,8,512]{2,1,0:T(8,128)} %shard_map.71), calls=%async_computation.1 | async-start | bytes 524288 | tf_op jit(solution)/shard_map/all_to_all | solution.py:533
  77.3 5.2 %collective-permute-start.9 = (f32[256,128]{1,0:T(8,128)S(1)}, f32[256,128]{1,0:T(8,128)S(1)}, u32[]{:S(2)}, u32[]{:S(2)}) collective-permute-start(f32[256,128]{1,0:T(8,128)S(1)} %shard_map.70.mine_ref), channel_id=1, source_target_pairs={{0,16},{16,0},{32,48},{48,32},{64,80},{80,64},{96,112},{112,96},{1... | collective-permute-start | bytes 393224 | tf_op jit(solution)/shard_map/ppermute | solution.py:428
  86.5 3.9 %collective-permute-start.10 = (f32[256,128]{1,0:T(8,128)S(1)}, f32[256,128]{1,0:T(8,128)S(1)}, u32[]{:S(2)}, u32[]{:S(2)}) collective-permute-start(f32[256,128]{1,0:T(8,128)S(1)} %get-tuple-element.39.mine_ref), channel_id=1, source_target_pairs={{0,32},{16,48},{32,0},{48,16},{64,96},{80,112},{96,64},{112,80},{1... | collective-permute-start | bytes 393224 | tf_op jit(solution)/shard_map/ppermute | solution.py:428
  94.1 4.4 %collective-permute-start.11 = (f32[128,128]{1,0:T(8,128)S(1)}, f32[128,128]{1,0:T(8,128)S(1)}, u32[]{:S(2)}, u32[]{:S(2)}) collective-permute-start(f32[128,128]{1,0:T(8,128)S(1)} %get-tuple-element.41), channel_id=1, source_target_pairs={{0,64},{16,80},{32,96},{48,112},{64,0},{80,16},{96,32},{112,48},{1... | collective-permute-start | bytes 196616 | tf_op jit(solution)/shard_map/ppermute | solution.py:428
  98.5 6.6 %collective-permute-start.12 = (f32[128,128]{1,0:T(8,128)S(1)}, f32[128,128]{1,0:T(8,128)S(1)}, u32[]{:S(2)}, u32[]{:S(2)}) collective-permute-start(f32[128,128]{1,0:T(8,128)S(1)} %collective-permute-done.11.direct_ref), channel_id=1, source_target_pairs={{0,16},{16,0},{32,48},{48,32},{64,80},{80,64},{96,112},{112,96},{1... | collective-permute-start | bytes 196616 | tf_op jit(solution)/shard_map/ppermute | solution.py:428

commit v5 on v4

--- a/solution.py
+++ b/solution.py
@@ -183,8 +183,7 @@
             skeleton[index], skeleton[index ^ 1], LOG_SCALE * (STEP << level)
         )
         for side in range(2):
-            for part, value in enumerate(split3(pair[side])):
-                ref[side, part] = value
+            ref[side] = pair[side]
         joined = [
             jnp.concatenate(
                 [nodes[SUB * i : SUB * (i + 1)], nodes[SUB * (i + 1) : SUB * (i + 2)]], 1
@@ -328,8 +327,7 @@
 def far_kernel(second_ref, mine_ref, other_ref, pair_ref, *joined_refs):
     mine, other = mine_ref[...], other_ref[...]
     for side, block in enumerate(coupling(mine, other, LOG_SCALE)):
-        for part, value in enumerate(split3(block)):
-            pair_ref[side, part] = value
+        pair_ref[side] = block
     second = second_ref[0] == 1
     joined = jnp.concatenate(
         [jnp.where(second, other, mine), jnp.where(second, mine, other)], 1
@@ -341,22 +339,20 @@
 
 def parent_kernel(pair_ref, mine_ref, other_ref, *rest):
     hat_ref = rest[-1]
-    pair = [[pair_ref[side, part] for part in range(3)] for side in range(2)]
+    pair = [split3(pair_ref[side]) for side in range(2)]
     got = merge(*pair, mine_ref, other_ref)
     hat_ref[:S] = got[:, :S]
     hat_ref[S:] = got[:, S:]
 
 
-def laying_parent_kernel(
-    turned_ref, pair_ref, mine_ref, other_ref, parts_ref, hat_ref, basis_ref, sems
-):
-    copies = []
+def lay_kernel(turned_ref, parts_ref, top_ref, basis_ref, out_ref, sems):
+    copies = [pltpu.make_async_copy(top_ref, out_ref, sems.at[parts_ref.shape[0]])]
+    copies[0].start()
     for i in range(parts_ref.shape[0]):
         leaf = turn(jnp.int32(i), turned_ref[0])
         to = basis_ref.at[:, pl.ds(pl.multiple_of(leaf * LEAF, LEAF), LEAF)]
         copies.append(pltpu.make_async_copy(parts_ref.at[i], to, sems.at[i]))
         copies[-1].start()
-    parent_kernel(pair_ref, mine_ref, other_ref, hat_ref)
     for copy in copies:
         copy.wait()
 
@@ -372,7 +368,7 @@
     upper_direct = place_ref[2] == 0
     other_ref[:S] = jnp.where(upper_direct, direct_ref[...], passed_ref[...])
     other_ref[S:] = jnp.where(upper_direct, passed_ref[...], direct_ref[...])
-    pair = [[pair_ref[side, part] for part in range(3)] for side in range(2)]
+    pair = [split3(pair_ref[side]) for side in range(2)]
     z_mine, z_other = off_diagonal(*pair, mine_ref, other_ref)
     second = place_ref[0] == 1
     first = jnp.where(second, z_other, z_mine)
@@ -487,7 +483,7 @@
         prepare_kernel,
         [((3 * LEAF, LEAF), BF16)] * 2
         + [((SUB, S), F32)]
-        + [((2, 3, S, S), BF16)] * cell_levels,
+        + [((2, S, S), F32)] * cell_levels,
         [SMEM] + [VMEM] * 4,
         own.reshape(1),
         curve_coordinates,
@@ -508,7 +504,7 @@
     for level in range(3):
         pair, *joined = call(
             far_kernel,
-            [((2, 3, S, S), BF16), ((SUB, S), F32)][: 2 - level // 2],
+            [((2, S, S), F32), ((SUB, S), F32)][: 2 - level // 2],
             [SMEM] + [VMEM] * 2,
             (leaf >> level & 1).reshape(1),
             skeleton,
@@ -543,17 +539,8 @@
             swap(hat, *masks),
             *pairs[-1:] * (level == 1),
         )
-    hat, leaf_basis = call(
-        laying_parent_kernel,
-        [((2 * S, S), F32), ((columns, width), F32)],
-        [SMEM] + [VMEM] * 3 + [ANY],
-        turned.reshape(1),
-        pairs[-3],
-        hat,
-        cross(hat, 1),
-        parts,
-        out_specs=[VMEM, HBM],
-        scratch=[pltpu.SemaphoreType.DMA((cells,))],
+    (hat,) = call(
+        parent_kernel, [((2 * S, S), F32)], [VMEM] * 3, pairs[-3], hat, cross(hat, 1)
     )
     hat, half = call(
         last_parent_kernel,
@@ -579,6 +566,16 @@
             pltpu.VMEM((2 * S, S), F32),
         ],
     )
+    leaf_basis, top = call(
+        lay_kernel,
+        [((columns, width), F32), ((columns, 2 * S), F32)],
+        [SMEM, VMEM, VMEM],
+        turned.reshape(1),
+        parts,
+        top,
+        out_specs=[HBM, HBM],
+        scratch=[pltpu.SemaphoreType.DMA((cells + 1,))],
+    )
     return (leaf_basis, top[None])
 
 

time: 110 us -> 111 us (level)
  waiting for transfers between devices: 17.5 us -> 25.1 us
  starting transfers between devices: 44.6 us -> 39.1 us
  local copies, waits for them, and re-layouts: 2.05 us -> 0.68 us
    ppermute x4, waiting for transfers between devices: 6.17 us -> 12.3 us  [swap(): return lax.ppermute(block, ('leaf', 'rep'), route)]
    ppermute x4, starting transfers between devices: 4.68 us -> 2.22 us  [swap(): return lax.ppermute(block, ('leaf', 'rep'), route)]
    all_to_all x1, starting transfers between devices: 5.54 us -> 3.8 us  [body(): parts = lax.all_to_all(basis, 'rep', 0, 0)]
    unnamed x16 -> x12, local copies, waits for them, and re-layouts: 2.05 us -> 0.68 us
    all_to_all x1, waiting for transfers between devices: 0.01 us -> 1.34 us  [body(): data = lax.all_to_all(parcels, 'rep', 0, 0)]
    ppermute x7, starting transfers between devices: 24.2 us -> 22.9 us  [cross(): return lax.ppermute(block, 'leaf', [(i, i ^ mask) for i in range(count)])]
    pallas_call x15 -> x16, Pallas kernels: 43.4 us -> 42.8 us  [call(): pl.pallas_call(kernel, out_shape=[(pltpu.HBM if spec is HBM else jax.Shap...]
  transfers between devices with their start and end apart: 15 -> 15, of which waited for: 10 -> 12; matrix products, arithmetic and copies ran while one was open for 0% -> 0% of each run, Pallas kernels for 12% -> 12%
where the time goes in v5:
time: 111 us; the launch traced here: 110 us
  Pallas kernels  44.2 us (40%)
  starting transfers between devices  39.1 us (35%)
  waiting for transfers between devices  25.1 us (23%)
    pallas_call x16, Pallas kernels, call(): pl.pallas_call(kernel, out_shape=[(pltpu.HBM if spec is HBM else jax.Shap...  42.8 us
    ppermute x7, starting transfers between devices, cross(): return lax.ppermute(block, 'leaf', [(i, i ^ mask) for i in range(count)])  22.9 us
    ppermute x4, waiting for transfers between devices, swap(): return lax.ppermute(block, ('leaf', 'rep'), route)  12.3 us
    ppermute x7, waiting for transfers between devices, cross(): return lax.ppermute(block, 'leaf', [(i, i ^ mask) for i in range(count)])  9.95 us
    all_to_all x1, starting transfers between devices, body(): data = lax.all_to_all(parcels, 'rep', 0, 0)  6.9 us
    all_to_all x1, starting transfers between devices, body(): parts = lax.all_to_all(basis, 'rep', 0, 0)  3.8 us
    ppermute x1, starting transfers between devices, body(): lax.ppermute(low, 'leaf', [(i, (i + 1) % count) for i in range(count)])  3.03 us
  transfers between devices with their start and end apart: 15, of which 12 were waited for; matrix products, arithmetic and copies ran while one was open for 0% of the time, Pallas kernels for 12%

profile of v5, /device:TPU:1, one launch (start us, length us, event | category | flops | bytes accessed | tf_op | source)
XLA Modules:
  0.0 110.2 jit_solution(11621526478127619726)
XLA Ops:
  0.6 1.5 %shard_map.60 = (f32[16,512]{1,0:T(8,128)}, f32[16,512]{1,0:T(8,128)}) custom-call(f32[8,8192]{1,0:T(8,128)} %last_ref.1, f32[8,8192]{1,0:T(8,128)} %last_ref.1, f32[2,8192]{1,0:T(2,128)} %coords_ref.1, f32[2,8192]{1,0:T(2,128)} %coords_ref.1, f32[1,8192]{1,0:T(1,128)} %bitcast.8), custom_call_target="tpu_custom_call" | custom-call | tf_op jit(solution)/shard_map/pallas_call | solution.py:442
  2.1 3.0 %collective-permute-start = (f32[16,512]{1,0:T(8,128)}, f32[16,512]{1,0:T(8,128)S(1)}, u32[]{:S(2)}, u32[]{:S(2)}) collective-permute-start(f32[16,512]{1,0:T(8,128)} %get-tuple-element.22), channel_id=1, source_target_pairs={{0,16},{16,32},{32,48},{48,64},{64,80},{80,96},{96,112},{112,128},... | collective-permute-start | bytes 98312 | tf_op jit(solution)/shard_map/ppermute | solution.py:450
  5.3 2.6 %shard_map.59.packed_ref = f32[16,4,8,512]{3,2,1,0:T(8,128)} custom-call(s32[1]{0:T(128)} %bitcast.turned_ref, f32[8,8192]{1,0:T(8,128)} %samples_hbm.1, f32[8,8192]{1,0:T(8,128)} %last_ref.1), custom_call_target="tpu_custom_call" | custom-call | flops 1000000000 | bytes 1048576 | tf_op jit(solution)/shard_map/pallas_call | solution.py:391
  9.3 6.9 %all-to-all-start = ((f32[16,4,8,512]{3,2,1,0:T(8,128)}), f32[16,4,8,512]{3,2,1,0:T(8,128)S(1)}, u32[]{:S(2)}, u32[]{:S(2)}) async-start(f32[16,4,8,512]{3,2,1,0:T(8,128)} %shard_map.61), calls=%async_computation | async-start | bytes 2097152 | tf_op jit(solution)/shard_map/all_to_all | solution.py:480
  16.3 4.8 %shard_map.62 = (bf16[1536,512]{1,0:T(8,128)(2,1)S(1)}, bf16[1536,512]{1,0:T(8,128)(2,1)}, f32[8,128]{1,0:T(8,128)S(1)}, f32[2,128,128]{2,1,0:T(8,128)S(1)}, f32...) custom-call(s32[1]{0:T(128)} %bitcast.2.rep_ref, f32[2,8192]{1,0:T(2,128)S(1)} %copy-done, ...), custom_call_target="tpu_custom_call" | custom-call | flops 10000000000 | bytes 1048576 | tf_op jit(solution)/shard_map/pallas_call | solution.py:391
  21.7 3.1 %collective-permute-start.2 = (f32[8,128]{1,0:T(8,128)S(1)}, f32[8,128]{1,0:T(8,128)S(1)}, u32[]{:S(2)}, u32[]{:S(2)}) collective-permute-start(f32[8,128]{1,0:T(8,128)S(1)} %get-tuple-element.26.mine_ref), channel_id=1, source_target_pairs={{0,16},{16,0},{32,48},{48,32},{64,80},{80,64},{96,112},{112,96},{1... | collective-permute-start | bytes 12296 | tf_op jit(solution)/shard_map/ppermute | solution.py:424
  26.0 2.7 %collective-permute-done.3.other_ref = f32[8,128]{1,0:T(8,128)S(1)} collective-permute-done((f32[8,128]{1,0:T(8,128)S(1)}, f32[8,128]{1,0:T(8,128)S(1)}, u32[]{:S(2)}, u32[]{:S(2)}) %collective-permute-start.3) | collective-permute-done | bytes 4128 | tf_op jit(solution)/shard_map/ppermute | solution.py:424
  29.0 1.3 %all-to-all-done.data_ref = f32[16,4,8,512]{3,2,1,0:T(8,128)S(1)} async-done(((f32[16,4,8,512]{3,2,1,0:T(8,128)}), f32[16,4,8,512]{3,2,1,0:T(8,128)S(1)}, u32[]{:S(2)}, u32[]{:S(2)}) %all-to-all-start) | async-done | bytes 1048608 | tf_op jit(solution)/shard_map/all_to_all | solution.py:480
  30.4 5.8 %shard_map.65 = (f32[128,512]{1,0:T(8,128)S(1)}, f32[128,128]{1,0:T(8,128)S(1)}, f32[256,128]{1,0:T(8,128)S(1)}) custom-call(f32[16,4,8,512]{3,2,1,0:T(8,128)S(1)} %all-to-all-done.data_ref, bf16[1536,512]{1,0:T(8,128)(2,1)S(1)} %get-tuple-element.24.near_high_ref, bf16[1536,512]{1,0:T(8,128)(2,1)} %get-tuple-element.25.near_mid_hbm, ...), custom_call_target="tpu_custom_call" | custom-call | flops 1000000000 | bytes 1048576 | tf_op jit(solution)/shard_map/pallas_call | solution.py:391
  36.6 3.5 %collective-permute-done.5.other_ref = f32[256,128]{1,0:T(8,128)S(1)} collective-permute-done((f32[256,128]{1,0:T(8,128)S(1)}, f32[256,128]{1,0:T(8,128)S(1)}, u32[]{:S(2)}, u32[]{:S(2)}) %collective-permute-start.5) | collective-permute-done | bytes 131104 | tf_op jit(solution)/shard_map/ppermute | solution.py:419
  40.1 3.7 %shard_map.68.mine_ref = f32[256,128]{1,0:T(8,128)S(1)} custom-call(f32[2,128,128]{2,1,0:T(8,128)S(1)} %copy-done.5, f32[256,128]{1,0:T(8,128)S(1)} %get-tuple-element.37.mine_ref, f32[256,128]{1,0:T(8,128)S(1)} %collective-permute-done.5.other_ref), custom_call_target="tpu_custom_call" | custom-call | flops 1000000000 | bytes 1048576 | tf_op jit(solution)/shard_map/pallas_call | solution.py:391
  43.9 1.6 %collective-permute-start.6 = (f32[256,128]{1,0:T(8,128)S(1)}, f32[256,128]{1,0:T(8,128)S(1)}, u32[]{:S(2)}, u32[]{:S(2)}) collective-permute-start(f32[256,128]{1,0:T(8,128)S(1)} %shard_map.68.mine_ref), channel_id=1, source_target_pairs={{0,3},{1,2},{2,1},{3,0},{4,7},{5,6},{6,5},{7,4},{8,11},{9,10},{10,... | collective-permute-start | bytes 393224 | tf_op jit(solution)/shard_map/ppermute | solution.py:419
  45.5 8.9 %collective-permute-start.4 = (f32[8,128]{1,0:T(8,128)S(1)}, f32[8,128]{1,0:T(8,128)S(1)}, u32[]{:S(2)}, u32[]{:S(2)}) collective-permute-start(f32[8,128]{1,0:T(8,128)S(1)} %get-tuple-element.31.mine_ref), channel_id=1, source_target_pairs={{0,64},{16,80},{32,96},{48,112},{64,0},{80,16},{96,32},{112,48},{1... | collective-permute-start | bytes 12296 | tf_op jit(solution)/shard_map/ppermute | solution.py:424
  54.3 1.0 collective-permute-done.4.other_ref
  55.6 3.7 %shard_map.69.mine_ref = f32[256,128]{1,0:T(8,128)S(1)} custom-call(f32[2,128,128]{2,1,0:T(8,128)S(1)} %get-tuple-element.35.pair_ref, f32[256,128]{1,0:T(8,128)S(1)} %shard_map.68.mine_ref, f32[256,128]{1,0:T(8,128)S(1)} %collective-permute-done.6.other_ref, f32[2,128,128]{2,1,0:T(8,128)S(1)} %shard_map.67.rest_0_.pair_ref), custom_call_target="tpu_custom_call" | custom-call | flops 1000000000 | bytes 1048576 | tf_op jit(solution)/shard_map/pallas_call | solution.py:391
  59.4 3.8 %collective-permute-done.7.other_ref = f32[256,128]{1,0:T(8,128)S(1)} collective-permute-done((f32[256,128]{1,0:T(8,128)S(1)}, f32[256,128]{1,0:T(8,128)S(1)}, u32[]{:S(2)}, u32[]{:S(2)}) %collective-permute-start.7) | collective-permute-done | bytes 131104 | tf_op jit(solution)/shard_map/ppermute | solution.py:419
  63.2 3.7 %shard_map.70.mine_ref = f32[256,128]{1,0:T(8,128)S(1)} custom-call(f32[2,128,128]{2,1,0:T(8,128)S(1)} %copy-done.3, f32[256,128]{1,0:T(8,128)S(1)} %shard_map.69.mine_ref, f32[256,128]{1,0:T(8,128)S(1)} %collective-permute-done.7.other_ref), custom_call_target="tpu_custom_call" | custom-call | flops 1000000000 | bytes 1048576 | tf_op jit(solution)/shard_map/pallas_call | solution.py:391
  67.0 5.0 %collective-permute-done.8.other_ref = f32[256,128]{1,0:T(8,128)S(1)} collective-permute-done((f32[256,128]{1,0:T(8,128)S(1)}, f32[256,128]{1,0:T(8,128)S(1)}, u32[]{:S(2)}, u32[]{:S(2)}) %collective-permute-start.8) | collective-permute-done | bytes 131104 | tf_op jit(solution)/shard_map/ppermute | solution.py:419
  72.0 3.7 %shard_map.71.mine_ref = f32[256,128]{1,0:T(8,128)S(1)} custom-call(f32[2,128,128]{2,1,0:T(8,128)S(1)} %get-tuple-element.33.pair_ref, f32[256,128]{1,0:T(8,128)S(1)} %shard_map.70.mine_ref, f32[256,128]{1,0:T(8,128)S(1)} %collective-permute-done.8.other_ref), custom_call_target="tpu_custom_call" | custom-call | flops 1000000000 | bytes 1048576 | tf_op jit(solution)/shard_map/pallas_call | solution.py:391
  75.7 3.9 %collective-permute-start.9 = (f32[256,128]{1,0:T(8,128)S(1)}, f32[256,128]{1,0:T(8,128)S(1)}, u32[]{:S(2)}, u32[]{:S(2)}) collective-permute-start(f32[256,128]{1,0:T(8,128)S(1)} %shard_map.71.mine_ref), channel_id=1, source_target_pairs={{0,16},{16,0},{32,48},{48,32},{64,80},{80,64},{96,112},{112,96},{1... | collective-permute-start | bytes 393224 | tf_op jit(solution)/shard_map/ppermute | solution.py:424
  79.6 1.0 collective-permute-done.9.other_ref
  80.6 3.7 %shard_map.72.mine_ref = f32[256,128]{1,0:T(8,128)S(1)} custom-call(f32[2,128,128]{2,1,0:T(8,128)S(1)} %get-tuple-element.32.pair_ref, f32[256,128]{1,0:T(8,128)S(1)} %shard_map.71.mine_ref, f32[256,128]{1,0:T(8,128)S(1)} %collective-permute-done.9.other_ref), custom_call_target="tpu_custom_call" | custom-call | flops 1000000000 | bytes 1048576 | tf_op jit(solution)/shard_map/pallas_call | solution.py:391
  84.3 2.5 %collective-permute-start.10 = (f32[256,128]{1,0:T(8,128)S(1)}, f32[256,128]{1,0:T(8,128)S(1)}, u32[]{:S(2)}, u32[]{:S(2)}) collective-permute-start(f32[256,128]{1,0:T(8,128)S(1)} %shard_map.72.mine_ref), channel_id=1, source_target_pairs={{0,32},{16,48},{32,0},{48,16},{64,96},{80,112},{96,64},{112,80},{1... | collective-permute-start | bytes 393224 | tf_op jit(solution)/shard_map/ppermute | solution.py:424
  86.8 3.6 %collective-permute-done.10.other_ref = f32[256,128]{1,0:T(8,128)S(1)} collective-permute-done((f32[256,128]{1,0:T(8,128)S(1)}, f32[256,128]{1,0:T(8,128)S(1)}, u32[]{:S(2)}, u32[]{:S(2)}) %collective-permute-start.10) | collective-permute-done | bytes 131104 | tf_op jit(solution)/shard_map/ppermute | solution.py:424
  90.4 3.7 %shard_map.73 = (f32[256,128]{1,0:T(8,128)S(1)}, f32[128,128]{1,0:T(8,128)S(1)}) custom-call(s32[1]{0:T(128)} %bitcast.turned_ref, f32[2,128,128]{2,1,0:T(8,128)S(1)} %get-tuple-element.28._.pair_ref, f32[256,128]{1,0:T(8,128)S(1)} %shard_map.72.mine_ref, f32[256,128]{1,0:T(8,128)S(1)} %collective-permute-done.10.other_ref), custom_call_target="tpu_custom_call" | custom-call | flops 1000000000 | bytes 1048576 | tf_op jit(solution)/shard_map/pallas_call | solution.py:391
  94.1 2.6 %collective-permute-start.11 = (f32[128,128]{1,0:T(8,128)S(1)}, f32[128,128]{1,0:T(8,128)S(1)}, u32[]{:S(2)}, u32[]{:S(2)}) collective-permute-start(f32[128,128]{1,0:T(8,128)S(1)} %get-tuple-element.39), channel_id=1, source_target_pairs={{0,64},{16,80},{32,96},{48,112},{64,0},{80,16},{96,32},{112,48},{1... | collective-permute-start | bytes 196616 | tf_op jit(solution)/shard_map/ppermute | solution.py:424
  96.7 1.0 shard_map.66
  97.7 3.8 %all-to-all-start.1 = ((f32[16,8,512]{2,1,0:T(8,128)}), f32[16,8,512]{2,1,0:T(8,128)S(1)}, u32[]{:S(2)}, u32[]{:S(2)}) async-start(f32[16,8,512]{2,1,0:T(8,128)} %shard_map.66), calls=%async_computation.1 | async-start | bytes 524288 | tf_op jit(solution)/shard_map/all_to_all | solution.py:529
  101.5 1.8 %collective-permute-start.12 = (f32[128,128]{1,0:T(8,128)S(1)}, f32[128,128]{1,0:T(8,128)S(1)}, u32[]{:S(2)}, u32[]{:S(2)}) collective-permute-start(f32[128,128]{1,0:T(8,128)S(1)} %collective-permute-done.11.direct_ref), channel_id=1, source_target_pairs={{0,16},{16,0},{32,48},{48,32},{64,80},{80,64},{96,112},{112,96},{1... | collective-permute-start | bytes 196616 | tf_op jit(solution)/shard_map/ppermute | solution.py:424
  103.4 0.8 collective-permute-done.12.passed_ref
  104.3 4.2 %shard_map.74.top_ref = f32[8,256]{1,0:T(8,128)S(1)} custom-call(s32[3]{0:T(128)S(1)} %pad_add_fusion.place_ref, f32[2,128,128]{2,1,0:T(8,128)S(1)} %shard_map.67.rest_0_.pair_ref, f32[256,128]{1,0:T(8,128)S(1)} %get-tuple-element.38.mine_ref, f32[128,128]{1,0:T(8,128)S(1)} %collective-permute-done.11.direct_ref, ...), custom_call_target="tpu_custom_call" | custom-call | flops 1000000000 | bytes 1048576 | tf_op jit(solution)/shard_map/pallas_call | solution.py:391
  109.2 0.8 shard_map.75
  (28 shorter events, 5.4 us)
Async XLA Ops:
  2.1 5.9 %collective-permute-start = (f32[16,512]{1,0:T(8,128)}, f32[16,512]{1,0:T(8,128)S(1)}, u32[]{:S(2)}, u32[]{:S(2)}) collective-permute-start(f32[16,512]{1,0:T(8,128)} %get-tuple-element.22), channel_id=1, source_target_pairs={{0,16},{16,32},{32,48},{48,64},{64,80},{80,96},{96,112},{112,128},... | collective-permute-start | bytes 98312 | tf_op jit(solution)/shard_map/ppermute | solution.py:450
  5.1 3.6 %collective-permute-start.1 = (f32[16,512]{1,0:T(8,128)}, f32[16,512]{1,0:T(8,128)S(1)}, u32[]{:S(2)}, u32[]{:S(2)}) collective-permute-start(f32[16,512]{1,0:T(8,128)} %get-tuple-element.23), channel_id=1, source_target_pairs={{0,240},{16,0},{32,16},{48,32},{64,48},{80,64},{96,80},{112,96},{1... | collective-permute-start | bytes 98312 | tf_op jit(solution)/shard_map/ppermute | solution.py:451
  9.3 6.9 %copy-start = (f32[2,8192]{1,0:T(2,128)S(1)}, f32[2,8192]{1,0:T(2,128)}, u32[]{:S(2)}) copy-start(f32[2,8192]{1,0:T(2,128)} %coords_ref.1) | copy-start | bytes 196612
  9.3 6.9 %copy-start.1 = (f32[8192]{0:T(1024)S(1)}, f32[8192]{0:T(1024)}, u32[]{:S(2)}) copy-start(f32[8192]{0:T(1024)} %param.5) | copy-start | bytes 98308
  9.3 21.0 %all-to-all-start = ((f32[16,4,8,512]{3,2,1,0:T(8,128)}), f32[16,4,8,512]{3,2,1,0:T(8,128)S(1)}, u32[]{:S(2)}, u32[]{:S(2)}) async-start(f32[16,4,8,512]{3,2,1,0:T(8,128)} %shard_map.61), calls=%async_computation | async-start | bytes 2097152 | tf_op jit(solution)/shard_map/all_to_all | solution.py:480
  21.1 0.7 copy-start.2
  21.7 4.2 %copy-start.4 = (f32[2,128,128]{2,1,0:T(8,128)}, f32[2,128,128]{2,1,0:T(8,128)S(1)}, u32[]{:S(2)}) copy-start(f32[2,128,128]{2,1,0:T(8,128)S(1)} %get-tuple-element.36.pair_ref) | copy-start | bytes 393220
  21.7 4.0 %collective-permute-start.2 = (f32[8,128]{1,0:T(8,128)S(1)}, f32[8,128]{1,0:T(8,128)S(1)}, u32[]{:S(2)}, u32[]{:S(2)}) collective-permute-start(f32[8,128]{1,0:T(8,128)S(1)} %get-tuple-element.26.mine_ref), channel_id=1, source_target_pairs={{0,16},{16,0},{32,48},{48,32},{64,80},{80,64},{96,112},{112,96},{1... | collective-permute-start | bytes 12296 | tf_op jit(solution)/shard_map/ppermute | solution.py:424
  25.9 2.8 %collective-permute-start.3 = (f32[8,128]{1,0:T(8,128)S(1)}, f32[8,128]{1,0:T(8,128)S(1)}, u32[]{:S(2)}, u32[]{:S(2)}) collective-permute-start(f32[8,128]{1,0:T(8,128)S(1)} %get-tuple-element.27.mine_ref), channel_id=1, source_target_pairs={{0,32},{16,48},{32,0},{48,16},{64,96},{80,112},{96,64},{112,80},{1... | collective-permute-start | bytes 12296 | tf_op jit(solution)/shard_map/ppermute | solution.py:424
  30.4 9.8 %copy-start.5 = (f32[2,128,128]{2,1,0:T(8,128)S(1)}, f32[2,128,128]{2,1,0:T(8,128)}, u32[]{:S(2)}) copy-start(f32[2,128,128]{2,1,0:T(8,128)} %copy-done.4) | copy-start | bytes 393220
  36.2 3.9 %collective-permute-start.5 = (f32[256,128]{1,0:T(8,128)S(1)}, f32[256,128]{1,0:T(8,128)S(1)}, u32[]{:S(2)}, u32[]{:S(2)}) collective-permute-start(f32[256,128]{1,0:T(8,128)S(1)} %get-tuple-element.37.mine_ref), channel_id=1, source_target_pairs={{0,1},{1,0},{2,3},{3,2},{4,5},{5,4},{6,7},{7,6},{8,9},{9,8},{10,11... | collective-permute-start | bytes 393224 | tf_op jit(solution)/shard_map/ppermute | solution.py:419
  43.9 11.7 %collective-permute-start.6 = (f32[256,128]{1,0:T(8,128)S(1)}, f32[256,128]{1,0:T(8,128)S(1)}, u32[]{:S(2)}, u32[]{:S(2)}) collective-permute-start(f32[256,128]{1,0:T(8,128)S(1)} %shard_map.68.mine_ref), channel_id=1, source_target_pairs={{0,3},{1,2},{2,1},{3,0},{4,7},{5,6},{6,5},{7,4},{8,11},{9,10},{10,... | collective-permute-start | bytes 393224 | tf_op jit(solution)/shard_map/ppermute | solution.py:419
  45.5 9.9 %collective-permute-start.4 = (f32[8,128]{1,0:T(8,128)S(1)}, f32[8,128]{1,0:T(8,128)S(1)}, u32[]{:S(2)}, u32[]{:S(2)}) collective-permute-start(f32[8,128]{1,0:T(8,128)S(1)} %get-tuple-element.31.mine_ref), channel_id=1, source_target_pairs={{0,64},{16,80},{32,96},{48,112},{64,0},{80,16},{96,32},{112,48},{1... | collective-permute-start | bytes 12296 | tf_op jit(solution)/shard_map/ppermute | solution.py:424
  55.6 7.6 %copy-start.3 = (f32[2,128,128]{2,1,0:T(8,128)S(1)}, f32[2,128,128]{2,1,0:T(8,128)}, u32[]{:S(2)}) copy-start(f32[2,128,128]{2,1,0:T(8,128)} %copy-done.2) | copy-start | bytes 393220
  59.3 3.9 %collective-permute-start.7 = (f32[256,128]{1,0:T(8,128)S(1)}, f32[256,128]{1,0:T(8,128)S(1)}, u32[]{:S(2)}, u32[]{:S(2)}) collective-permute-start(f32[256,128]{1,0:T(8,128)S(1)} %shard_map.69.mine_ref), channel_id=1, source_target_pairs={{0,4},{1,5},{2,6},{3,7},{4,0},{5,1},{6,2},{7,3},{8,12},{9,13},{10,... | collective-permute-start | bytes 393224 | tf_op jit(solution)/shard_map/ppermute | solution.py:419
  66.9 5.1 %collective-permute-start.8 = (f32[256,128]{1,0:T(8,128)S(1)}, f32[256,128]{1,0:T(8,128)S(1)}, u32[]{:S(2)}, u32[]{:S(2)}) collective-permute-start(f32[256,128]{1,0:T(8,128)S(1)} %shard_map.70.mine_ref), channel_id=1, source_target_pairs={{0,12},{1,13},{2,14},{3,15},{4,8},{5,9},{6,10},{7,11},{8,4},{9,5},... | collective-permute-start | bytes 393224 | tf_op jit(solution)/shard_map/ppermute | solution.py:419
  75.7 4.9 %collective-permute-start.9 = (f32[256,128]{1,0:T(8,128)S(1)}, f32[256,128]{1,0:T(8,128)S(1)}, u32[]{:S(2)}, u32[]{:S(2)}) collective-permute-start(f32[256,128]{1,0:T(8,128)S(1)} %shard_map.71.mine_ref), channel_id=1, source_target_pairs={{0,16},{16,0},{32,48},{48,32},{64,80},{80,64},{96,112},{112,96},{1... | collective-permute-start | bytes 393224 | tf_op jit(solution)/shard_map/ppermute | solution.py:424
  84.3 6.1 %collective-permute-start.10 = (f32[256,128]{1,0:T(8,128)S(1)}, f32[256,128]{1,0:T(8,128)S(1)}, u32[]{:S(2)}, u32[]{:S(2)}) collective-permute-start(f32[256,128]{1,0:T(8,128)S(1)} %shard_map.72.mine_ref), channel_id=1, source_target_pairs={{0,32},{16,48},{32,0},{48,16},{64,96},{80,112},{96,64},{112,80},{1... | collective-permute-start | bytes 393224 | tf_op jit(solution)/shard_map/ppermute | solution.py:424
  94.1 7.4 %collective-permute-start.11 = (f32[128,128]{1,0:T(8,128)S(1)}, f32[128,128]{1,0:T(8,128)S(1)}, u32[]{:S(2)}, u32[]{:S(2)}) collective-permute-start(f32[128,128]{1,0:T(8,128)S(1)} %get-tuple-element.39), channel_id=1, source_target_pairs={{0,64},{16,80},{32,96},{48,112},{64,0},{80,16},{96,32},{112,48},{1... | collective-permute-start | bytes 196616 | tf_op jit(solution)/shard_map/ppermute | solution.py:424
  97.7 11.5 %all-to-all-start.1 = ((f32[16,8,512]{2,1,0:T(8,128)}), f32[16,8,512]{2,1,0:T(8,128)S(1)}, u32[]{:S(2)}, u32[]{:S(2)}) async-start(f32[16,8,512]{2,1,0:T(8,128)} %shard_map.66), calls=%async_computation.1 | async-start | bytes 524288 | tf_op jit(solution)/shard_map/all_to_all | solution.py:529
  101.5 2.7 %collective-permute-start.12 = (f32[128,128]{1,0:T(8,128)S(1)}, f32[128,128]{1,0:T(8,128)S(1)}, u32[]{:S(2)}, u32[]{:S(2)}) collective-permute-start(f32[128,128]{1,0:T(8,128)S(1)} %collective-permute-done.11.direct_ref), channel_id=1, source_target_pairs={{0,16},{16,0},{32,48},{48,32},{64,80},{80,64},{96,112},{112,96},{1... | collective-permute-start | bytes 196616 | tf_op jit(solution)/shard_map/ppermute | solution.py:424

commit v6 on v5

--- a/solution.py
+++ b/solution.py
@@ -345,9 +345,8 @@
     hat_ref[S:] = got[:, S:]
 
 
-def lay_kernel(turned_ref, parts_ref, top_ref, basis_ref, out_ref, sems):
-    copies = [pltpu.make_async_copy(top_ref, out_ref, sems.at[parts_ref.shape[0]])]
-    copies[0].start()
+def lay_kernel(turned_ref, parts_ref, basis_ref, sems):
+    copies = []
     for i in range(parts_ref.shape[0]):
         leaf = turn(jnp.int32(i), turned_ref[0])
         to = basis_ref.at[:, pl.ds(pl.multiple_of(leaf * LEAF, LEAF), LEAF)]
@@ -363,7 +362,7 @@
 
 
 def top_kernel(
-    place_ref, pair_ref, mine_ref, direct_ref, passed_ref, q_ref, all_rows, other_ref
+    place_ref, pair_ref, mine_ref, direct_ref, passed_ref, _, q_ref, all_rows, other_ref
 ):
     upper_direct = place_ref[2] == 0
     other_ref[:S] = jnp.where(upper_direct, direct_ref[...], passed_ref[...])
@@ -552,29 +551,29 @@
         cross(hat, 2),
     )
     direct = cross(half, 4)
+    (leaf_basis,) = call(
+        lay_kernel,
+        [((columns, width), F32)],
+        [SMEM, VMEM],
+        turned.reshape(1),
+        parts,
+        out_specs=[HBM],
+        scratch=[pltpu.SemaphoreType.DMA((cells,))],
+    )
     (top,) = call(
         top_kernel,
         [((columns, 2 * S), F32)],
-        [SMEM] + [VMEM] * 4,
+        [SMEM] + [VMEM] * 4 + [HBM],
         jnp.stack([leaf >> 2 & 1, rep, turned]),
         pairs[-1],
         hat,
         direct,
         cross(direct, 1),
+        in_hbm(leaf_basis),
         scratch=[
             pltpu.VMEM((S, 2 * S), F32),
             pltpu.VMEM((2 * S, S), F32),
         ],
-    )
-    leaf_basis, top = call(
-        lay_kernel,
-        [((columns, width), F32), ((columns, 2 * S), F32)],
-        [SMEM, VMEM, VMEM],
-        turned.reshape(1),
-        parts,
-        top,
-        out_specs=[HBM, HBM],
-        scratch=[pltpu.SemaphoreType.DMA((cells + 1,))],
     )
     return (leaf_basis, top[None])
 

time: 111 us -> 108 us (0.973)
  starting transfers between devices: 39.1 us -> 37.2 us
    ppermute x7, starting transfers between devices: 22.9 us -> 21 us  [cross(): return lax.ppermute(block, 'leaf', [(i, i ^ mask) for i in range(count)])]
  transfers between devices with their start and end apart: 15 -> 15, of which waited for: 12 -> 11; matrix products, arithmetic and copies ran while one was open for 0% -> 0% of each run, Pallas kernels for 12% -> 13%
where the time goes in v6:
time: 108 us
  Pallas kernels  44.8 us (41%)
  starting transfers between devices  37.2 us (34%)
  waiting for transfers between devices  24.3 us (22%)
    pallas_call x16, Pallas kernels, call(): pl.pallas_call(kernel, out_shape=[(pltpu.HBM if spec is HBM else jax.Shap...  43.4 us
    ppermute x7, starting transfers between devices, cross(): return lax.ppermute(block, 'leaf', [(i, i ^ mask) for i in range(count)])  21 us
    ppermute x4, waiting for transfers between devices, swap(): return lax.ppermute(block, ('leaf', 'rep'), route)  12.3 us
    ppermute x7, waiting for transfers between devices, cross(): return lax.ppermute(block, 'leaf', [(i, i ^ mask) for i in range(count)])  9.93 us
    all_to_all x1, starting transfers between devices, body(): data = lax.all_to_all(parcels, 'rep', 0, 0)  6.9 us
    all_to_all x1, starting transfers between devices, body(): parts = lax.all_to_all(basis, 'rep', 0, 0)  3.8 us
    ppermute x1, starting transfers between devices, body(): lax.ppermute(low, 'leaf', [(i, (i + 1) % count) for i in range(count)])  3.03 us
    ppermute x4, starting transfers between devices, swap(): return lax.ppermute(block, ('leaf', 'rep'), route)  2.25 us
  transfers between devices with their start and end apart: 15, of which 11 were waited for; matrix products, arithmetic and copies ran while one was open for 0% of the time, Pallas kernels for 13%

profile of v6, /device:TPU:1, one launch (start us, length us, event | category | flops | bytes accessed | tf_op | source)
XLA Modules:
  0.0 107.9 jit_solution(18343871222873166708)
XLA Ops:
  0.6 1.5 %shard_map.60 = (f32[16,512]{1,0:T(8,128)}, f32[16,512]{1,0:T(8,128)}) custom-call(f32[8,8192]{1,0:T(8,128)} %last_ref.1, f32[8,8192]{1,0:T(8,128)} %last_ref.1, f32[2,8192]{1,0:T(2,128)} %coords_ref.1, f32[2,8192]{1,0:T(2,128)} %coords_ref.1, f32[1,8192]{1,0:T(1,128)} %bitcast.8), custom_call_target="tpu_custom_call" | custom-call | tf_op jit(solution)/shard_map/pallas_call | solution.py:441
  2.1 3.0 %collective-permute-start = (f32[16,512]{1,0:T(8,128)}, f32[16,512]{1,0:T(8,128)S(1)}, u32[]{:S(2)}, u32[]{:S(2)}) collective-permute-start(f32[16,512]{1,0:T(8,128)} %get-tuple-element.20), channel_id=1, source_target_pairs={{0,16},{16,32},{32,48},{48,64},{64,80},{80,96},{96,112},{112,128},... | collective-permute-start | bytes 98312 | tf_op jit(solution)/shard_map/ppermute | solution.py:449
  5.3 2.6 %shard_map.59.packed_ref = f32[16,4,8,512]{3,2,1,0:T(8,128)} custom-call(s32[1]{0:T(128)} %bitcast.turned_ref, f32[8,8192]{1,0:T(8,128)} %samples_hbm.1, f32[8,8192]{1,0:T(8,128)} %last_ref.1), custom_call_target="tpu_custom_call" | custom-call | flops 1000000000 | bytes 1048576 | tf_op jit(solution)/shard_map/pallas_call | solution.py:390
  9.3 6.9 %all-to-all-start = ((f32[16,4,8,512]{3,2,1,0:T(8,128)}), f32[16,4,8,512]{3,2,1,0:T(8,128)S(1)}, u32[]{:S(2)}, u32[]{:S(2)}) async-start(f32[16,4,8,512]{3,2,1,0:T(8,128)} %shard_map.61), calls=%async_computation | async-start | bytes 2097152 | tf_op jit(solution)/shard_map/all_to_all | solution.py:479
  16.3 4.8 %shard_map.62 = (bf16[1536,512]{1,0:T(8,128)(2,1)S(1)}, bf16[1536,512]{1,0:T(8,128)(2,1)}, f32[8,128]{1,0:T(8,128)S(1)}, f32[2,128,128]{2,1,0:T(8,128)S(1)}, f32...) custom-call(s32[1]{0:T(128)} %bitcast.2.rep_ref, f32[2,8192]{1,0:T(2,128)S(1)} %copy-done, ...), custom_call_target="tpu_custom_call" | custom-call | flops 10000000000 | bytes 1048576 | tf_op jit(solution)/shard_map/pallas_call | solution.py:390
  21.7 3.1 %collective-permute-start.2 = (f32[8,128]{1,0:T(8,128)S(1)}, f32[8,128]{1,0:T(8,128)S(1)}, u32[]{:S(2)}, u32[]{:S(2)}) collective-permute-start(f32[8,128]{1,0:T(8,128)S(1)} %get-tuple-element.24.mine_ref), channel_id=1, source_target_pairs={{0,16},{16,0},{32,48},{48,32},{64,80},{80,64},{96,112},{112,96},{1... | collective-permute-start | bytes 12296 | tf_op jit(solution)/shard_map/ppermute | solution.py:423
  24.9 0.8 collective-permute-done.2.other_ref
  26.1 2.7 %collective-permute-done.3.other_ref = f32[8,128]{1,0:T(8,128)S(1)} collective-permute-done((f32[8,128]{1,0:T(8,128)S(1)}, f32[8,128]{1,0:T(8,128)S(1)}, u32[]{:S(2)}, u32[]{:S(2)}) %collective-permute-start.3) | collective-permute-done | bytes 4128 | tf_op jit(solution)/shard_map/ppermute | solution.py:423
  29.0 1.3 %all-to-all-done.data_ref = f32[16,4,8,512]{3,2,1,0:T(8,128)S(1)} async-done(((f32[16,4,8,512]{3,2,1,0:T(8,128)}), f32[16,4,8,512]{3,2,1,0:T(8,128)S(1)}, u32[]{:S(2)}, u32[]{:S(2)}) %all-to-all-start) | async-done | bytes 1048608 | tf_op jit(solution)/shard_map/all_to_all | solution.py:479
  30.4 5.8 %shard_map.65 = (f32[128,512]{1,0:T(8,128)S(1)}, f32[128,128]{1,0:T(8,128)S(1)}, f32[256,128]{1,0:T(8,128)S(1)}) custom-call(f32[16,4,8,512]{3,2,1,0:T(8,128)S(1)} %all-to-all-done.data_ref, bf16[1536,512]{1,0:T(8,128)(2,1)S(1)} %get-tuple-element.22.near_high_ref, bf16[1536,512]{1,0:T(8,128)(2,1)} %get-tuple-element.23.near_mid_hbm, ...), custom_call_target="tpu_custom_call" | custom-call | flops 1000000000 | bytes 1048576 | tf_op jit(solution)/shard_map/pallas_call | solution.py:390
  36.6 3.5 %collective-permute-done.5.other_ref = f32[256,128]{1,0:T(8,128)S(1)} collective-permute-done((f32[256,128]{1,0:T(8,128)S(1)}, f32[256,128]{1,0:T(8,128)S(1)}, u32[]{:S(2)}, u32[]{:S(2)}) %collective-permute-start.5) | collective-permute-done | bytes 131104 | tf_op jit(solution)/shard_map/ppermute | solution.py:418
  40.1 3.7 %shard_map.69.mine_ref = f32[256,128]{1,0:T(8,128)S(1)} custom-call(f32[2,128,128]{2,1,0:T(8,128)S(1)} %copy-done.5, f32[256,128]{1,0:T(8,128)S(1)} %get-tuple-element.35.mine_ref, f32[256,128]{1,0:T(8,128)S(1)} %collective-permute-done.5.other_ref), custom_call_target="tpu_custom_call" | custom-call | flops 1000000000 | bytes 1048576 | tf_op jit(solution)/shard_map/pallas_call | solution.py:390
  43.8 1.6 %collective-permute-start.6 = (f32[256,128]{1,0:T(8,128)S(1)}, f32[256,128]{1,0:T(8,128)S(1)}, u32[]{:S(2)}, u32[]{:S(2)}) collective-permute-start(f32[256,128]{1,0:T(8,128)S(1)} %shard_map.69.mine_ref), channel_id=1, source_target_pairs={{0,3},{1,2},{2,1},{3,0},{4,7},{5,6},{6,5},{7,4},{8,11},{9,10},{10,... | collective-permute-start | bytes 393224 | tf_op jit(solution)/shard_map/ppermute | solution.py:418
  45.5 8.9 %collective-permute-start.4 = (f32[8,128]{1,0:T(8,128)S(1)}, f32[8,128]{1,0:T(8,128)S(1)}, u32[]{:S(2)}, u32[]{:S(2)}) collective-permute-start(f32[8,128]{1,0:T(8,128)S(1)} %get-tuple-element.29.mine_ref), channel_id=1, source_target_pairs={{0,64},{16,80},{32,96},{48,112},{64,0},{80,16},{96,32},{112,48},{1... | collective-permute-start | bytes 12296 | tf_op jit(solution)/shard_map/ppermute | solution.py:423
  54.4 1.0 collective-permute-done.4.other_ref
  55.6 3.7 %shard_map.70.mine_ref = f32[256,128]{1,0:T(8,128)S(1)} custom-call(f32[2,128,128]{2,1,0:T(8,128)S(1)} %get-tuple-element.33.pair_ref, f32[256,128]{1,0:T(8,128)S(1)} %shard_map.69.mine_ref, f32[256,128]{1,0:T(8,128)S(1)} %collective-permute-done.6.other_ref, f32[2,128,128]{2,1,0:T(8,128)S(1)} %shard_map.68.rest_0_.pair_ref), custom_call_target="tpu_custom_call" | custom-call | flops 1000000000 | bytes 1048576 | tf_op jit(solution)/shard_map/pallas_call | solution.py:390
  59.4 3.8 %collective-permute-done.7.other_ref = f32[256,128]{1,0:T(8,128)S(1)} collective-permute-done((f32[256,128]{1,0:T(8,128)S(1)}, f32[256,128]{1,0:T(8,128)S(1)}, u32[]{:S(2)}, u32[]{:S(2)}) %collective-permute-start.7) | collective-permute-done | bytes 131104 | tf_op jit(solution)/shard_map/ppermute | solution.py:418
  63.2 3.7 %shard_map.71.mine_ref = f32[256,128]{1,0:T(8,128)S(1)} custom-call(f32[2,128,128]{2,1,0:T(8,128)S(1)} %copy-done.3, f32[256,128]{1,0:T(8,128)S(1)} %shard_map.70.mine_ref, f32[256,128]{1,0:T(8,128)S(1)} %collective-permute-done.7.other_ref), custom_call_target="tpu_custom_call" | custom-call | flops 1000000000 | bytes 1048576 | tf_op jit(solution)/shard_map/pallas_call | solution.py:390
  67.0 5.0 %collective-permute-done.8.other_ref = f32[256,128]{1,0:T(8,128)S(1)} collective-permute-done((f32[256,128]{1,0:T(8,128)S(1)}, f32[256,128]{1,0:T(8,128)S(1)}, u32[]{:S(2)}, u32[]{:S(2)}) %collective-permute-start.8) | collective-permute-done | bytes 131104 | tf_op jit(solution)/shard_map/ppermute | solution.py:418
  72.0 3.7 %shard_map.72.mine_ref = f32[256,128]{1,0:T(8,128)S(1)} custom-call(f32[2,128,128]{2,1,0:T(8,128)S(1)} %get-tuple-element.31.pair_ref, f32[256,128]{1,0:T(8,128)S(1)} %shard_map.71.mine_ref, f32[256,128]{1,0:T(8,128)S(1)} %collective-permute-done.8.other_ref), custom_call_target="tpu_custom_call" | custom-call | flops 1000000000 | bytes 1048576 | tf_op jit(solution)/shard_map/pallas_call | solution.py:390
  75.8 3.9 %collective-permute-start.9 = (f32[256,128]{1,0:T(8,128)S(1)}, f32[256,128]{1,0:T(8,128)S(1)}, u32[]{:S(2)}, u32[]{:S(2)}) collective-permute-start(f32[256,128]{1,0:T(8,128)S(1)} %shard_map.72.mine_ref), channel_id=1, source_target_pairs={{0,16},{16,0},{32,48},{48,32},{64,80},{80,64},{96,112},{112,96},{1... | collective-permute-start | bytes 393224 | tf_op jit(solution)/shard_map/ppermute | solution.py:423
  79.6 1.0 collective-permute-done.9.other_ref
  80.6 3.7 %shard_map.73.mine_ref = f32[256,128]{1,0:T(8,128)S(1)} custom-call(f32[2,128,128]{2,1,0:T(8,128)S(1)} %get-tuple-element.30.pair_ref, f32[256,128]{1,0:T(8,128)S(1)} %shard_map.72.mine_ref, f32[256,128]{1,0:T(8,128)S(1)} %collective-permute-done.9.other_ref), custom_call_target="tpu_custom_call" | custom-call | flops 1000000000 | bytes 1048576 | tf_op jit(solution)/shard_map/pallas_call | solution.py:390
  84.3 2.5 %collective-permute-start.10 = (f32[256,128]{1,0:T(8,128)S(1)}, f32[256,128]{1,0:T(8,128)S(1)}, u32[]{:S(2)}, u32[]{:S(2)}) collective-permute-start(f32[256,128]{1,0:T(8,128)S(1)} %shard_map.73.mine_ref), channel_id=1, source_target_pairs={{0,32},{16,48},{32,0},{48,16},{64,96},{80,112},{96,64},{112,80},{1... | collective-permute-start | bytes 393224 | tf_op jit(solution)/shard_map/ppermute | solution.py:423
  86.8 1.0 shard_map.66
  87.8 3.8 %all-to-all-start.1 = ((f32[16,8,512]{2,1,0:T(8,128)}), f32[16,8,512]{2,1,0:T(8,128)S(1)}, u32[]{:S(2)}, u32[]{:S(2)}) async-start(f32[16,8,512]{2,1,0:T(8,128)} %shard_map.66), calls=%async_computation.1 | async-start | bytes 524288 | tf_op jit(solution)/shard_map/all_to_all | solution.py:528
  91.6 3.7 %shard_map.74 = (f32[256,128]{1,0:T(8,128)S(1)}, f32[128,128]{1,0:T(8,128)S(1)}) custom-call(s32[1]{0:T(128)} %bitcast.turned_ref, f32[2,128,128]{2,1,0:T(8,128)S(1)} %get-tuple-element.26._.pair_ref, f32[256,128]{1,0:T(8,128)S(1)} %shard_map.73.mine_ref, f32[256,128]{1,0:T(8,128)S(1)} %collective-permute-done.10.other_ref), custom_call_target="tpu_custom_call" | custom-call | flops 1000000000 | bytes 1048576 | tf_op jit(solution)/shard_map/pallas_call | solution.py:390
  95.4 1.5 %collective-permute-start.11 = (f32[128,128]{1,0:T(8,128)S(1)}, f32[128,128]{1,0:T(8,128)S(1)}, u32[]{:S(2)}, u32[]{:S(2)}) collective-permute-start(f32[128,128]{1,0:T(8,128)S(1)} %get-tuple-element.37), channel_id=1, source_target_pairs={{0,64},{16,80},{32,96},{48,112},{64,0},{80,16},{96,32},{112,48},{1... | collective-permute-start | bytes 196616 | tf_op jit(solution)/shard_map/ppermute | solution.py:423
  96.9 4.3 %collective-permute-done.11.direct_ref = f32[128,128]{1,0:T(8,128)S(1)} collective-permute-done((f32[128,128]{1,0:T(8,128)S(1)}, f32[128,128]{1,0:T(8,128)S(1)}, u32[]{:S(2)}, u32[]{:S(2)}) %collective-permute-start.11) | collective-permute-done | bytes 65568 | tf_op jit(solution)/shard_map/ppermute | solution.py:423
  101.2 1.0 collective-permute-start.12
  102.3 0.8 shard_map.67._
  103.2 4.8 %shard_map.75 = f32[8,256]{1,0:T(8,128)} custom-call(s32[3]{0:T(128)S(1)} %pad_add_fusion.place_ref, f32[2,128,128]{2,1,0:T(8,128)S(1)} %shard_map.68.rest_0_.pair_ref, f32[256,128]{1,0:T(8,128)S(1)} %get-tuple-element.36.mine_ref, f32[128,128]{1,0:T(8,128)S(1)} %collective-permute-done.11.direct_ref, f32[128,128]{1,0:T(8,128)S(1)} %collective-permute-done.12.passed_ref, ...), custom_call_target="tpu_custom_call" | custom-call | flops 1000000000 | bytes 1048576 | tf_op jit(solution)/shard_map/pallas_call | solution.py:390
  (28 shorter events, 3.8 us)
Async XLA Ops:
  2.1 5.9 %collective-permute-start = (f32[16,512]{1,0:T(8,128)}, f32[16,512]{1,0:T(8,128)S(1)}, u32[]{:S(2)}, u32[]{:S(2)}) collective-permute-start(f32[16,512]{1,0:T(8,128)} %get-tuple-element.20), channel_id=1, source_target_pairs={{0,16},{16,32},{32,48},{48,64},{64,80},{80,96},{96,112},{112,128},... | collective-permute-start | bytes 98312 | tf_op jit(solution)/shard_map/ppermute | solution.py:449
  5.1 3.6 %collective-permute-start.1 = (f32[16,512]{1,0:T(8,128)}, f32[16,512]{1,0:T(8,128)S(1)}, u32[]{:S(2)}, u32[]{:S(2)}) collective-permute-start(f32[16,512]{1,0:T(8,128)} %get-tuple-element.21), channel_id=1, source_target_pairs={{0,240},{16,0},{32,16},{48,32},{64,48},{80,64},{96,80},{112,96},{1... | collective-permute-start | bytes 98312 | tf_op jit(solution)/shard_map/ppermute | solution.py:450
  9.3 6.9 %copy-start = (f32[2,8192]{1,0:T(2,128)S(1)}, f32[2,8192]{1,0:T(2,128)}, u32[]{:S(2)}) copy-start(f32[2,8192]{1,0:T(2,128)} %coords_ref.1) | copy-start | bytes 196612
  9.3 6.9 %copy-start.1 = (f32[8192]{0:T(1024)S(1)}, f32[8192]{0:T(1024)}, u32[]{:S(2)}) copy-start(f32[8192]{0:T(1024)} %param.5) | copy-start | bytes 98308
  9.3 21.0 %all-to-all-start = ((f32[16,4,8,512]{3,2,1,0:T(8,128)}), f32[16,4,8,512]{3,2,1,0:T(8,128)S(1)}, u32[]{:S(2)}, u32[]{:S(2)}) async-start(f32[16,4,8,512]{3,2,1,0:T(8,128)} %shard_map.61), calls=%async_computation | async-start | bytes 2097152 | tf_op jit(solution)/shard_map/all_to_all | solution.py:479
  21.1 0.7 copy-start.2
  21.7 4.2 %copy-start.4 = (f32[2,128,128]{2,1,0:T(8,128)}, f32[2,128,128]{2,1,0:T(8,128)S(1)}, u32[]{:S(2)}) copy-start(f32[2,128,128]{2,1,0:T(8,128)S(1)} %get-tuple-element.34.pair_ref) | copy-start | bytes 393220
  21.7 4.0 %collective-permute-start.2 = (f32[8,128]{1,0:T(8,128)S(1)}, f32[8,128]{1,0:T(8,128)S(1)}, u32[]{:S(2)}, u32[]{:S(2)}) collective-permute-start(f32[8,128]{1,0:T(8,128)S(1)} %get-tuple-element.24.mine_ref), channel_id=1, source_target_pairs={{0,16},{16,0},{32,48},{48,32},{64,80},{80,64},{96,112},{112,96},{1... | collective-permute-start | bytes 12296 | tf_op jit(solution)/shard_map/ppermute | solution.py:423
  25.9 2.8 %collective-permute-start.3 = (f32[8,128]{1,0:T(8,128)S(1)}, f32[8,128]{1,0:T(8,128)S(1)}, u32[]{:S(2)}, u32[]{:S(2)}) collective-permute-start(f32[8,128]{1,0:T(8,128)S(1)} %get-tuple-element.25.mine_ref), channel_id=1, source_target_pairs={{0,32},{16,48},{32,0},{48,16},{64,96},{80,112},{96,64},{112,80},{1... | collective-permute-start | bytes 12296 | tf_op jit(solution)/shard_map/ppermute | solution.py:423
  30.4 9.8 %copy-start.5 = (f32[2,128,128]{2,1,0:T(8,128)S(1)}, f32[2,128,128]{2,1,0:T(8,128)}, u32[]{:S(2)}) copy-start(f32[2,128,128]{2,1,0:T(8,128)} %copy-done.4) | copy-start | bytes 393220
  36.2 3.9 %collective-permute-start.5 = (f32[256,128]{1,0:T(8,128)S(1)}, f32[256,128]{1,0:T(8,128)S(1)}, u32[]{:S(2)}, u32[]{:S(2)}) collective-permute-start(f32[256,128]{1,0:T(8,128)S(1)} %get-tuple-element.35.mine_ref), channel_id=1, source_target_pairs={{0,1},{1,0},{2,3},{3,2},{4,5},{5,4},{6,7},{7,6},{8,9},{9,8},{10,11... | collective-permute-start | bytes 393224 | tf_op jit(solution)/shard_map/ppermute | solution.py:418
  43.8 11.7 %collective-permute-start.6 = (f32[256,128]{1,0:T(8,128)S(1)}, f32[256,128]{1,0:T(8,128)S(1)}, u32[]{:S(2)}, u32[]{:S(2)}) collective-permute-start(f32[256,128]{1,0:T(8,128)S(1)} %shard_map.69.mine_ref), channel_id=1, source_target_pairs={{0,3},{1,2},{2,1},{3,0},{4,7},{5,6},{6,5},{7,4},{8,11},{9,10},{10,... | collective-permute-start | bytes 393224 | tf_op jit(solution)/shard_map/ppermute | solution.py:418
  45.5 9.9 %collective-permute-start.4 = (f32[8,128]{1,0:T(8,128)S(1)}, f32[8,128]{1,0:T(8,128)S(1)}, u32[]{:S(2)}, u32[]{:S(2)}) collective-permute-start(f32[8,128]{1,0:T(8,128)S(1)} %get-tuple-element.29.mine_ref), channel_id=1, source_target_pairs={{0,64},{16,80},{32,96},{48,112},{64,0},{80,16},{96,32},{112,48},{1... | collective-permute-start | bytes 12296 | tf_op jit(solution)/shard_map/ppermute | solution.py:423
  55.6 7.6 %copy-start.3 = (f32[2,128,128]{2,1,0:T(8,128)S(1)}, f32[2,128,128]{2,1,0:T(8,128)}, u32[]{:S(2)}) copy-start(f32[2,128,128]{2,1,0:T(8,128)} %copy-done.2) | copy-start | bytes 393220
  59.3 3.9 %collective-permute-start.7 = (f32[256,128]{1,0:T(8,128)S(1)}, f32[256,128]{1,0:T(8,128)S(1)}, u32[]{:S(2)}, u32[]{:S(2)}) collective-permute-start(f32[256,128]{1,0:T(8,128)S(1)} %shard_map.70.mine_ref), channel_id=1, source_target_pairs={{0,4},{1,5},{2,6},{3,7},{4,0},{5,1},{6,2},{7,3},{8,12},{9,13},{10,... | collective-permute-start | bytes 393224 | tf_op jit(solution)/shard_map/ppermute | solution.py:418
  66.9 5.1 %collective-permute-start.8 = (f32[256,128]{1,0:T(8,128)S(1)}, f32[256,128]{1,0:T(8,128)S(1)}, u32[]{:S(2)}, u32[]{:S(2)}) collective-permute-start(f32[256,128]{1,0:T(8,128)S(1)} %shard_map.71.mine_ref), channel_id=1, source_target_pairs={{0,12},{1,13},{2,14},{3,15},{4,8},{5,9},{6,10},{7,11},{8,4},{9,5},... | collective-permute-start | bytes 393224 | tf_op jit(solution)/shard_map/ppermute | solution.py:418
  75.8 4.9 %collective-permute-start.9 = (f32[256,128]{1,0:T(8,128)S(1)}, f32[256,128]{1,0:T(8,128)S(1)}, u32[]{:S(2)}, u32[]{:S(2)}) collective-permute-start(f32[256,128]{1,0:T(8,128)S(1)} %shard_map.72.mine_ref), channel_id=1, source_target_pairs={{0,16},{16,0},{32,48},{48,32},{64,80},{80,64},{96,112},{112,96},{1... | collective-permute-start | bytes 393224 | tf_op jit(solution)/shard_map/ppermute | solution.py:423
  84.3 7.3 %collective-permute-start.10 = (f32[256,128]{1,0:T(8,128)S(1)}, f32[256,128]{1,0:T(8,128)S(1)}, u32[]{:S(2)}, u32[]{:S(2)}) collective-permute-start(f32[256,128]{1,0:T(8,128)S(1)} %shard_map.73.mine_ref), channel_id=1, source_target_pairs={{0,32},{16,48},{32,0},{48,16},{64,96},{80,112},{96,64},{112,80},{1... | collective-permute-start | bytes 393224 | tf_op jit(solution)/shard_map/ppermute | solution.py:423
  87.8 14.4 %all-to-all-start.1 = ((f32[16,8,512]{2,1,0:T(8,128)}), f32[16,8,512]{2,1,0:T(8,128)S(1)}, u32[]{:S(2)}, u32[]{:S(2)}) async-start(f32[16,8,512]{2,1,0:T(8,128)} %shard_map.66), calls=%async_computation.1 | async-start | bytes 524288 | tf_op jit(solution)/shard_map/all_to_all | solution.py:528
  95.4 5.9 %collective-permute-start.11 = (f32[128,128]{1,0:T(8,128)S(1)}, f32[128,128]{1,0:T(8,128)S(1)}, u32[]{:S(2)}, u32[]{:S(2)}) collective-permute-start(f32[128,128]{1,0:T(8,128)S(1)} %get-tuple-element.37), channel_id=1, source_target_pairs={{0,64},{16,80},{32,96},{48,112},{64,0},{80,16},{96,32},{112,48},{1... | collective-permute-start | bytes 196616 | tf_op jit(solution)/shard_map/ppermute | solution.py:423
  101.2 1.9 %collective-permute-start.12 = (f32[128,128]{1,0:T(8,128)S(1)}, f32[128,128]{1,0:T(8,128)S(1)}, u32[]{:S(2)}, u32[]{:S(2)}) collective-permute-start(f32[128,128]{1,0:T(8,128)S(1)} %collective-permute-done.11.direct_ref), channel_id=1, source_target_pairs={{0,16},{16,0},{32,48},{48,32},{64,80},{80,64},{96,112},{112,96},{1... | collective-permute-start | bytes 196616 | tf_op jit(solution)/shard_map/ppermute | solution.py:423
